TPU v7x, 32 devices: a whole 2x2x4 slice. The times are simulated.
32 devices in a mesh: dp: 4 (over z), ctx: 8 (over y, x, core).
Axes of the slice: x: 2, y: 2, z: 4, core: 2. Of those that a mesh axis runs over, the one named last changes fastest.
Arguments:
- values: bfloat16 [4, 1024, 512], P('dp', 'ctx'), may hold values from -6 to 6
- gates: bfloat16 [4, 1024, 512], P('dp', 'ctx'), may hold values from -6 to 6
- grad_out: bfloat16 [4, 1024, 512], P('dp', 'ctx'), may hold values from -6 to 6
- filters: float32 [512, 1024], P('ctx'), may hold values from -6 to 6
- skip: float32 [512], P('ctx'), may hold values from 0.5 to 1.5
Outputs:
- grad_values: bfloat16 [4, 1024, 512], P('dp', 'ctx')
- grad_gates: bfloat16 [4, 1024, 512], P('dp', 'ctx')
- grad_filters: float32 [512, 1024], P('ctx')
All inputs are finite; a program needn't handle non-finite values.
Results may differ from a plain program's by a relative error of at most 0.0049.
Values may be sent and summed in bfloat16 or wider, within the bound.
No kernel may reach another device: no remote copies, remote signals or barrier semaphores. Data moves between devices by JAX's collectives and lax.ppermute only.
A program may use at most 64 MiB of HBM per device.

v0:
```python
import functools
import math

import jax
import jax.numpy as jnp
import numpy as np
from jax import lax
from jax.experimental import pallas as pl
from jax.experimental.pallas import tpu as pltpu
from jax.sharding import PartitionSpec as P

HIGH = lax.Precision.HIGHEST
BF16 = jnp.bfloat16
F32 = jnp.float32
DENSE_LIMIT = 1024
VMEM_BYTES = 48 * 2**20


def twiddle(rows, cols, period):
    left = lax.broadcasted_iota(jnp.int32, (rows, cols), 0)
    right = lax.broadcasted_iota(jnp.int32, (rows, cols), 1)
    angle = (left * right % period).astype(jnp.float32) * (2.0 * math.pi / period)
    return (jnp.cos(angle), jnp.sin(angle))


def pick_first(period):
    best = 2
    for cand in range(2, math.isqrt(period) + 1):
        if period % cand == 0 and cand % 2 == 0:
            best = cand
    return best


def make_tables(length):
    period = 2 * length
    first = pick_first(period)
    second = period // first
    half = first // 2
    return (
        twiddle(half, first, first),
        twiddle(first, second, period),
        twiddle(second, second, second),
        half,
        first,
        second,
        period,
    )


def forward(signal, tables):
    (cos_one, sin_one), (cos_mid, sin_mid), (cos_two, sin_two), half, first, second, period = tables
    shaped = signal.reshape(signal.shape[0], half, second)
    part_re = jnp.einsum("cmn,mk->ckn", shaped, cos_one, precision=HIGH)
    part_im = -jnp.einsum("cmn,mk->ckn", shaped, sin_one, precision=HIGH)
    mid_re = part_re * cos_mid + part_im * sin_mid
    mid_im = part_im * cos_mid - part_re * sin_mid
    spec_re = jnp.einsum("ckn,nm->ckm", mid_re, cos_two, precision=HIGH) + jnp.einsum(
        "ckn,nm->ckm", mid_im, sin_two, precision=HIGH
    )
    spec_im = jnp.einsum("ckn,nm->ckm", mid_im, cos_two, precision=HIGH) - jnp.einsum(
        "ckn,nm->ckm", mid_re, sin_two, precision=HIGH
    )
    return (spec_re, spec_im)


def inverse(spec_re, spec_im, tables):
    (cos_one, sin_one), (cos_mid, sin_mid), (cos_two, sin_two), half, first, second, period = tables
    back_re = jnp.einsum("ckm,nm->ckn", spec_re, cos_two, precision=HIGH) - jnp.einsum(
        "ckm,nm->ckn", spec_im, sin_two, precision=HIGH
    )
    back_im = jnp.einsum("ckm,nm->ckn", spec_im, cos_two, precision=HIGH) + jnp.einsum(
        "ckm,nm->ckn", spec_re, sin_two, precision=HIGH
    )
    turned_re = back_re * cos_mid - back_im * sin_mid
    turned_im = back_im * cos_mid + back_re * sin_mid
    result = jnp.einsum("ckn,mk->cmn", turned_re, cos_one, precision=HIGH) - jnp.einsum(
        "ckn,mk->cmn", turned_im, sin_one, precision=HIGH
    )
    return result.reshape(spec_re.shape[0], half * second) * (1.0 / period)


def spectral(vals_f, dz_f, filt, gains, tables, scale_a):
    vals_re, vals_im = forward(vals_f, tables)
    dz_re, dz_im = forward(dz_f, tables)
    filt_re, filt_im = forward(filt, tables)
    conv_raw = inverse(
        filt_re * vals_re - filt_im * vals_im, filt_re * vals_im + filt_im * vals_re, tables
    )
    conv = (scale_a * conv_raw + gains * vals_f).astype(BF16)
    corr = inverse(filt_re * dz_re + filt_im * dz_im, filt_re * dz_im - filt_im * dz_re, tables)
    grad_val = (scale_a * corr + gains * dz_f).astype(BF16)
    cross = inverse(vals_re * dz_re + vals_im * dz_im, vals_re * dz_im - vals_im * dz_re, tables)
    return (grad_val, conv, cross)


def per_device_long(values, gates, grad_out, filters, skip):
    length = filters.shape[1]
    scale_a = length ** (-0.5)
    scale_b = (lax.axis_size("dp") * length) ** (-0.5)
    tok_grad = grad_out[0].astype(F32)
    dz_tok = (tok_grad * gates[0].astype(F32)).astype(BF16)
    vals_ch, dz_ch = (
        lax.all_to_all(values[0].T, "ctx", split_axis=0, concat_axis=1, tiled=True),
        lax.all_to_all(dz_tok.T, "ctx", split_axis=0, concat_axis=1, tiled=True),
    )
    grad_val, conv, cross = spectral(
        vals_ch.astype(F32),
        dz_ch.astype(F32),
        filters,
        skip[:, None],
        make_tables(length),
        scale_a,
    )
    total = lax.psum(cross, "dp")
    val_back, conv_back = (
        lax.all_to_all(grad_val, "ctx", split_axis=1, concat_axis=0, tiled=True),
        lax.all_to_all(conv, "ctx", split_axis=1, concat_axis=0, tiled=True),
    )
    grad_gate_tok = (tok_grad * conv_back.T.astype(F32)).astype(BF16)
    return (val_back.T[None], grad_gate_tok[None], scale_b * total)


def dense_tables(length):
    n = np.arange(length, dtype=np.int64)[:, None]
    k = np.arange(length, dtype=np.int64)[None, :]
    angle = ((2 * k + 1) * n % (4 * length)).astype(np.float64) * (math.pi / (2 * length))
    full = np.concatenate([np.cos(angle), -np.sin(angle)], axis=1)
    high = full.astype(BF16)
    low = (full - high.astype(np.float64)).astype(BF16)
    return high, low, np.ascontiguousarray(high.T)


def vmem_specs(count):
    return [pl.BlockSpec(memory_space=pltpu.VMEM)] * count


def in_vmem(array):
    return pltpu.with_memory_space_constraint(array, pltpu.VMEM)


def pack_kernel(parts, vals_ref, gate_ref, grad_ref, out_ref):
    chans = vals_ref.shape[2] // parts
    vals = vals_ref[0].astype(F32).T.astype(BF16)
    dz = (grad_ref[0].astype(F32) * gate_ref[0].astype(F32)).T.astype(BF16)
    for d in range(parts):
        out_ref[d, :chans, :] = vals[d * chans : (d + 1) * chans, :]
        out_ref[d, chans:, :] = dz[d * chans : (d + 1) * chans, :]


def filter_kernel(filt_ref, high_ref, low_ref, out_ref):
    filt = filt_ref[...]
    f_high = filt.astype(BF16)
    f_low = (filt - f_high.astype(F32)).astype(BF16)
    high = high_ref[...]
    total = jnp.dot(f_high, low_ref[...], preferred_element_type=F32)
    total = total + jnp.dot(f_low, high, preferred_element_type=F32)
    out_ref[...] = total + jnp.dot(f_high, high, preferred_element_type=F32)


def main_kernel(x_ref, fwd_ref, inv_ref, filt_ref, skip_ref, back_ref, cross_ref):
    parts, rows, pos = x_ref.shape
    chans = rows // 2
    length = parts * pos
    x = jnp.concatenate([x_ref[s] for s in range(parts)], axis=1)
    spec = jnp.dot(x, fwd_ref[...], preferred_element_type=F32)
    vr, vi = spec[:chans, :length], spec[:chans, length:]
    gr, gi = spec[chans:, :length], spec[chans:, length:]
    hr, hi = filt_ref[:, :length], filt_ref[:, length:]
    real = jnp.concatenate([hr * vr - hi * vi, hr * gr + hi * gi, vr * gr + vi * gi], axis=0)
    imag = jnp.concatenate([hr * vi + hi * vr, hr * gi - hi * gr, vr * gi - vi * gr], axis=0)
    prod = jnp.concatenate([real.astype(BF16), imag.astype(BF16)], axis=1)
    res = jnp.dot(prod, inv_ref[...], preferred_element_type=F32)
    cross_ref[...] = (res[rows:] * (1.0 / length)).astype(BF16)
    row = lax.broadcasted_iota(jnp.int32, (chans, chans), 0)
    col = lax.broadcasted_iota(jnp.int32, (chans, chans), 1)
    gain = jnp.sum(jnp.where(row == col, skip_ref[...], 0.0), axis=1, keepdims=True)
    gains = jnp.concatenate([gain, gain], axis=0)
    scale = length**-0.5 / length
    both = (res[:rows] * scale + gains * x.astype(F32)).astype(BF16)
    for s in range(parts):
        back_ref[s] = both[:, s * pos : (s + 1) * pos]


def unpack_kernel(back_ref, grad_ref, val_ref, gate_ref):
    parts, rows, _ = back_ref.shape
    chans = rows // 2
    conv = jnp.concatenate([back_ref[s, :chans, :] for s in range(parts)], axis=0)
    vals = jnp.concatenate([back_ref[s, chans:, :] for s in range(parts)], axis=0)
    gate_ref[0] = (grad_ref[0].astype(F32) * conv.astype(F32).T).astype(BF16)
    val_ref[0] = vals.astype(F32).T.astype(BF16)


def sum_over_dp(part, count):
    terms = [part.astype(F32)] + [
        lax.ppermute(part, "dp", [(j, j ^ d) for j in range(count)]).astype(F32)
        for d in range(1, count)
    ]
    while len(terms) > 1:
        terms = [a + b for a, b in zip(terms[::2], terms[1::2])]
    return terms[0]


def per_device_short(values, gates, grad_out, filters, skip):
    chans, length = filters.shape
    parts = lax.axis_size("ctx")
    seqs = lax.axis_size("dp")
    _, pos, width = values.shape
    rows = 2 * chans
    high, low, inv = dense_tables(length)
    params = pltpu.CompilerParams(vmem_limit_bytes=VMEM_BYTES)
    sent = pl.pallas_call(
        functools.partial(pack_kernel, parts),
        out_shape=jax.ShapeDtypeStruct((parts, rows, pos), BF16),
        in_specs=vmem_specs(3),
        out_specs=vmem_specs(1)[0],
        compiler_params=params,
        name="pack",
    )(values, gates, grad_out)
    held = lax.all_to_all(sent, "ctx", split_axis=0, concat_axis=0, tiled=True)
    fwd = in_vmem(jnp.asarray(high))
    spec = pl.pallas_call(
        filter_kernel,
        out_shape=jax.ShapeDtypeStruct((chans, 2 * length), F32),
        in_specs=vmem_specs(3),
        out_specs=vmem_specs(1)[0],
        compiler_params=params,
        cost_estimate=pl.CostEstimate(
            flops=12 * chans * length * length, bytes_accessed=8 * length * length, transcendentals=0
        ),
        name="filter_spectrum",
    )(filters, fwd, in_vmem(jnp.asarray(low)))
    back, cross = pl.pallas_call(
        main_kernel,
        out_shape=(
            jax.ShapeDtypeStruct((parts, rows, pos), BF16),
            jax.ShapeDtypeStruct((chans, length), BF16),
        ),
        in_specs=vmem_specs(5),
        out_specs=tuple(vmem_specs(2)),
        compiler_params=params,
        name="products",
    )(held, fwd, in_vmem(jnp.asarray(inv)), in_vmem(spec), skip.reshape(1, chans))
    total = sum_over_dp(cross, seqs)
    home = lax.all_to_all(back, "ctx", split_axis=0, concat_axis=0, tiled=True)
    grad_values, grad_gates = pl.pallas_call(
        unpack_kernel,
        out_shape=(
            jax.ShapeDtypeStruct((1, pos, width), BF16),
            jax.ShapeDtypeStruct((1, pos, width), BF16),
        ),
        in_specs=vmem_specs(2),
        out_specs=tuple(vmem_specs(2)),
        compiler_params=params,
        name="unpack",
    )(home, grad_out)
    return (grad_values, grad_gates, (seqs * length) ** (-0.5) * total)


def per_device(values, gates, grad_out, filters, skip):
    seqs = lax.axis_size("dp")
    if filters.shape[1] <= DENSE_LIMIT and seqs & (seqs - 1) == 0:
        return per_device_short(values, gates, grad_out, filters, skip)
    return per_device_long(values, gates, grad_out, filters, skip)


def solution(mesh):
    in_specs = (
        P("dp", "ctx", None),
        P("dp", "ctx", None),
        P("dp", "ctx", None),
        P("ctx", None),
        P("ctx"),
    )
    out_specs = (P("dp", "ctx", None), P("dp", "ctx", None), P("ctx", None))
    return jax.shard_map(
        per_device, mesh=mesh, in_specs=in_specs, out_specs=out_specs, check_vma=False
    )
```

profile of v0, /device:TPU:0, one launch (start us, length us, event | category | flops | bytes accessed | tf_op | source)
XLA Modules:
  0.0 45.5 jit_solution(12369529872566931218)
XLA Ops:
  0.6 0.0 copy-start.5
  0.6 0.9 %copy-done.5 = bf16[1,128,512]{2,1,0:T(8,128)(2,1)S(1)} copy-done((bf16[1,128,512]{2,1,0:T(8,128)(2,1)S(1)}, bf16[1,128,512]{2,1,0:T(8,128)(2,1)}, u32[]{:S(2)}) %copy-start.5) | copy-done | bytes 131096
  1.5 0.9 %copy-done.7 = bf16[1,128,512]{2,1,0:T(8,128)(2,1)S(1)} copy-done((bf16[1,128,512]{2,1,0:T(8,128)(2,1)S(1)}, bf16[1,128,512]{2,1,0:T(8,128)(2,1)}, u32[]{:S(2)}) %copy-start.7) | copy-done | bytes 131096
  2.4 0.9 %copy-done.8 = bf16[1,128,512]{2,1,0:T(8,128)(2,1)S(1)} copy-done((bf16[1,128,512]{2,1,0:T(8,128)(2,1)S(1)}, bf16[1,128,512]{2,1,0:T(8,128)(2,1)}, u32[]{:S(2)}) %copy-start.8) | copy-done | bytes 131096
  3.3 0.8 %pack.1 = bf16[8,128,128]{2,1,0:T(8,128)(2,1)} custom-call(bf16[1,128,512]{2,1,0:T(8,128)(2,1)S(1)} %copy-done.7, bf16[1,128,512]{2,1,0:T(8,128)(2,1)S(1)} %copy-done.8, bf16[1,128,512]{2,1,0:T(8,128)(2,1)S(1)} %copy-done.5), custom_call_target="tpu_custom_call" | custom-call | tf_op jit(solution)/shard_map/pack/pallas_call | solution.py:211
  4.2 5.2 %all-to-all-start = ((bf16[8,128,128]{2,1,0:T(8,128)(2,1)}), bf16[8,128,128]{2,1,0:T(8,128)(2,1)S(1)}, u32[]{:S(2)}, u32[]{:S(2)}) async-start(bf16[8,128,128]{2,1,0:T(8,128)(2,1)} %pack.1), calls=%async_computation | async-start | bytes 524288 | tf_op jit(solution)/shard_map/all_to_all | solution.py:219
  9.4 2.2 %copy-done = bf16[1024,2048]{1,0:T(8,128)(2,1)S(1)} copy-done((bf16[1024,2048]{1,0:T(8,128)(2,1)S(1)}, bf16[1024,2048]{1,0:T(8,128)(2,1)}, u32[]{:S(2)}) %copy-start) | copy-done | bytes 4194328
  11.5 2.2 %copy-done.3 = bf16[1024,2048]{1,0:T(8,128)(2,1)S(1)} copy-done((bf16[1024,2048]{1,0:T(8,128)(2,1)S(1)}, bf16[1024,2048]{1,0:T(8,128)(2,1)}, u32[]{:S(2)}) %copy-start.3) | copy-done | bytes 4194328
  13.7 4.0 %filter_spectrum.1.filt_ref = f32[64,2048]{1,0:T(8,128)} custom-call(f32[64,1024]{1,0:T(8,128)} %filt_ref.1, bf16[1024,2048]{1,0:T(8,128)(2,1)S(1)} %copy-done, bf16[1024,2048]{1,0:T(8,128)(2,1)S(1)} %copy-done.3), custom_call_target="tpu_custom_call" | custom-call | flops 805306368 | bytes 8388608 | tf_op jit(solution)/shard_map/filter_spectrum/pallas_call | solution.py:221
  17.8 0.0 all-to-all-done.x_ref
  17.8 0.7 %copy-done.9 = bf16[8,128,128]{2,1,0:T(8,128)(2,1)} copy-done((bf16[8,128,128]{2,1,0:T(8,128)(2,1)}, bf16[8,128,128]{2,1,0:T(8,128)(2,1)S(1)}, u32[]{:S(2)}) %copy-start.9) | copy-done | bytes 262168
  18.5 2.2 %copy-done.1 = bf16[1024,2048]{1,0:T(8,128)(2,1)S(1)} copy-done((bf16[1024,2048]{1,0:T(8,128)(2,1)S(1)}, bf16[1024,2048]{1,0:T(8,128)(2,1)}, u32[]{:S(2)}) %copy-start.1) | copy-done | bytes 4194328
  20.7 2.2 %copy-done.2 = bf16[2048,1024]{1,0:T(8,128)(2,1)S(1)} copy-done((bf16[2048,1024]{1,0:T(8,128)(2,1)S(1)}, bf16[2048,1024]{1,0:T(8,128)(2,1)}, u32[]{:S(2)}) %copy-start.2) | copy-done | bytes 4194328
  22.9 1.0 %copy-done.4 = f32[64,2048]{1,0:T(8,128)S(1)} copy-done((f32[64,2048]{1,0:T(8,128)S(1)}, f32[64,2048]{1,0:T(8,128)}, u32[]{:S(2)}) %copy-start.4) | copy-done | bytes 524312
  23.9 3.5 %products.1 = (bf16[8,128,128]{2,1,0:T(8,128)(2,1)}, bf16[64,1024]{1,0:T(8,128)(2,1)}) custom-call(bf16[8,128,128]{2,1,0:T(8,128)(2,1)} %copy-done.9, bf16[1024,2048]{1,0:T(8,128)(2,1)S(1)} %copy-done.1, bf16[2048,1024]{1,0:T(8,128)(2,1)S(1)} %copy-done.2, f32[64,2048]{1,0:T(8,128)S(1)} %copy-done.4, f32[1,64]{1,0:T(1,128)} %bitcast.1), custom_call_target="tpu_custom_call" | custom-call | tf_op jit(solution)/shard_map/products/pallas_call | solution.py:232
  27.4 3.6 %collective-permute-start.2 = (bf16[64,1024]{1,0:T(8,128)(2,1)}, bf16[64,1024]{1,0:T(8,128)(2,1)S(1)}, u32[]{:S(2)}, u32[]{:S(2)}) collective-permute-start(bf16[64,1024]{1,0:T(8,128)(2,1)} %get-tuple-element.10), channel_id=1, source_target_pairs={{0,24},{8,16},{16,8},{24,0},{1,25},{9,17},{17,9},{25,1},{2,26},{10... | collective-permute-start | bytes 393224 | tf_op jit(solution)/shard_map/ppermute | solution.py:195
  31.0 0.0 collective-permute-start.1
  31.0 0.8 %collective-permute-start = (bf16[64,1024]{1,0:T(8,128)(2,1)}, bf16[64,1024]{1,0:T(8,128)(2,1)S(1)}, u32[]{:S(2)}, u32[]{:S(2)}) collective-permute-start(bf16[64,1024]{1,0:T(8,128)(2,1)} %get-tuple-element.10), channel_id=1, source_target_pairs={{0,8},{8,0},{16,24},{24,16},{1,9},{9,1},{17,25},{25,17},{2,10},{10... | collective-permute-start | bytes 393224 | tf_op jit(solution)/shard_map/ppermute | solution.py:195
  31.8 4.2 %all-to-all-start.1 = ((bf16[8,128,128]{2,1,0:T(8,128)(2,1)}), bf16[8,128,128]{2,1,0:T(8,128)(2,1)S(1)}, u32[]{:S(2)}, u32[]{:S(2)}) async-start(bf16[8,128,128]{2,1,0:T(8,128)(2,1)} %get-tuple-element.7), calls=%async_computation.1 | async-start | bytes 524288 | tf_op jit(solution)/shard_map/all_to_all | solution.py:244
  36.0 7.0 %collective-permute-done.1 = bf16[64,1024]{1,0:T(8,128)(2,1)S(1)} collective-permute-done((bf16[64,1024]{1,0:T(8,128)(2,1)}, bf16[64,1024]{1,0:T(8,128)(2,1)S(1)}, u32[]{:S(2)}, u32[]{:S(2)}) %collective-permute-start.1) | collective-permute-done | bytes 131104 | tf_op jit(solution)/shard_map/ppermute | solution.py:195
  43.0 0.0 collective-permute-done
  43.0 1.7 %add_multiply_fusion = f32[64,1024]{1,0:T(8,128)} fusion(bf16[64,1024]{1,0:T(8,128)(2,1)S(1)} %collective-permute-done.2, bf16[64,1024]{1,0:T(8,128)(2,1)S(1)} %collective-permute-done.1, bf16[64,1024]{1,0:T(8,128)(2,1)S(1)} %collective-permute-done, bf16[64,1024]{1,0:T(8,128)(2,1)} %get-tuple-element.10), kind=kLoop, calls=%fused_computation | loop fusion | flops 524288 | bytes 786432 | tf_op jit(solution)/shard_map/mul | solution.py:256
  44.7 0.0 all-to-all-done.1.back_ref
  44.7 0.8 %unpack.1 = (bf16[1,128,512]{2,1,0:T(8,128)(2,1)}, bf16[1,128,512]{2,1,0:T(8,128)(2,1)}) custom-call(bf16[8,128,128]{2,1,0:T(8,128)(2,1)S(1)} %all-to-all-done.1.back_ref, bf16[1,128,512]{2,1,0:T(8,128)(2,1)S(1)} %copy-done.6), custom_call_target="tpu_custom_call" | custom-call | tf_op jit(solution)/shard_map/unpack/pallas_call | solution.py:245
  (11 shorter events, 0.0 us)
Async XLA Ops:
  0.6 0.9 %copy-start.5 = (bf16[1,128,512]{2,1,0:T(8,128)(2,1)S(1)}, bf16[1,128,512]{2,1,0:T(8,128)(2,1)}, u32[]{:S(2)}) copy-start(bf16[1,128,512]{2,1,0:T(8,128)(2,1)} %grad_ref.3) | copy-start | bytes 393220
  1.5 0.9 %copy-start.7 = (bf16[1,128,512]{2,1,0:T(8,128)(2,1)S(1)}, bf16[1,128,512]{2,1,0:T(8,128)(2,1)}, u32[]{:S(2)}) copy-start(bf16[1,128,512]{2,1,0:T(8,128)(2,1)} %vals_ref.1) | copy-start | bytes 393220
  2.4 0.9 %copy-start.8 = (bf16[1,128,512]{2,1,0:T(8,128)(2,1)S(1)}, bf16[1,128,512]{2,1,0:T(8,128)(2,1)}, u32[]{:S(2)}) copy-start(bf16[1,128,512]{2,1,0:T(8,128)(2,1)} %gate_ref.1) | copy-start | bytes 393220
  4.2 13.6 %all-to-all-start = ((bf16[8,128,128]{2,1,0:T(8,128)(2,1)}), bf16[8,128,128]{2,1,0:T(8,128)(2,1)S(1)}, u32[]{:S(2)}, u32[]{:S(2)}) async-start(bf16[8,128,128]{2,1,0:T(8,128)(2,1)} %pack.1), calls=%async_computation | async-start | bytes 524288 | tf_op jit(solution)/shard_map/all_to_all | solution.py:219
  9.4 2.2 %copy-start = (bf16[1024,2048]{1,0:T(8,128)(2,1)S(1)}, bf16[1024,2048]{1,0:T(8,128)(2,1)}, u32[]{:S(2)}) copy-start(bf16[1024,2048]{1,0:T(8,128)(2,1)} %constant.8.clone.high_ref.fwd_ref) | copy-start | bytes 12582916
  11.5 2.2 %copy-start.3 = (bf16[1024,2048]{1,0:T(8,128)(2,1)S(1)}, bf16[1024,2048]{1,0:T(8,128)(2,1)}, u32[]{:S(2)}) copy-start(bf16[1024,2048]{1,0:T(8,128)(2,1)} %constant.9.clone.low_ref) | copy-start | bytes 12582916
  17.8 0.7 %copy-start.9 = (bf16[8,128,128]{2,1,0:T(8,128)(2,1)}, bf16[8,128,128]{2,1,0:T(8,128)(2,1)S(1)}, u32[]{:S(2)}) copy-start(bf16[8,128,128]{2,1,0:T(8,128)(2,1)S(1)} %all-to-all-done.x_ref) | copy-start | bytes 786436
  18.5 2.2 %copy-start.1 = (bf16[1024,2048]{1,0:T(8,128)(2,1)S(1)}, bf16[1024,2048]{1,0:T(8,128)(2,1)}, u32[]{:S(2)}) copy-start(bf16[1024,2048]{1,0:T(8,128)(2,1)} %constant.8.clone.high_ref.fwd_ref) | copy-start | bytes 12582916
  20.7 2.2 %copy-start.2 = (bf16[2048,1024]{1,0:T(8,128)(2,1)S(1)}, bf16[2048,1024]{1,0:T(8,128)(2,1)}, u32[]{:S(2)}) copy-start(bf16[2048,1024]{1,0:T(8,128)(2,1)} %constant.10.clone.inv_ref) | copy-start | bytes 12582916
  22.9 1.0 %copy-start.4 = (f32[64,2048]{1,0:T(8,128)S(1)}, f32[64,2048]{1,0:T(8,128)}, u32[]{:S(2)}) copy-start(f32[64,2048]{1,0:T(8,128)} %filter_spectrum.1.filt_ref) | copy-start | bytes 1572868
  23.9 20.8 %copy-start.6 = (bf16[1,128,512]{2,1,0:T(8,128)(2,1)S(1)}, bf16[1,128,512]{2,1,0:T(8,128)(2,1)}, u32[]{:S(2)}) copy-start(bf16[1,128,512]{2,1,0:T(8,128)(2,1)} %grad_ref.3) | copy-start | bytes 393220
  27.4 8.6 %collective-permute-start.2 = (bf16[64,1024]{1,0:T(8,128)(2,1)}, bf16[64,1024]{1,0:T(8,128)(2,1)S(1)}, u32[]{:S(2)}, u32[]{:S(2)}) collective-permute-start(bf16[64,1024]{1,0:T(8,128)(2,1)} %get-tuple-element.10), channel_id=1, source_target_pairs={{0,24},{8,16},{16,8},{24,0},{1,25},{9,17},{17,9},{25,1},{2,26},{10... | collective-permute-start | bytes 393224 | tf_op jit(solution)/shard_map/ppermute | solution.py:195
  31.0 12.0 %collective-permute-start.1 = (bf16[64,1024]{1,0:T(8,128)(2,1)}, bf16[64,1024]{1,0:T(8,128)(2,1)S(1)}, u32[]{:S(2)}, u32[]{:S(2)}) collective-permute-start(bf16[64,1024]{1,0:T(8,128)(2,1)} %get-tuple-element.10), channel_id=1, source_target_pairs={{0,16},{8,24},{16,0},{24,8},{1,17},{9,25},{17,1},{25,9},{2,18},{10... | collective-permute-start | bytes 393224 | tf_op jit(solution)/shard_map/ppermute | solution.py:195
  31.0 12.0 %collective-permute-start = (bf16[64,1024]{1,0:T(8,128)(2,1)}, bf16[64,1024]{1,0:T(8,128)(2,1)S(1)}, u32[]{:S(2)}, u32[]{:S(2)}) collective-permute-start(bf16[64,1024]{1,0:T(8,128)(2,1)} %get-tuple-element.10), channel_id=1, source_target_pairs={{0,8},{8,0},{16,24},{24,16},{1,9},{9,1},{17,25},{25,17},{2,10},{10... | collective-permute-start | bytes 393224 | tf_op jit(solution)/shard_map/ppermute | solution.py:195
  31.8 12.9 %all-to-all-start.1 = ((bf16[8,128,128]{2,1,0:T(8,128)(2,1)}), bf16[8,128,128]{2,1,0:T(8,128)(2,1)S(1)}, u32[]{:S(2)}, u32[]{:S(2)}) async-start(bf16[8,128,128]{2,1,0:T(8,128)(2,1)} %get-tuple-element.7), calls=%async_computation.1 | async-start | bytes 524288 | tf_op jit(solution)/shard_map/all_to_all | solution.py:244
where the time goes:
time: 46.1 us; the launch traced here: 45.5 us
  starting transfers between devices  13.8 us (30%)
  local copies, waits for them, and re-layouts  13.2 us (29%)
  Pallas kernels  9.22 us (20%)
  waiting for transfers between devices  6.98 us (15%)
  other arithmetic  1.68 us (4%)
  between operations  0.66 us (1%)
    unnamed x20, local copies, waits for them, and re-layouts  13.2 us
    ppermute x3, waiting for transfers between devices, sum_over_dp(): lax.ppermute(part, 'dp', [(j, j ^ d) for j in range(count)]).astype(F32)  6.97 us
    all_to_all x1, starting transfers between devices, per_device_short(): held = lax.all_to_all(sent, 'ctx', split_axis=0, concat_axis=0, tiled=True)  5.17 us
    ppermute x3, starting transfers between devices, sum_over_dp(): lax.ppermute(part, 'dp', [(j, j ^ d) for j in range(count)]).astype(F32)  4.39 us
    all_to_all x1, starting transfers between devices, per_device_short(): home = lax.all_to_all(back, 'ctx', split_axis=0, concat_axis=0, tiled=True)  4.2 us
    pallas_call x1, Pallas kernels, per_device_short(): pl.pallas_call(filter_kernel, out_shape=jax.ShapeDtypeStruct((chans, 2 *...  4.05 us
    pallas_call x1, Pallas kernels, per_device_short(): pl.pallas_call(main_kernel, out_shape=(jax.ShapeDtypeStruct((parts, rows,...  3.53 us
    mul x1, other arithmetic, per_device_short(): return (grad_values, grad_gates, (seqs * length) ** (-0.5) * total)  1.68 us
  transfers between devices with their start and end apart: 5, of which 1 were waited for; matrix products, arithmetic and copies ran while one was open for 4% of the time, Pallas kernels for 9%

commit v1 on v0

v1 whole, which is shorter than its diff:
```python
import functools
import math

import jax
import jax.numpy as jnp
import numpy as np
from jax import lax
from jax.experimental import pallas as pl
from jax.experimental.pallas import tpu as pltpu
from jax.sharding import PartitionSpec as P

HIGH = lax.Precision.HIGHEST
BF16 = jnp.bfloat16
F32 = jnp.float32
DENSE_LIMIT = 1024
VMEM_BYTES = 16 * 2**20


def twiddle(rows, cols, period):
    left = lax.broadcasted_iota(jnp.int32, (rows, cols), 0)
    right = lax.broadcasted_iota(jnp.int32, (rows, cols), 1)
    angle = (left * right % period).astype(jnp.float32) * (2.0 * math.pi / period)
    return (jnp.cos(angle), jnp.sin(angle))


def pick_first(period):
    best = 2
    for cand in range(2, math.isqrt(period) + 1):
        if period % cand == 0 and cand % 2 == 0:
            best = cand
    return best


def make_tables(length):
    period = 2 * length
    first = pick_first(period)
    second = period // first
    half = first // 2
    return (
        twiddle(half, first, first),
        twiddle(first, second, period),
        twiddle(second, second, second),
        half,
        first,
        second,
        period,
    )


def forward(signal, tables):
    (cos_one, sin_one), (cos_mid, sin_mid), (cos_two, sin_two), half, first, second, period = tables
    shaped = signal.reshape(signal.shape[0], half, second)
    part_re = jnp.einsum("cmn,mk->ckn", shaped, cos_one, precision=HIGH)
    part_im = -jnp.einsum("cmn,mk->ckn", shaped, sin_one, precision=HIGH)
    mid_re = part_re * cos_mid + part_im * sin_mid
    mid_im = part_im * cos_mid - part_re * sin_mid
    spec_re = jnp.einsum("ckn,nm->ckm", mid_re, cos_two, precision=HIGH) + jnp.einsum(
        "ckn,nm->ckm", mid_im, sin_two, precision=HIGH
    )
    spec_im = jnp.einsum("ckn,nm->ckm", mid_im, cos_two, precision=HIGH) - jnp.einsum(
        "ckn,nm->ckm", mid_re, sin_two, precision=HIGH
    )
    return (spec_re, spec_im)


def inverse(spec_re, spec_im, tables):
    (cos_one, sin_one), (cos_mid, sin_mid), (cos_two, sin_two), half, first, second, period = tables
    back_re = jnp.einsum("ckm,nm->ckn", spec_re, cos_two, precision=HIGH) - jnp.einsum(
        "ckm,nm->ckn", spec_im, sin_two, precision=HIGH
    )
    back_im = jnp.einsum("ckm,nm->ckn", spec_im, cos_two, precision=HIGH) + jnp.einsum(
        "ckm,nm->ckn", spec_re, sin_two, precision=HIGH
    )
    turned_re = back_re * cos_mid - back_im * sin_mid
    turned_im = back_im * cos_mid + back_re * sin_mid
    result = jnp.einsum("ckn,mk->cmn", turned_re, cos_one, precision=HIGH) - jnp.einsum(
        "ckn,mk->cmn", turned_im, sin_one, precision=HIGH
    )
    return result.reshape(spec_re.shape[0], half * second) * (1.0 / period)


def spectral(vals_f, dz_f, filt, gains, tables, scale_a):
    vals_re, vals_im = forward(vals_f, tables)
    dz_re, dz_im = forward(dz_f, tables)
    filt_re, filt_im = forward(filt, tables)
    conv_raw = inverse(
        filt_re * vals_re - filt_im * vals_im, filt_re * vals_im + filt_im * vals_re, tables
    )
    conv = (scale_a * conv_raw + gains * vals_f).astype(BF16)
    corr = inverse(filt_re * dz_re + filt_im * dz_im, filt_re * dz_im - filt_im * dz_re, tables)
    grad_val = (scale_a * corr + gains * dz_f).astype(BF16)
    cross = inverse(vals_re * dz_re + vals_im * dz_im, vals_re * dz_im - vals_im * dz_re, tables)
    return (grad_val, conv, cross)


def per_device_long(values, gates, grad_out, filters, skip):
    length = filters.shape[1]
    scale_a = length ** (-0.5)
    scale_b = (lax.axis_size("dp") * length) ** (-0.5)
    tok_grad = grad_out[0].astype(F32)
    dz_tok = (tok_grad * gates[0].astype(F32)).astype(BF16)
    vals_ch, dz_ch = (
        lax.all_to_all(values[0].T, "ctx", split_axis=0, concat_axis=1, tiled=True),
        lax.all_to_all(dz_tok.T, "ctx", split_axis=0, concat_axis=1, tiled=True),
    )
    grad_val, conv, cross = spectral(
        vals_ch.astype(F32),
        dz_ch.astype(F32),
        filters,
        skip[:, None],
        make_tables(length),
        scale_a,
    )
    total = lax.psum(cross, "dp")
    val_back, conv_back = (
        lax.all_to_all(grad_val, "ctx", split_axis=1, concat_axis=0, tiled=True),
        lax.all_to_all(conv, "ctx", split_axis=1, concat_axis=0, tiled=True),
    )
    grad_gate_tok = (tok_grad * conv_back.T.astype(F32)).astype(BF16)
    return (val_back.T[None], grad_gate_tok[None], scale_b * total)


def dense_tables(half):
    n = np.arange(half, dtype=np.int64)[:, None]
    k = np.concatenate([np.arange(0, half, 2), np.arange(1, half, 2)])[None, :]
    angle = ((2 * k + 1) * n % (4 * half)).astype(np.float64) * (math.pi / (2 * half))
    full = np.concatenate([np.cos(angle), -np.sin(angle)], axis=1).astype(BF16)
    return full, np.ascontiguousarray(full.T)


def vmem_specs(count):
    return [pl.BlockSpec(memory_space=pltpu.VMEM)] * count


def hbm_specs(count):
    return [pl.BlockSpec(memory_space=pltpu.HBM)] * count


def in_vmem(array):
    return pltpu.with_memory_space_constraint(array, pltpu.VMEM)


def in_hbm(array):
    return pltpu.with_memory_space_constraint(array, pltpu.HBM)


def start_copies(pairs, sems):
    copies = [pltpu.make_async_copy(a, b, sems.at[i]) for i, (a, b) in enumerate(pairs)]
    for copy in copies:
        copy.start()
    return copies


def pack_kernel(parts, vals_hbm, gate_hbm, grad_hbm, out_ref, grad_ref, vals_ref, gate_ref, sems):
    chans = vals_ref.shape[2] // parts
    copies = start_copies(
        [(vals_hbm, vals_ref), (gate_hbm, gate_ref), (grad_hbm, grad_ref)], sems
    )
    copies[0].wait()
    vals = vals_ref[0].astype(F32).T.astype(BF16)
    for d in range(parts):
        out_ref[d, :chans, :] = vals[d * chans : (d + 1) * chans, :]
    copies[1].wait()
    copies[2].wait()
    dz = (grad_ref[0].astype(F32) * gate_ref[0].astype(F32)).T.astype(BF16)
    for d in range(parts):
        out_ref[d, chans:, :] = dz[d * chans : (d + 1) * chans, :]


def filter_kernel(filt_hbm, fwd_hbm, inv_hbm, spec_ref, fwd_ref, inv_ref, filt_ref, sems):
    copies = start_copies([(filt_hbm, filt_ref), (fwd_hbm, fwd_ref), (inv_hbm, inv_ref)], sems)
    half = fwd_ref.shape[0]
    copies[0].wait()
    filt = jnp.concatenate([filt_ref[:, :half], filt_ref[:, half:]], axis=0)
    high = filt.astype(BF16)
    low = (filt - high.astype(F32)).astype(BF16)
    copies[1].wait()
    both = jnp.dot(
        jnp.concatenate([high, low], axis=0), fwd_ref[...], preferred_element_type=F32
    )
    spec_ref[...] = both[: filt.shape[0]] + both[filt.shape[0] :]
    copies[2].wait()


def mul(a, b):
    return (a[0] * b[0] - a[1] * b[1], a[0] * b[1] + a[1] * b[0])


def conj_mul(a, b):
    return (a[0] * b[0] + a[1] * b[1], a[0] * b[1] - a[1] * b[0])


def add(a, b):
    return (a[0] + b[0], a[1] + b[1])


def later(a, odd):
    return (a[1], -a[0]) if odd else (-a[1], a[0])


def main_kernel(
    x_ref, fwd_ref, inv_ref, filt_ref, skip_ref, back_ref, cross_ref, spec_ref, prod_ref
):
    parts, rows, pos = x_ref.shape
    chans = rows // 2
    half = parts // 2 * pos
    x = [
        jnp.concatenate([x_ref[s] for s in range(parts // 2)], axis=1),
        jnp.concatenate([x_ref[s] for s in range(parts // 2, parts)], axis=1),
    ]
    spec_ref[...] = jnp.dot(
        jnp.concatenate(x, axis=0), fwd_ref[...], preferred_element_type=F32
    )
    for r in range(0, chans, 16):
        for c in range(0, half, 128):
            odd = c >= half // 2

            def load(ref, row):
                at = slice(row + r, row + r + 16)
                return (ref[at, c : c + 128], ref[at, half + c : half + c + 128])

            v0, g0, v1, g1 = [load(spec_ref, i * chans) for i in range(4)]
            h0, h1 = [load(filt_ref, i * chans) for i in range(2)]
            conv0 = mul(h0, v0)
            conv1 = add(add(mul(h0, v1), mul(h1, v0)), later(conv0, odd))
            corr1 = conj_mul(h0, g1)
            corr0 = add(add(conj_mul(h0, g0), conj_mul(h1, g1)), later(corr1, not odd))
            cross1 = conj_mul(v0, g1)
            cross0 = add(add(conj_mul(v0, g0), conj_mul(v1, g1)), later(cross1, not odd))
            for i, (re, im) in enumerate((conv0, corr0, cross0, conv1, corr1, cross1)):
                at = slice(i * chans + r, i * chans + r + 16)
                prod_ref[at, c : c + 128] = re.astype(BF16)
                prod_ref[at, half + c : half + c + 128] = im.astype(BF16)
    res = jnp.dot(prod_ref[...], inv_ref[...], preferred_element_type=F32)
    row = lax.broadcasted_iota(jnp.int32, (chans, chans), 0)
    col = lax.broadcasted_iota(jnp.int32, (chans, chans), 1)
    gain = jnp.sum(jnp.where(row == col, skip_ref[...], 0.0), axis=1, keepdims=True)
    gains = jnp.concatenate([gain, gain], axis=0)
    scale = (2 * half) ** -0.5 / half
    for i in range(2):
        top = i * 3 * chans
        cross_ref[:, i * half : (i + 1) * half] = (
            res[top + rows : top + rows + chans] * (1.0 / half)
        ).astype(BF16)
        both = (res[top : top + rows] * scale + gains * x[i].astype(F32)).astype(BF16)
        for s in range(parts // 2):
            back_ref[i * (parts // 2) + s] = both[:, s * pos : (s + 1) * pos]


def unpack_kernel(back_ref, grad_ref, val_hbm, gate_hbm, val_ref, gate_ref, sems):
    parts, rows, _ = back_ref.shape
    chans = rows // 2
    vals = jnp.concatenate([back_ref[s, chans:, :] for s in range(parts)], axis=0)
    val_ref[0] = vals.astype(F32).T.astype(BF16)
    first = start_copies([(val_ref, val_hbm)], sems)
    conv = jnp.concatenate([back_ref[s, :chans, :] for s in range(parts)], axis=0)
    gate_ref[0] = (grad_ref[0].astype(F32) * conv.astype(F32).T).astype(BF16)
    second = pltpu.make_async_copy(gate_ref, gate_hbm, sems.at[1])
    second.start()
    first[0].wait()
    second.wait()


def total_kernel(scale, *refs):
    part_refs, out_hbm, out_ref, sems = refs[:-3], refs[-3], refs[-2], refs[-1]
    half = out_ref.shape[0] // 2
    copies = []
    for i in range(2):
        at = pl.ds(i * half, half)
        terms = [ref[at, :].astype(F32) for ref in part_refs]
        while len(terms) > 1:
            terms = [a + b for a, b in zip(terms[::2], terms[1::2])]
        out_ref[at, :] = terms[0] * scale
        copies.append(pltpu.make_async_copy(out_ref.at[at, :], out_hbm.at[at, :], sems.at[i]))
        copies[-1].start()
    for copy in copies:
        copy.wait()


def call(kernel, name, outs, ins, in_specs, scratch=(), sems=0, flops=0, moved=0):
    return pl.pallas_call(
        kernel,
        out_shape=tuple(
            pltpu.VMEM(shape, dtype) if near else jax.ShapeDtypeStruct(shape, dtype)
            for shape, dtype, near in outs
        ),
        in_specs=in_specs,
        out_specs=tuple(vmem_specs(1)[0] if near else hbm_specs(1)[0] for _, _, near in outs),
        scratch_shapes=[pltpu.VMEM(s, t) for s, t in scratch]
        + ([pltpu.SemaphoreType.DMA((sems,))] if sems else []),
        compiler_params=pltpu.CompilerParams(vmem_limit_bytes=VMEM_BYTES),
        cost_estimate=pl.CostEstimate(flops=flops, bytes_accessed=moved, transcendentals=0),
        name=name,
    )(*ins)


def per_device_short(values, gates, grad_out, filters, skip):
    chans, length = filters.shape
    parts = lax.axis_size("ctx")
    seqs = lax.axis_size("dp")
    _, pos, width = values.shape
    rows = 2 * chans
    fwd, inv = (jnp.asarray(table) for table in dense_tables(length // 2))
    token = ((1, pos, width), BF16)
    sent, grad_near = call(
        functools.partial(pack_kernel, parts),
        "pack",
        [((parts, rows, pos), BF16, True), (*token, True)],
        tuple(in_hbm(x) for x in (values, gates, grad_out)),
        hbm_specs(3),
        scratch=[token, token],
        sems=3,
        moved=8 * pos * width,
    )
    held = lax.all_to_all(sent, "ctx", split_axis=0, concat_axis=0, tiled=True)
    spec, fwd_near, inv_near = call(
        filter_kernel,
        "filter_spectrum",
        [((rows, length), F32, True), (fwd.shape, BF16, True), (inv.shape, BF16, True)],
        tuple(in_hbm(x) for x in (filters, fwd, inv)),
        hbm_specs(3),
        scratch=[((chans, length), F32)],
        sems=3,
        flops=4 * chans * length * length,
        moved=8 * length * length,
    )
    back, cross = call(
        main_kernel,
        "products",
        [((parts, rows, pos), BF16, True), ((chans, length), BF16, True)],
        (in_vmem(held), in_vmem(fwd_near), in_vmem(inv_near), in_vmem(spec), skip.reshape(1, chans)),
        vmem_specs(5),
        scratch=[((2 * rows, length), F32), ((3 * rows, length), BF16)],
        flops=10 * chans * length * length,
        moved=8 * length * length,
    )
    others = [
        lax.ppermute(cross, "dp", [(j, j ^ d) for j in range(seqs)]) for d in range(1, seqs)
    ]
    home = lax.all_to_all(back, "ctx", split_axis=0, concat_axis=0, tiled=True)
    grad_values, grad_gates = call(
        unpack_kernel,
        "unpack",
        [(*token, False), (*token, False)],
        (in_vmem(home), in_vmem(grad_near)),
        vmem_specs(2),
        scratch=[token, token],
        sems=2,
        moved=10 * pos * width,
    )
    (grad_filters,) = call(
        functools.partial(total_kernel, (seqs * length) ** (-0.5)),
        "total",
        [((chans, length), F32, False)],
        tuple(in_vmem(part) for part in [cross] + others),
        vmem_specs(seqs),
        scratch=[((chans, length), F32)],
        sems=2,
        moved=12 * chans * length,
    )
    return (grad_values, grad_gates, grad_filters)


def per_device(values, gates, grad_out, filters, skip):
    chans, length = filters.shape
    pos = values.shape[1]
    seqs = lax.axis_size("dp")
    dense = length <= DENSE_LIMIT and length % 512 == 0 and chans % 16 == 0 and pos % 128 == 0
    if dense and seqs & (seqs - 1) == 0:
        return per_device_short(values, gates, grad_out, filters, skip)
    return per_device_long(values, gates, grad_out, filters, skip)


def solution(mesh):
    in_specs = (
        P("dp", "ctx", None),
        P("dp", "ctx", None),
        P("dp", "ctx", None),
        P("ctx", None),
        P("ctx"),
    )
    out_specs = (P("dp", "ctx", None), P("dp", "ctx", None), P("ctx", None))
    return jax.shard_map(
        per_device, mesh=mesh, in_specs=in_specs, out_specs=out_specs, check_vma=False
    )
```

time: 46.1 us -> 37.9 us (0.82)
  local copies, waits for them, and re-layouts: 13.2 us -> 0.66 us
  waiting for transfers between devices: 6.98 us -> 15.9 us
  Pallas kernels: 9.22 us -> 7.21 us
  other arithmetic: 1.68 us -> 0 us
  starting transfers between devices: 13.8 us -> 13 us
    unnamed x20 -> x2, local copies, waits for them, and re-layouts: 13.2 us -> 0.66 us
    all_to_all x1, waiting for transfers between devices: 0.01 us -> 5.15 us  [per_device_short(): held = lax.all_to_all(sent, 'ctx', split_axis=0, concat_axis=0, tiled=True)]
    ppermute x3, waiting for transfers between devices: 6.97 us -> 10.8 us  [per_device_short(): lax.ppermute(cross, 'dp', [(j, j ^ d) for j in range(seqs)])]
    pallas_call x4 -> x5, Pallas kernels: 9.22 us -> 7.21 us  [call(): pl.pallas_call(kernel, out_shape=tuple((pltpu.VMEM(shape, dtype) if near...]
    mul x1 -> x0, other arithmetic: 1.68 us -> none  [per_device_short(): return (grad_values, grad_gates, (seqs * length) ** (-0.5) * total)]
    all_to_all x1, starting transfers between devices: 4.2 us -> 3.41 us  [per_device_short(): home = lax.all_to_all(back, 'ctx', split_axis=0, concat_axis=0, tiled=True)]
  transfers between devices with their start and end apart: 5 -> 5, of which waited for: 1 -> 3; matrix products, arithmetic and copies ran while one was open for 4% -> 0% of each run, Pallas kernels for 9% -> 7%
where the time goes in v1:
time: 37.9 us; the launch traced here: 37.5 us
  waiting for transfers between devices  15.9 us (42%)
  starting transfers between devices  13 us (34%)
  Pallas kernels  7.21 us (19%)
  between operations  0.68 us (2%)
  local copies, waits for them, and re-layouts  0.66 us (2%)
    ppermute x3, waiting for transfers between devices, per_device_short(): lax.ppermute(cross, 'dp', [(j, j ^ d) for j in range(seqs)])  10.8 us
    pallas_call x5, Pallas kernels, call(): pl.pallas_call(kernel, out_shape=tuple((pltpu.VMEM(shape, dtype) if near...  7.21 us
    all_to_all x1, starting transfers between devices, per_device_short(): held = lax.all_to_all(sent, 'ctx', split_axis=0, concat_axis=0, tiled=True)  5.18 us
    all_to_all x1, waiting for transfers between devices, per_device_short(): held = lax.all_to_all(sent, 'ctx', split_axis=0, concat_axis=0, tiled=True)  5.15 us
    ppermute x3, starting transfers between devices, per_device_short(): lax.ppermute(cross, 'dp', [(j, j ^ d) for j in range(seqs)])  4.45 us
    all_to_all x1, starting transfers between devices, per_device_short(): home = lax.all_to_all(back, 'ctx', split_axis=0, concat_axis=0, tiled=True)  3.41 us
  transfers between devices with their start and end apart: 5, of which 3 were waited for; matrix products, arithmetic and copies ran while one was open for 0% of the time, Pallas kernels for 7%

profile of v1, /device:TPU:0, one launch (start us, length us, event | category | flops | bytes accessed | tf_op | source)
XLA Modules:
  0.0 37.5 jit_solution(11151728974642991315)
XLA Ops:
  0.6 1.9 %pack.1 = (bf16[8,128,128]{2,1,0:T(8,128)(2,1)}, bf16[1,128,512]{2,1,0:T(8,128)(2,1)S(1)}) custom-call(bf16[1,128,512]{2,1,0:T(8,128)(2,1)} %vals_hbm.1, bf16[1,128,512]{2,1,0:T(8,128)(2,1)} %gate_hbm.1, bf16[1,128,512]{2,1,0:T(8,128)(2,1)} %grad_hbm.1), custom_call_target="tpu_custom_call" | custom-call | bytes 524288 | tf_op jit(solution)/shard_map/pack/pallas_call | solution.py:281
  2.5 5.2 %all-to-all-start = ((bf16[8,128,128]{2,1,0:T(8,128)(2,1)}), bf16[8,128,128]{2,1,0:T(8,128)(2,1)S(1)}, u32[]{:S(2)}, u32[]{:S(2)}) async-start(bf16[8,128,128]{2,1,0:T(8,128)(2,1)} %get-tuple-element.12), calls=%async_computation | async-start | bytes 524288 | tf_op jit(solution)/shard_map/all_to_all | solution.py:315
  7.7 1.8 %filter_spectrum.1 = (f32[128,1024]{1,0:T(8,128)S(1)}, bf16[512,1024]{1,0:T(8,128)(2,1)S(1)}, bf16[1024,512]{1,0:T(8,128)(2,1)S(1)}) custom-call(f32[64,1024]{1,0:T(8,128)} %filt_hbm.1, bf16[512,1024]{1,0:T(8,128)(2,1)} %constant.4.clone.fwd_hbm, bf16[1024,512]{1,0:T(8,128)(2,1)} %constant.5.clone.inv_hbm), custom_call_target="tpu_custom_call" | custom-call | flops 268435456 | bytes 8388608 | tf_op jit(solution)/shard_map/filter_spectrum/pallas_call | solution.py:281
  9.5 5.1 %all-to-all-done.x_ref = bf16[8,128,128]{2,1,0:T(8,128)(2,1)S(1)} async-done(((bf16[8,128,128]{2,1,0:T(8,128)(2,1)}), bf16[8,128,128]{2,1,0:T(8,128)(2,1)S(1)}, u32[]{:S(2)}, u32[]{:S(2)}) %all-to-all-start) | async-done | bytes 262176 | tf_op jit(solution)/shard_map/all_to_all | solution.py:315
  14.6 0.0 copy-start
  14.6 0.7 %copy-done = f32[64]{0:T(128)S(1)} copy-done((f32[64]{0:T(128)S(1)}, f32[64]{0:T(128)}, u32[]{:S(2)}) %copy-start) | copy-done | bytes 280
  15.3 2.0 %products.1 = (bf16[8,128,128]{2,1,0:T(8,128)(2,1)}, bf16[64,1024]{1,0:T(8,128)(2,1)S(1)}) custom-call(bf16[8,128,128]{2,1,0:T(8,128)(2,1)S(1)} %all-to-all-done.x_ref, bf16[512,1024]{1,0:T(8,128)(2,1)S(1)} %get-tuple-element.13.fwd_ref, bf16[1024,512]{1,0:T(8,128)(2,1)S(1)} %get-tuple-element.14.inv_ref, f32[128,1024]{1,0:T(8,128)S(1)} %get-tuple-element.15.filt_ref, ...), custom_call_target="tpu_custom_call" | custom-call | flops 671088640 | bytes 8388608 | tf_op jit(solution)/shard_map/products/pallas_call | solution.py:281
  17.3 3.4 %all-to-all-start.1 = ((bf16[8,128,128]{2,1,0:T(8,128)(2,1)}), bf16[8,128,128]{2,1,0:T(8,128)(2,1)S(1)}, u32[]{:S(2)}, u32[]{:S(2)}) async-start(bf16[8,128,128]{2,1,0:T(8,128)(2,1)} %get-tuple-element.16), calls=%async_computation.1 | async-start | bytes 524288 | tf_op jit(solution)/shard_map/all_to_all | solution.py:340
  20.7 3.7 %collective-permute-start.2 = (bf16[64,1024]{1,0:T(8,128)(2,1)S(1)}, bf16[64,1024]{1,0:T(8,128)(2,1)S(1)}, u32[]{:S(2)}, u32[]{:S(2)}) collective-permute-start(bf16[64,1024]{1,0:T(8,128)(2,1)S(1)} %get-tuple-element.20.refs_0_), channel_id=1, source_target_pairs={{0,24},{8,16},{16,8},{24,0},{1,25},{9,17},{17,9},{25,1},{2,26},{10... | collective-permute-start | bytes 393224 | tf_op jit(solution)/shard_map/ppermute | solution.py:338
  24.4 0.0 collective-permute-start.1
  24.4 0.8 %collective-permute-start = (bf16[64,1024]{1,0:T(8,128)(2,1)S(1)}, bf16[64,1024]{1,0:T(8,128)(2,1)S(1)}, u32[]{:S(2)}, u32[]{:S(2)}) collective-permute-start(bf16[64,1024]{1,0:T(8,128)(2,1)S(1)} %get-tuple-element.20.refs_0_), channel_id=1, source_target_pairs={{0,8},{8,0},{16,24},{24,16},{1,9},{9,1},{17,25},{25,17},{2,10},{10... | collective-permute-start | bytes 393224 | tf_op jit(solution)/shard_map/ppermute | solution.py:338
  25.1 3.8 %collective-permute-done.2.refs_3_ = bf16[64,1024]{1,0:T(8,128)(2,1)S(1)} collective-permute-done((bf16[64,1024]{1,0:T(8,128)(2,1)S(1)}, bf16[64,1024]{1,0:T(8,128)(2,1)S(1)}, u32[]{:S(2)}, u32[]{:S(2)}) %collective-permute-start.2) | collective-permute-done | bytes 131104 | tf_op jit(solution)/shard_map/ppermute | solution.py:338
  29.0 7.0 %collective-permute-done.1.refs_2_ = bf16[64,1024]{1,0:T(8,128)(2,1)S(1)} collective-permute-done((bf16[64,1024]{1,0:T(8,128)(2,1)S(1)}, bf16[64,1024]{1,0:T(8,128)(2,1)S(1)}, u32[]{:S(2)}, u32[]{:S(2)}) %collective-permute-start.1) | collective-permute-done | bytes 131104 | tf_op jit(solution)/shard_map/ppermute | solution.py:338
  35.9 0.0 collective-permute-done.refs_1_
  35.9 0.8 %total.1 = f32[64,1024]{1,0:T(8,128)} custom-call(bf16[64,1024]{1,0:T(8,128)(2,1)S(1)} %get-tuple-element.20.refs_0_, bf16[64,1024]{1,0:T(8,128)(2,1)S(1)} %collective-permute-done.refs_1_, bf16[64,1024]{1,0:T(8,128)(2,1)S(1)} %collective-permute-done.1.refs_2_, bf16[64,1024]{1,0:T(8,128)(2,1)S(1)} %collective-permute-done.2.refs_3_), custom_call_target="tpu_custom_call" | custom-call | bytes 786432 | tf_op jit(solution)/shard_map/total/pallas_call | solution.py:281
  36.7 0.0 all-to-all-done.1.back_ref
  36.7 0.8 %unpack.1 = (bf16[1,128,512]{2,1,0:T(8,128)(2,1)}, bf16[1,128,512]{2,1,0:T(8,128)(2,1)}) custom-call(bf16[8,128,128]{2,1,0:T(8,128)(2,1)S(1)} %all-to-all-done.1.back_ref, bf16[1,128,512]{2,1,0:T(8,128)(2,1)S(1)} %get-tuple-element.17.grad_ref), custom_call_target="tpu_custom_call" | custom-call | bytes 655360 | tf_op jit(solution)/shard_map/unpack/pallas_call | solution.py:281
Async XLA Ops:
  2.5 12.1 %all-to-all-start = ((bf16[8,128,128]{2,1,0:T(8,128)(2,1)}), bf16[8,128,128]{2,1,0:T(8,128)(2,1)S(1)}, u32[]{:S(2)}, u32[]{:S(2)}) async-start(bf16[8,128,128]{2,1,0:T(8,128)(2,1)} %get-tuple-element.12), calls=%async_computation | async-start | bytes 524288 | tf_op jit(solution)/shard_map/all_to_all | solution.py:315
  14.6 0.7 %copy-start = (f32[64]{0:T(128)S(1)}, f32[64]{0:T(128)}, u32[]{:S(2)}) copy-start(f32[64]{0:T(128)} %param.11) | copy-start | bytes 772
  17.3 19.4 %all-to-all-start.1 = ((bf16[8,128,128]{2,1,0:T(8,128)(2,1)}), bf16[8,128,128]{2,1,0:T(8,128)(2,1)S(1)}, u32[]{:S(2)}, u32[]{:S(2)}) async-start(bf16[8,128,128]{2,1,0:T(8,128)(2,1)} %get-tuple-element.16), calls=%async_computation.1 | async-start | bytes 524288 | tf_op jit(solution)/shard_map/all_to_all | solution.py:340
  20.7 8.3 %collective-permute-start.2 = (bf16[64,1024]{1,0:T(8,128)(2,1)S(1)}, bf16[64,1024]{1,0:T(8,128)(2,1)S(1)}, u32[]{:S(2)}, u32[]{:S(2)}) collective-permute-start(bf16[64,1024]{1,0:T(8,128)(2,1)S(1)} %get-tuple-element.20.refs_0_), channel_id=1, source_target_pairs={{0,24},{8,16},{16,8},{24,0},{1,25},{9,17},{17,9},{25,1},{2,26},{10... | collective-permute-start | bytes 393224 | tf_op jit(solution)/shard_map/ppermute | solution.py:338
  24.4 11.6 %collective-permute-start.1 = (bf16[64,1024]{1,0:T(8,128)(2,1)S(1)}, bf16[64,1024]{1,0:T(8,128)(2,1)S(1)}, u32[]{:S(2)}, u32[]{:S(2)}) collective-permute-start(bf16[64,1024]{1,0:T(8,128)(2,1)S(1)} %get-tuple-element.20.refs_0_), channel_id=1, source_target_pairs={{0,16},{8,24},{16,0},{24,8},{1,17},{9,25},{17,1},{25,9},{2,18},{10... | collective-permute-start | bytes 393224 | tf_op jit(solution)/shard_map/ppermute | solution.py:338
  24.4 11.6 %collective-permute-start = (bf16[64,1024]{1,0:T(8,128)(2,1)S(1)}, bf16[64,1024]{1,0:T(8,128)(2,1)S(1)}, u32[]{:S(2)}, u32[]{:S(2)}) collective-permute-start(bf16[64,1024]{1,0:T(8,128)(2,1)S(1)} %get-tuple-element.20.refs_0_), channel_id=1, source_target_pairs={{0,8},{8,0},{16,24},{24,16},{1,9},{9,1},{17,25},{25,17},{2,10},{10... | collective-permute-start | bytes 393224 | tf_op jit(solution)/shard_map/ppermute | solution.py:338

commit v2 on v1

--- a/solution.py
+++ b/solution.py
@@ -133,7 +133,7 @@
 
 
 def hbm_specs(count):
-    return [pl.BlockSpec(memory_space=pltpu.HBM)] * count
+    return [pl.BlockSpec(memory_space=pl.ANY)] * count
 
 
 def in_vmem(array):
@@ -151,23 +151,46 @@
     return copies
 
 
-def pack_kernel(parts, vals_hbm, gate_hbm, grad_hbm, out_ref, grad_ref, vals_ref, gate_ref, sems):
-    chans = vals_ref.shape[2] // parts
+def places(parts):
+    me = lax.axis_index("ctx")
+    return [
+        (f, d, 2 * ((me // 2) ^ d) + ((me % 2) ^ f)) for f in range(2) for d in range(parts // 2)
+    ]
+
+
+def pack_kernel(
+    vals_hbm, gate_hbm, grad_hbm, own_ref, sib_ref, grad_ref, vals_ref, gate_ref, turn_ref, sems
+):
+    pairs, rows, _ = own_ref.shape
+    chans = rows // 2
     copies = start_copies(
         [(vals_hbm, vals_ref), (gate_hbm, gate_ref), (grad_hbm, grad_ref)], sems
     )
     copies[0].wait()
-    vals = vals_ref[0].astype(F32).T.astype(BF16)
-    for d in range(parts):
-        out_ref[d, :chans, :] = vals[d * chans : (d + 1) * chans, :]
+    turn_ref[0] = vals_ref[0].astype(F32).T.astype(BF16)
     copies[1].wait()
     copies[2].wait()
-    dz = (grad_ref[0].astype(F32) * gate_ref[0].astype(F32)).T.astype(BF16)
-    for d in range(parts):
-        out_ref[d, chans:, :] = dz[d * chans : (d + 1) * chans, :]
-
-
-def filter_kernel(filt_hbm, fwd_hbm, inv_hbm, spec_ref, fwd_ref, inv_ref, filt_ref, sems):
+    turn_ref[1] = (grad_ref[0].astype(F32) * gate_ref[0].astype(F32)).T.astype(BF16)
+    for f, d, at in places(2 * pairs):
+        out_ref = sib_ref if f else own_ref
+        at = pl.multiple_of(at * chans, chans)
+        out_ref[d, :chans, :] = turn_ref[0, pl.ds(at, chans), :]
+        out_ref[d, chans:, :] = turn_ref[1, pl.ds(at, chans), :]
+
+
+def merge_kernel(own_ref, got_ref, *out_refs):
+    for d, out_ref in enumerate(out_refs, 1):
+        out_ref[0] = own_ref[d]
+        out_ref[1] = got_ref[d]
+
+
+def arrived(own_ref, got_ref, *pair_refs):
+    return lambda f, d: pair_refs[d - 1][f] if d else (got_ref if f else own_ref)[0]
+
+
+def filter_kernel(
+    filt_hbm, fwd_hbm, inv_hbm, skip_ref, spec_ref, fwd_ref, inv_ref, gain_ref, filt_ref, sems
+):
     copies = start_copies([(filt_hbm, filt_ref), (fwd_hbm, fwd_ref), (inv_hbm, inv_ref)], sems)
     half = fwd_ref.shape[0]
     copies[0].wait()
@@ -179,6 +202,11 @@
         jnp.concatenate([high, low], axis=0), fwd_ref[...], preferred_element_type=F32
     )
     spec_ref[...] = both[: filt.shape[0]] + both[filt.shape[0] :]
+    chans = filt_ref.shape[0]
+    row = lax.broadcasted_iota(jnp.int32, (chans, chans), 0)
+    col = lax.broadcasted_iota(jnp.int32, (chans, chans), 1)
+    gain = jnp.sum(jnp.where(row == col, skip_ref[...], 0.0), axis=1, keepdims=True)
+    gain_ref[...] = jnp.broadcast_to(jnp.concatenate([gain, gain], axis=0), gain_ref.shape)
     copies[2].wait()
 
 
@@ -198,15 +226,18 @@
     return (a[1], -a[0]) if odd else (-a[1], a[0])
 
 
-def main_kernel(
-    x_ref, fwd_ref, inv_ref, filt_ref, skip_ref, back_ref, cross_ref, spec_ref, prod_ref
-):
-    parts, rows, pos = x_ref.shape
+def main_kernel(pairs, *refs):
+    fwd_ref, inv_ref, filt_ref, gain_ref = refs[pairs + 1 : pairs + 5]
+    own_ref, sib_ref, cross_ref, spec_ref, prod_ref, block_ref = refs[pairs + 5 :]
+    parts, rows, pos = block_ref.shape
     chans = rows // 2
     half = parts // 2 * pos
+    block = arrived(*refs[: pairs + 1])
+    for f, d, at in places(parts):
+        block_ref[at] = block(f, d)
     x = [
-        jnp.concatenate([x_ref[s] for s in range(parts // 2)], axis=1),
-        jnp.concatenate([x_ref[s] for s in range(parts // 2, parts)], axis=1),
+        jnp.concatenate([block_ref[s] for s in range(parts // 2)], axis=1),
+        jnp.concatenate([block_ref[s] for s in range(parts // 2, parts)], axis=1),
     ]
     spec_ref[...] = jnp.dot(
         jnp.concatenate(x, axis=0), fwd_ref[...], preferred_element_type=F32
@@ -232,10 +263,7 @@
                 prod_ref[at, c : c + 128] = re.astype(BF16)
                 prod_ref[at, half + c : half + c + 128] = im.astype(BF16)
     res = jnp.dot(prod_ref[...], inv_ref[...], preferred_element_type=F32)
-    row = lax.broadcasted_iota(jnp.int32, (chans, chans), 0)
-    col = lax.broadcasted_iota(jnp.int32, (chans, chans), 1)
-    gain = jnp.sum(jnp.where(row == col, skip_ref[...], 0.0), axis=1, keepdims=True)
-    gains = jnp.concatenate([gain, gain], axis=0)
+    gains = jnp.concatenate([gain_ref[...]] * (half // 128), axis=1)
     scale = (2 * half) ** -0.5 / half
     for i in range(2):
         top = i * 3 * chans
@@ -244,33 +272,40 @@
         ).astype(BF16)
         both = (res[top : top + rows] * scale + gains * x[i].astype(F32)).astype(BF16)
         for s in range(parts // 2):
-            back_ref[i * (parts // 2) + s] = both[:, s * pos : (s + 1) * pos]
-
-
-def unpack_kernel(back_ref, grad_ref, val_hbm, gate_hbm, val_ref, gate_ref, sems):
-    parts, rows, _ = back_ref.shape
-    chans = rows // 2
-    vals = jnp.concatenate([back_ref[s, chans:, :] for s in range(parts)], axis=0)
-    val_ref[0] = vals.astype(F32).T.astype(BF16)
+            block_ref[i * (parts // 2) + s] = both[:, s * pos : (s + 1) * pos]
+    for f, d, at in places(parts):
+        (sib_ref if f else own_ref)[d] = block_ref[at]
+
+
+def unpack_kernel(pairs, *refs):
+    grad_ref, val_hbm, gate_hbm, val_ref, gate_ref, turn_ref, sems = refs[pairs + 1 :]
+    chans = turn_ref.shape[1] // (2 * pairs)
+    block = arrived(*refs[: pairs + 1])
+    for f, d, at in places(2 * pairs):
+        at = pl.multiple_of(at * chans, chans)
+        both = block(f, d)
+        turn_ref[0, pl.ds(at, chans), :] = both[:chans]
+        turn_ref[1, pl.ds(at, chans), :] = both[chans:]
+    val_ref[0] = turn_ref[1].astype(F32).T.astype(BF16)
     first = start_copies([(val_ref, val_hbm)], sems)
-    conv = jnp.concatenate([back_ref[s, :chans, :] for s in range(parts)], axis=0)
-    gate_ref[0] = (grad_ref[0].astype(F32) * conv.astype(F32).T).astype(BF16)
+    gate_ref[0] = (grad_ref[0].astype(F32) * turn_ref[0].astype(F32).T).astype(BF16)
     second = pltpu.make_async_copy(gate_ref, gate_hbm, sems.at[1])
     second.start()
     first[0].wait()
     second.wait()
 
 
-def total_kernel(scale, *refs):
-    part_refs, out_hbm, out_ref, sems = refs[:-3], refs[-3], refs[-2], refs[-1]
+def pair_kernel(left_ref, right_ref, *rest):
+    out_ref = rest[-1]
+    out_ref[...] = (left_ref[...].astype(F32) + right_ref[...].astype(F32)).astype(BF16)
+
+
+def total_kernel(scale, left_ref, right_ref, out_hbm, out_ref, sems):
     half = out_ref.shape[0] // 2
     copies = []
     for i in range(2):
         at = pl.ds(i * half, half)
-        terms = [ref[at, :].astype(F32) for ref in part_refs]
-        while len(terms) > 1:
-            terms = [a + b for a, b in zip(terms[::2], terms[1::2])]
-        out_ref[at, :] = terms[0] * scale
+        out_ref[at, :] = (left_ref[at, :].astype(F32) + right_ref[at, :].astype(F32)) * scale
         copies.append(pltpu.make_async_copy(out_ref.at[at, :], out_hbm.at[at, :], sems.at[i]))
         copies[-1].start()
     for copy in copies:
@@ -294,6 +329,21 @@
     )(*ins)
 
 
+def exchange(own, sib, name):
+    pairs, rows, pos = own.shape
+    got = lax.ppermute(sib, "ctx", [(j, j ^ 1) for j in range(2 * pairs)])
+    sent = call(
+        merge_kernel,
+        "merge_" + name,
+        [((2, rows, pos), BF16, True)] * (pairs - 1),
+        (in_vmem(own), in_vmem(got)),
+        vmem_specs(2),
+        moved=8 * (pairs - 1) * rows * pos,
+    )
+    pair_of = [(d, [(j, j ^ (2 * d)) for j in range(2 * pairs)]) for d in range(1, pairs)]
+    return [own, got] + [lax.ppermute(sent[d - 1], "ctx", perm) for d, perm in pair_of]
+
+
 def per_device_short(values, gates, grad_out, filters, skip):
     chans, length = filters.shape
     parts = lax.axis_size("ctx")
@@ -302,49 +352,66 @@
     rows = 2 * chans
     fwd, inv = (jnp.asarray(table) for table in dense_tables(length // 2))
     token = ((1, pos, width), BF16)
-    sent, grad_near = call(
-        functools.partial(pack_kernel, parts),
+    pairs = parts // 2
+    pair_blocks = ((pairs, rows, pos), BF16)
+    turned = ((2, width, pos), BF16)
+    own, sib, grad_near = call(
+        pack_kernel,
         "pack",
-        [((parts, rows, pos), BF16, True), (*token, True)],
+        [(*pair_blocks, True), (*pair_blocks, True), (*token, True)],
         tuple(in_hbm(x) for x in (values, gates, grad_out)),
         hbm_specs(3),
-        scratch=[token, token],
+        scratch=[token, token, turned],
         sems=3,
         moved=8 * pos * width,
     )
-    held = lax.all_to_all(sent, "ctx", split_axis=0, concat_axis=0, tiled=True)
-    spec, fwd_near, inv_near = call(
+    held = exchange(own, sib, "out")
+    spec, fwd_near, inv_near, gains = call(
         filter_kernel,
         "filter_spectrum",
-        [((rows, length), F32, True), (fwd.shape, BF16, True), (inv.shape, BF16, True)],
-        tuple(in_hbm(x) for x in (filters, fwd, inv)),
-        hbm_specs(3),
+        [((rows, length), F32, True), (fwd.shape, BF16, True), (inv.shape, BF16, True), ((rows, 128), F32, True)],
+        tuple(in_hbm(x) for x in (filters, fwd, inv)) + (skip.reshape(1, chans),),
+        hbm_specs(3) + vmem_specs(1),
         scratch=[((chans, length), F32)],
         sems=3,
         flops=4 * chans * length * length,
         moved=8 * length * length,
     )
-    back, cross = call(
-        main_kernel,
+    own, sib, cross = call(
+        functools.partial(main_kernel, pairs),
         "products",
-        [((parts, rows, pos), BF16, True), ((chans, length), BF16, True)],
-        (in_vmem(held), in_vmem(fwd_near), in_vmem(inv_near), in_vmem(spec), skip.reshape(1, chans)),
-        vmem_specs(5),
-        scratch=[((2 * rows, length), F32), ((3 * rows, length), BF16)],
+        [(*pair_blocks, True), (*pair_blocks, True), ((chans, length), BF16, True)],
+        tuple(in_vmem(x) for x in held + [fwd_near, inv_near, spec, gains]),
+        vmem_specs(pairs + 5),
+        scratch=[
+            ((2 * rows, length), F32),
+            ((3 * rows, length), BF16),
+            ((parts, rows, pos), BF16),
+        ],
         flops=10 * chans * length * length,
         moved=8 * length * length,
     )
-    others = [
-        lax.ppermute(cross, "dp", [(j, j ^ d) for j in range(seqs)]) for d in range(1, seqs)
-    ]
-    home = lax.all_to_all(back, "ctx", split_axis=0, concat_axis=0, tiled=True)
+    home = exchange(own, sib, "home")
+    step = seqs // 2
+    while step:
+        other = lax.ppermute(cross, "dp", [(j, j ^ step) for j in range(seqs)])
+        step //= 2
+        if step:
+            (cross,) = call(
+                pair_kernel,
+                "pair_sum",
+                [((chans, length), BF16, True)],
+                (in_vmem(cross), in_vmem(other), *home[2:]),
+                vmem_specs(2) + hbm_specs(len(home) - 2),
+                moved=6 * chans * length,
+            )
     grad_values, grad_gates = call(
-        unpack_kernel,
+        functools.partial(unpack_kernel, pairs),
         "unpack",
         [(*token, False), (*token, False)],
-        (in_vmem(home), in_vmem(grad_near)),
-        vmem_specs(2),
-        scratch=[token, token],
+        tuple(in_vmem(x) for x in home + [grad_near]),
+        vmem_specs(pairs + 2),
+        scratch=[token, token, turned],
         sems=2,
         moved=10 * pos * width,
     )
@@ -352,8 +419,8 @@
         functools.partial(total_kernel, (seqs * length) ** (-0.5)),
         "total",
         [((chans, length), F32, False)],
-        tuple(in_vmem(part) for part in [cross] + others),
-        vmem_specs(seqs),
+        (in_vmem(cross), in_vmem(other)),
+        vmem_specs(2),
         scratch=[((chans, length), F32)],
         sems=2,
         moved=12 * chans * length,
@@ -366,7 +433,8 @@
     pos = values.shape[1]
     seqs = lax.axis_size("dp")
     dense = length <= DENSE_LIMIT and length % 512 == 0 and chans % 16 == 0 and pos % 128 == 0
-    if dense and seqs & (seqs - 1) == 0:
+    powers = all(n > 1 and n & (n - 1) == 0 for n in (seqs, lax.axis_size("ctx")))
+    if dense and powers:
         return per_device_short(values, gates, grad_out, filters, skip)
     return per_device_long(values, gates, grad_out, filters, skip)
 

time: 37.9 us -> 30 us (0.79)
  waiting for transfers between devices: 15.9 us -> 10.4 us
  Pallas kernels: 7.21 us -> 5.92 us
  starting transfers between devices: 13 us -> 12.2 us
    all_to_all x2 -> x0, starting transfers between devices: 8.59 us -> none  [the longest x1 5.18 us: per_device_short(): held = lax.all_to_all(sent, 'ctx', split_axis=0, concat_axis=0, tiled=True)]
    ppermute x3 -> x10, starting transfers between devices: 4.45 us -> 12.2 us  [the longest x6 8 us: exchange(): lax.ppermute(sent[d - 1], 'ctx', perm)]
    all_to_all x2 -> x0, waiting for transfers between devices: 5.15 us -> none  [the longest x1 5.15 us: per_device_short(): held = lax.all_to_all(sent, 'ctx', split_axis=0, concat_axis=0, tiled=True)]
    pallas_call x5 -> x8, Pallas kernels: 7.21 us -> 5.92 us  [call(): pl.pallas_call(kernel, out_shape=tuple((pltpu.VMEM(shape, dtype) if near...]
    ppermute x3 -> x10, waiting for transfers between devices: 10.8 us -> 10.4 us  [the longest x2 6.71 us: per_device_short(): other = lax.ppermute(cross, 'dp', [(j, j ^ step) for j in range(seqs)])]
  transfers between devices with their start and end apart: 5 -> 10, of which waited for: 3 -> 5; matrix products, arithmetic and copies ran while one was open for 0% -> 0% of each run, Pallas kernels for 7% -> 9%
where the time goes in v2:
time: 30 us; the launch traced here: 29.9 us
  starting transfers between devices  12.2 us (41%)
  waiting for transfers between devices  10.4 us (35%)
  Pallas kernels  5.92 us (20%)
  between operations  0.7 us (2%)
  local copies, waits for them, and re-layouts  0.63 us (2%)
    ppermute x6, starting transfers between devices, exchange(): lax.ppermute(sent[d - 1], 'ctx', perm)  8 us
    ppermute x2, waiting for transfers between devices, per_device_short(): other = lax.ppermute(cross, 'dp', [(j, j ^ step) for j in range(seqs)])  6.71 us
    pallas_call x8, Pallas kernels, call(): pl.pallas_call(kernel, out_shape=tuple((pltpu.VMEM(shape, dtype) if near...  5.92 us
    ppermute x2, starting transfers between devices, per_device_short(): other = lax.ppermute(cross, 'dp', [(j, j ^ step) for j in range(seqs)])  3.61 us
    ppermute x6, waiting for transfers between devices, exchange(): lax.ppermute(sent[d - 1], 'ctx', perm)  2.72 us
    ppermute x2, waiting for transfers between devices, exchange(): got = lax.ppermute(sib, 'ctx', [(j, j ^ 1) for j in range(2 * pairs)])  0.99 us
    unnamed x2, local copies, waits for them, and re-layouts  0.63 us
  transfers between devices with their start and end apart: 10, of which 5 were waited for; matrix products, arithmetic and copies ran while one was open for 0% of the time, Pallas kernels for 9%

profile of v2, /device:TPU:0, one launch (start us, length us, event | category | flops | bytes accessed | tf_op | source)
XLA Modules:
  0.0 29.9 jit_solution(2661669404194111331)
XLA Ops:
  0.6 1.2 %pack.1 = (bf16[4,128,128]{2,1,0:T(8,128)(2,1)S(1)}, bf16[4,128,128]{2,1,0:T(8,128)(2,1)S(1)}, bf16[1,128,512]{2,1,0:T(8,128)(2,1)S(1)}) custom-call(bf16[1,128,512]{2,1,0:T(8,128)(2,1)} %vals_hbm.1, bf16[1,128,512]{2,1,0:T(8,128)(2,1)} %gate_hbm.1, bf16[1,128,512]{2,1,0:T(8,128)(2,1)} %grad_hbm.1), custom_call_target="tpu_custom_call" | custom-call | bytes 524288 | tf_op jit(solution)/shard_map/pack/pallas_call | solution.py:316
  1.8 0.5 %collective-permute-start = (bf16[4,128,128]{2,1,0:T(8,128)(2,1)S(1)}, bf16[4,128,128]{2,1,0:T(8,128)(2,1)S(1)}, u32[]{:S(2)}, u32[]{:S(2)}) collective-permute-start(bf16[4,128,128]{2,1,0:T(8,128)(2,1)S(1)} %get-tuple-element.22), channel_id=1, source_target_pairs={{0,1},{1,0},{2,3},{3,2},{4,5},{5,4},{6,7},{7,6},{8,9},{9,8},{10,11... | collective-permute-start | bytes 393224 | tf_op jit(solution)/shard_map/ppermute | solution.py:334
  2.3 1.0 %collective-permute-done.got_ref.refs_1_ = bf16[4,128,128]{2,1,0:T(8,128)(2,1)S(1)} collective-permute-done((bf16[4,128,128]{2,1,0:T(8,128)(2,1)S(1)}, bf16[4,128,128]{2,1,0:T(8,128)(2,1)S(1)}, u32[]{:S(2)}, u32[]{:S(2)}) %collective-permute-start) | collective-permute-done | bytes 131104 | tf_op jit(solution)/shard_map/ppermute | solution.py:334
  3.3 2.9 %collective-permute-start.1 = (bf16[2,128,128]{2,1,0:T(8,128)(2,1)S(1)}, bf16[2,128,128]{2,1,0:T(8,128)(2,1)S(1)}, u32[]{:S(2)}, u32[]{:S(2)}) collective-permute-start(bf16[2,128,128]{2,1,0:T(8,128)(2,1)S(1)} %get-tuple-element.23), channel_id=1, source_target_pairs={{0,2},{1,3},{2,0},{3,1},{4,6},{5,7},{6,4},{7,5},{8,10},{9,11},{10,... | collective-permute-start | bytes 196616 | tf_op jit(solution)/shard_map/ppermute | solution.py:344
  6.3 1.5 %collective-permute-start.2 = (bf16[2,128,128]{2,1,0:T(8,128)(2,1)S(1)}, bf16[2,128,128]{2,1,0:T(8,128)(2,1)S(1)}, u32[]{:S(2)}, u32[]{:S(2)}) collective-permute-start(bf16[2,128,128]{2,1,0:T(8,128)(2,1)S(1)} %get-tuple-element.24), channel_id=1, source_target_pairs={{0,4},{1,5},{2,6},{3,7},{4,0},{5,1},{6,2},{7,3},{8,12},{9,13},{10,... | collective-permute-start | bytes 196616 | tf_op jit(solution)/shard_map/ppermute | solution.py:344
  7.8 0.0 collective-permute-start.3
  7.8 0.6 %copy-done = f32[64]{0:T(128)S(1)} copy-done((f32[64]{0:T(128)S(1)}, f32[64]{0:T(128)}, u32[]{:S(2)}) %copy-start) | copy-done | bytes 280
  8.4 1.8 %filter_spectrum.1 = (f32[128,1024]{1,0:T(8,128)S(1)}, bf16[512,1024]{1,0:T(8,128)(2,1)S(1)}, bf16[1024,512]{1,0:T(8,128)(2,1)S(1)}, f32[128,128]{1,0:T(8,128)S(1)}) custom-call(f32[64,1024]{1,0:T(8,128)} %filt_hbm.1, bf16[512,1024]{1,0:T(8,128)(2,1)} %constant.4.clone.fwd_hbm, bf16[1024,512]{1,0:T(8,128)(2,1)} %constant.5.clone.inv_hbm, f32[1,64]{1,0:T(1,128)S(1)} %bitcast.1), custom_call_target="tpu_custom_call" | custom-call | flops 268435456 | bytes 8388608 | tf_op jit(solution)/shard_map/filter_spectrum/pallas_call | solution.py:316
  10.2 0.0 collective-permute-done.1.refs_2_
  10.2 0.3 collective-permute-done.2.refs_3_
  10.5 2.4 %collective-permute-done.3.refs_4_ = bf16[2,128,128]{2,1,0:T(8,128)(2,1)S(1)} collective-permute-done((bf16[2,128,128]{2,1,0:T(8,128)(2,1)S(1)}, bf16[2,128,128]{2,1,0:T(8,128)(2,1)S(1)}, u32[]{:S(2)}, u32[]{:S(2)}) %collective-permute-start.3) | collective-permute-done | bytes 65568 | tf_op jit(solution)/shard_map/ppermute | solution.py:344
  12.9 1.3 %products.1 = (bf16[4,128,128]{2,1,0:T(8,128)(2,1)S(1)}, bf16[4,128,128]{2,1,0:T(8,128)(2,1)S(1)}, bf16[64,1024]{1,0:T(8,128)(2,1)S(1)}) custom-call(bf16[4,128,128]{2,1,0:T(8,128)(2,1)S(1)} %get-tuple-element.21.own_ref.refs_0_, bf16[4,128,128]{2,1,0:T(8,128)(2,1)S(1)} %collective-permute-done.got_ref.refs_1_, ...), custom_call_target="tpu_custom_call" | custom-call | flops 671088640 | bytes 8388608 | tf_op jit(solution)/shard_map/products/pallas_call | solution.py:316
  14.3 0.1 collective-permute-start.4
  14.3 2.7 %collective-permute-start.8 = (bf16[64,1024]{1,0:T(8,128)(2,1)S(1)}, bf16[64,1024]{1,0:T(8,128)(2,1)S(1)}, u32[]{:S(2)}, u32[]{:S(2)}) collective-permute-start(bf16[64,1024]{1,0:T(8,128)(2,1)S(1)} %get-tuple-element.38.left_ref), channel_id=1, source_target_pairs={{0,16},{8,24},{16,0},{24,8},{1,17},{9,25},{17,1},{25,9},{2,18},{10... | collective-permute-start | bytes 393224 | tf_op jit(solution)/shard_map/ppermute | solution.py:397
  17.0 0.0 collective-permute-done.4.got_ref.refs_1_
  17.0 0.6 %collective-permute-start.5 = (bf16[2,128,128]{2,1,0:T(8,128)(2,1)S(1)}, bf16[2,128,128]{2,1,0:T(8,128)(2,1)S(1)}, u32[]{:S(2)}, u32[]{:S(2)}) collective-permute-start(bf16[2,128,128]{2,1,0:T(8,128)(2,1)S(1)} %get-tuple-element.32), channel_id=1, source_target_pairs={{0,2},{1,3},{2,0},{3,1},{4,6},{5,7},{6,4},{7,5},{8,10},{9,11},{10,... | collective-permute-start | bytes 196616 | tf_op jit(solution)/shard_map/ppermute | solution.py:344
  17.6 0.5 %collective-permute-start.6 = (bf16[2,128,128]{2,1,0:T(8,128)(2,1)S(1)}, bf16[2,128,128]{2,1,0:T(8,128)(2,1)S(1)}, u32[]{:S(2)}, u32[]{:S(2)}) collective-permute-start(bf16[2,128,128]{2,1,0:T(8,128)(2,1)S(1)} %get-tuple-element.33), channel_id=1, source_target_pairs={{0,4},{1,5},{2,6},{3,7},{4,0},{5,1},{6,2},{7,3},{8,12},{9,13},{10,... | collective-permute-start | bytes 196616 | tf_op jit(solution)/shard_map/ppermute | solution.py:344
  18.1 2.5 %collective-permute-start.7 = (bf16[2,128,128]{2,1,0:T(8,128)(2,1)S(1)}, bf16[2,128,128]{2,1,0:T(8,128)(2,1)S(1)}, u32[]{:S(2)}, u32[]{:S(2)}) collective-permute-start(bf16[2,128,128]{2,1,0:T(8,128)(2,1)S(1)} %get-tuple-element.34), channel_id=1, source_target_pairs={{0,6},{1,7},{2,4},{3,5},{4,2},{5,3},{6,0},{7,1},{8,14},{9,15},{10,... | collective-permute-start | bytes 196616 | tf_op jit(solution)/shard_map/ppermute | solution.py:344
  20.6 3.4 %collective-permute-done.8.right_ref = bf16[64,1024]{1,0:T(8,128)(2,1)S(1)} collective-permute-done((bf16[64,1024]{1,0:T(8,128)(2,1)S(1)}, bf16[64,1024]{1,0:T(8,128)(2,1)S(1)}, u32[]{:S(2)}, u32[]{:S(2)}) %collective-permute-start.8) | collective-permute-done | bytes 131104 | tf_op jit(solution)/shard_map/ppermute | solution.py:397
  24.0 0.0 collective-permute-done.5.refs_2_.rest_0_
  24.0 0.9 %collective-permute-start.9 = (bf16[64,1024]{1,0:T(8,128)(2,1)S(1)}, bf16[64,1024]{1,0:T(8,128)(2,1)S(1)}, u32[]{:S(2)}, u32[]{:S(2)}) collective-permute-start(bf16[64,1024]{1,0:T(8,128)(2,1)S(1)} %pair_sum.1.left_ref), channel_id=1, source_target_pairs={{0,8},{8,0},{16,24},{24,16},{1,9},{9,1},{17,25},{25,17},{2,10},{10... | collective-permute-start | bytes 393224 | tf_op jit(solution)/shard_map/ppermute | solution.py:397
  25.0 0.9 %unpack.1 = (bf16[1,128,512]{2,1,0:T(8,128)(2,1)}, bf16[1,128,512]{2,1,0:T(8,128)(2,1)}) custom-call(bf16[4,128,128]{2,1,0:T(8,128)(2,1)S(1)} %get-tuple-element.30.own_ref.refs_0_, bf16[4,128,128]{2,1,0:T(8,128)(2,1)S(1)} %collective-permute-done.4.got_ref.refs_1_, bf16[2,128,128]{2,1,0:T(8,128)(2,1)S(1)} %collective-permute-done.5.refs_2_.rest_0_, ...), custom_call_target="tpu_custom_call" | custom-call | bytes 655360 | tf_op jit(solution)/shard_map/unpack/pallas_call | solution.py:316
  25.8 3.3 %collective-permute-done.9.right_ref = bf16[64,1024]{1,0:T(8,128)(2,1)S(1)} collective-permute-done((bf16[64,1024]{1,0:T(8,128)(2,1)S(1)}, bf16[64,1024]{1,0:T(8,128)(2,1)S(1)}, u32[]{:S(2)}, u32[]{:S(2)}) %collective-permute-start.9) | collective-permute-done | bytes 131104 | tf_op jit(solution)/shard_map/ppermute | solution.py:397
  29.1 0.7 %total.1 = f32[64,1024]{1,0:T(8,128)} custom-call(bf16[64,1024]{1,0:T(8,128)(2,1)S(1)} %pair_sum.1.left_ref, bf16[64,1024]{1,0:T(8,128)(2,1)S(1)} %collective-permute-done.9.right_ref), custom_call_target="tpu_custom_call" | custom-call | bytes 786432 | tf_op jit(solution)/shard_map/total/pallas_call | solution.py:316
  (6 shorter events, 0.1 us)
Async XLA Ops:
  1.8 1.5 %collective-permute-start = (bf16[4,128,128]{2,1,0:T(8,128)(2,1)S(1)}, bf16[4,128,128]{2,1,0:T(8,128)(2,1)S(1)}, u32[]{:S(2)}, u32[]{:S(2)}) collective-permute-start(bf16[4,128,128]{2,1,0:T(8,128)(2,1)S(1)} %get-tuple-element.22), channel_id=1, source_target_pairs={{0,1},{1,0},{2,3},{3,2},{4,5},{5,4},{6,7},{7,6},{8,9},{9,8},{10,11... | collective-permute-start | bytes 393224 | tf_op jit(solution)/shard_map/ppermute | solution.py:334
  3.3 6.9 %collective-permute-start.1 = (bf16[2,128,128]{2,1,0:T(8,128)(2,1)S(1)}, bf16[2,128,128]{2,1,0:T(8,128)(2,1)S(1)}, u32[]{:S(2)}, u32[]{:S(2)}) collective-permute-start(bf16[2,128,128]{2,1,0:T(8,128)(2,1)S(1)} %get-tuple-element.23), channel_id=1, source_target_pairs={{0,2},{1,3},{2,0},{3,1},{4,6},{5,7},{6,4},{7,5},{8,10},{9,11},{10,... | collective-permute-start | bytes 196616 | tf_op jit(solution)/shard_map/ppermute | solution.py:344
  6.3 4.3 %collective-permute-start.2 = (bf16[2,128,128]{2,1,0:T(8,128)(2,1)S(1)}, bf16[2,128,128]{2,1,0:T(8,128)(2,1)S(1)}, u32[]{:S(2)}, u32[]{:S(2)}) collective-permute-start(bf16[2,128,128]{2,1,0:T(8,128)(2,1)S(1)} %get-tuple-element.24), channel_id=1, source_target_pairs={{0,4},{1,5},{2,6},{3,7},{4,0},{5,1},{6,2},{7,3},{8,12},{9,13},{10,... | collective-permute-start | bytes 196616 | tf_op jit(solution)/shard_map/ppermute | solution.py:344
  7.8 0.7 %copy-start = (f32[64]{0:T(128)S(1)}, f32[64]{0:T(128)}, u32[]{:S(2)}) copy-start(f32[64]{0:T(128)} %param.11) | copy-start | bytes 772
  7.8 5.2 %collective-permute-start.3 = (bf16[2,128,128]{2,1,0:T(8,128)(2,1)S(1)}, bf16[2,128,128]{2,1,0:T(8,128)(2,1)S(1)}, u32[]{:S(2)}, u32[]{:S(2)}) collective-permute-start(bf16[2,128,128]{2,1,0:T(8,128)(2,1)S(1)} %get-tuple-element.25), channel_id=1, source_target_pairs={{0,6},{1,7},{2,4},{3,5},{4,2},{5,3},{6,0},{7,1},{8,14},{9,15},{10,... | collective-permute-start | bytes 196616 | tf_op jit(solution)/shard_map/ppermute | solution.py:344
  14.3 2.7 %collective-permute-start.4 = (bf16[4,128,128]{2,1,0:T(8,128)(2,1)S(1)}, bf16[4,128,128]{2,1,0:T(8,128)(2,1)S(1)}, u32[]{:S(2)}, u32[]{:S(2)}) collective-permute-start(bf16[4,128,128]{2,1,0:T(8,128)(2,1)S(1)} %get-tuple-element.31), channel_id=1, source_target_pairs={{0,1},{1,0},{2,3},{3,2},{4,5},{5,4},{6,7},{7,6},{8,9},{9,8},{10,11... | collective-permute-start | bytes 393224 | tf_op jit(solution)/shard_map/ppermute | solution.py:334
  14.3 9.6 %collective-permute-start.8 = (bf16[64,1024]{1,0:T(8,128)(2,1)S(1)}, bf16[64,1024]{1,0:T(8,128)(2,1)S(1)}, u32[]{:S(2)}, u32[]{:S(2)}) collective-permute-start(bf16[64,1024]{1,0:T(8,128)(2,1)S(1)} %get-tuple-element.38.left_ref), channel_id=1, source_target_pairs={{0,16},{8,24},{16,0},{24,8},{1,17},{9,25},{17,1},{25,9},{2,18},{10... | collective-permute-start | bytes 393224 | tf_op jit(solution)/shard_map/ppermute | solution.py:397
  17.0 6.9 %collective-permute-start.5 = (bf16[2,128,128]{2,1,0:T(8,128)(2,1)S(1)}, bf16[2,128,128]{2,1,0:T(8,128)(2,1)S(1)}, u32[]{:S(2)}, u32[]{:S(2)}) collective-permute-start(bf16[2,128,128]{2,1,0:T(8,128)(2,1)S(1)} %get-tuple-element.32), channel_id=1, source_target_pairs={{0,2},{1,3},{2,0},{3,1},{4,6},{5,7},{6,4},{7,5},{8,10},{9,11},{10,... | collective-permute-start | bytes 196616 | tf_op jit(solution)/shard_map/ppermute | solution.py:344
  17.6 6.3 %collective-permute-start.6 = (bf16[2,128,128]{2,1,0:T(8,128)(2,1)S(1)}, bf16[2,128,128]{2,1,0:T(8,128)(2,1)S(1)}, u32[]{:S(2)}, u32[]{:S(2)}) collective-permute-start(bf16[2,128,128]{2,1,0:T(8,128)(2,1)S(1)} %get-tuple-element.33), channel_id=1, source_target_pairs={{0,4},{1,5},{2,6},{3,7},{4,0},{5,1},{6,2},{7,3},{8,12},{9,13},{10,... | collective-permute-start | bytes 196616 | tf_op jit(solution)/shard_map/ppermute | solution.py:344
  18.1 5.8 %collective-permute-start.7 = (bf16[2,128,128]{2,1,0:T(8,128)(2,1)S(1)}, bf16[2,128,128]{2,1,0:T(8,128)(2,1)S(1)}, u32[]{:S(2)}, u32[]{:S(2)}) collective-permute-start(bf16[2,128,128]{2,1,0:T(8,128)(2,1)S(1)} %get-tuple-element.34), channel_id=1, source_target_pairs={{0,6},{1,7},{2,4},{3,5},{4,2},{5,3},{6,0},{7,1},{8,14},{9,15},{10,... | collective-permute-start | bytes 196616 | tf_op jit(solution)/shard_map/ppermute | solution.py:344
  24.0 5.1 %collective-permute-start.9 = (bf16[64,1024]{1,0:T(8,128)(2,1)S(1)}, bf16[64,1024]{1,0:T(8,128)(2,1)S(1)}, u32[]{:S(2)}, u32[]{:S(2)}) collective-permute-start(bf16[64,1024]{1,0:T(8,128)(2,1)S(1)} %pair_sum.1.left_ref), channel_id=1, source_target_pairs={{0,8},{8,0},{16,24},{24,16},{1,9},{9,1},{17,25},{25,17},{2,10},{10... | collective-permute-start | bytes 393224 | tf_op jit(solution)/shard_map/ppermute | solution.py:397

commit v3 on v2

--- a/solution.py
+++ b/solution.py
@@ -185,7 +185,7 @@
 
 
 def arrived(own_ref, got_ref, *pair_refs):
-    return lambda f, d: pair_refs[d - 1][f] if d else (got_ref if f else own_ref)[0]
+    return lambda f, d: pair_refs[-d][f] if d else (got_ref if f else own_ref)[0]
 
 
 def filter_kernel(
@@ -228,7 +228,7 @@
 
 def main_kernel(pairs, *refs):
     fwd_ref, inv_ref, filt_ref, gain_ref = refs[pairs + 1 : pairs + 5]
-    own_ref, sib_ref, cross_ref, spec_ref, prod_ref, block_ref = refs[pairs + 5 :]
+    back_hbm, cross_ref, spec_ref, prod_ref, block_ref, back_ref, sems = refs[pairs + 5 :]
     parts, rows, pos = block_ref.shape
     chans = rows // 2
     half = parts // 2 * pos
@@ -258,56 +258,57 @@
             corr0 = add(add(conj_mul(h0, g0), conj_mul(h1, g1)), later(corr1, not odd))
             cross1 = conj_mul(v0, g1)
             cross0 = add(add(conj_mul(v0, g0), conj_mul(v1, g1)), later(cross1, not odd))
-            for i, (re, im) in enumerate((conv0, corr0, cross0, conv1, corr1, cross1)):
+            for i, (re, im) in enumerate((conv0, corr0, conv1, corr1, cross0, cross1)):
                 at = slice(i * chans + r, i * chans + r + 16)
                 prod_ref[at, c : c + 128] = re.astype(BF16)
                 prod_ref[at, half + c : half + c + 128] = im.astype(BF16)
-    res = jnp.dot(prod_ref[...], inv_ref[...], preferred_element_type=F32)
+    inv = inv_ref[...]
     gains = jnp.concatenate([gain_ref[...]] * (half // 128), axis=1)
     scale = (2 * half) ** -0.5 / half
+    copies = []
+    res = jnp.dot(prod_ref[: 2 * rows], inv, preferred_element_type=F32) * scale
     for i in range(2):
-        top = i * 3 * chans
-        cross_ref[:, i * half : (i + 1) * half] = (
-            res[top + rows : top + rows + chans] * (1.0 / half)
-        ).astype(BF16)
-        both = (res[top : top + rows] * scale + gains * x[i].astype(F32)).astype(BF16)
+        both = (res[i * rows : (i + 1) * rows] + gains * x[i].astype(F32)).astype(BF16)
+        first = i * (parts // 2)
         for s in range(parts // 2):
-            block_ref[i * (parts // 2) + s] = both[:, s * pos : (s + 1) * pos]
-    for f, d, at in places(parts):
-        (sib_ref if f else own_ref)[d] = block_ref[at]
-
-
-def unpack_kernel(pairs, *refs):
-    grad_ref, val_hbm, gate_hbm, val_ref, gate_ref, turn_ref, sems = refs[pairs + 1 :]
-    chans = turn_ref.shape[1] // (2 * pairs)
-    block = arrived(*refs[: pairs + 1])
-    for f, d, at in places(2 * pairs):
-        at = pl.multiple_of(at * chans, chans)
-        both = block(f, d)
-        turn_ref[0, pl.ds(at, chans), :] = both[:chans]
-        turn_ref[1, pl.ds(at, chans), :] = both[chans:]
-    val_ref[0] = turn_ref[1].astype(F32).T.astype(BF16)
-    first = start_copies([(val_ref, val_hbm)], sems)
-    gate_ref[0] = (grad_ref[0].astype(F32) * turn_ref[0].astype(F32).T).astype(BF16)
-    second = pltpu.make_async_copy(gate_ref, gate_hbm, sems.at[1])
-    second.start()
-    first[0].wait()
-    second.wait()
-
-
-def pair_kernel(left_ref, right_ref, *rest):
-    out_ref = rest[-1]
+            back_ref[first + s] = both[:, s * pos : (s + 1) * pos]
+        at = pl.ds(first, parts // 2)
+        copies += start_copies([(back_ref.at[at], back_hbm.at[at])], sems.at[pl.ds(i, 1)])
+    res = jnp.dot(prod_ref[2 * rows :], inv, preferred_element_type=F32) * (1.0 / half)
+    for i in range(2):
+        cross_ref[:, i * half : (i + 1) * half] = res[i * chans : (i + 1) * chans].astype(BF16)
+    for copy in copies:
+        copy.wait()
+
+
+def pair_kernel(left_ref, right_ref, out_ref):
     out_ref[...] = (left_ref[...].astype(F32) + right_ref[...].astype(F32)).astype(BF16)
 
 
-def total_kernel(scale, left_ref, right_ref, out_hbm, out_ref, sems):
-    half = out_ref.shape[0] // 2
-    copies = []
-    for i in range(2):
-        at = pl.ds(i * half, half)
-        out_ref[at, :] = (left_ref[at, :].astype(F32) + right_ref[at, :].astype(F32)) * scale
-        copies.append(pltpu.make_async_copy(out_ref.at[at, :], out_hbm.at[at, :], sems.at[i]))
-        copies[-1].start()
+def finish_kernel(
+    scale,
+    left_ref,
+    right_ref,
+    back_ref,
+    near_ref,
+    val_hbm,
+    gate_hbm,
+    filt_hbm,
+    val_ref,
+    gate_ref,
+    filt_ref,
+    sems,
+):
+    parts, rows, _ = back_ref.shape
+    chans = rows // 2
+    filt_ref[...] = (left_ref[...].astype(F32) + right_ref[...].astype(F32)) * scale
+    copies = start_copies([(filt_ref, filt_hbm)], sems)
+    vals = jnp.concatenate([back_ref[s, chans:, :] for s in range(parts)], axis=0)
+    val_ref[0] = vals.astype(F32).T.astype(BF16)
+    copies += start_copies([(val_ref, val_hbm)], sems.at[pl.ds(1, 1)])
+    conv = jnp.concatenate([back_ref[s, :chans, :] for s in range(parts)], axis=0)
+    gate_ref[0] = (near_ref[0].astype(F32) * conv.astype(F32).T).astype(BF16)
+    copies += start_copies([(gate_ref, gate_hbm)], sems.at[pl.ds(2, 1)])
     for copy in copies:
         copy.wait()
 
@@ -340,8 +341,20 @@
         vmem_specs(2),
         moved=8 * (pairs - 1) * rows * pos,
     )
-    pair_of = [(d, [(j, j ^ (2 * d)) for j in range(2 * pairs)]) for d in range(1, pairs)]
-    return [own, got] + [lax.ppermute(sent[d - 1], "ctx", perm) for d, perm in pair_of]
+    held = [
+        lax.ppermute(sent[d - 1], "ctx", [(j, j ^ (2 * d)) for j in range(2 * pairs)])
+        for d in reversed(range(1, pairs))
+    ]
+    return [own, got] + held
+
+
+def dp_pairs(seqs, parts, step):
+    pairs = []
+    for s in range(seqs):
+        for c in range(parts):
+            other = s ^ (seqs // 2 // step if c % 2 else step)
+            pairs.append((s * parts + c, other * parts + c))
+    return pairs
 
 
 def per_device_short(values, gates, grad_out, filters, skip):
@@ -369,7 +382,12 @@
     spec, fwd_near, inv_near, gains = call(
         filter_kernel,
         "filter_spectrum",
-        [((rows, length), F32, True), (fwd.shape, BF16, True), (inv.shape, BF16, True), ((rows, 128), F32, True)],
+        [
+            ((rows, length), F32, True),
+            (fwd.shape, BF16, True),
+            (inv.shape, BF16, True),
+            ((rows, 128), F32, True),
+        ],
         tuple(in_hbm(x) for x in (filters, fwd, inv)) + (skip.reshape(1, chans),),
         hbm_specs(3) + vmem_specs(1),
         scratch=[((chans, length), F32)],
@@ -377,53 +395,45 @@
         flops=4 * chans * length * length,
         moved=8 * length * length,
     )
-    own, sib, cross = call(
+    back, cross = call(
         functools.partial(main_kernel, pairs),
         "products",
-        [(*pair_blocks, True), (*pair_blocks, True), ((chans, length), BF16, True)],
+        [((parts, rows, pos), BF16, False), ((chans, length), BF16, True)],
         tuple(in_vmem(x) for x in held + [fwd_near, inv_near, spec, gains]),
         vmem_specs(pairs + 5),
         scratch=[
             ((2 * rows, length), F32),
             ((3 * rows, length), BF16),
             ((parts, rows, pos), BF16),
+            ((parts, rows, pos), BF16),
         ],
+        sems=2,
         flops=10 * chans * length * length,
         moved=8 * length * length,
     )
-    home = exchange(own, sib, "home")
+    home = lax.all_to_all(back, "ctx", split_axis=0, concat_axis=0, tiled=True)
     step = seqs // 2
     while step:
-        other = lax.ppermute(cross, "dp", [(j, j ^ step) for j in range(seqs)])
+        other = lax.ppermute(cross, ("dp", "ctx"), dp_pairs(seqs, parts, step))
         step //= 2
         if step:
             (cross,) = call(
                 pair_kernel,
                 "pair_sum",
                 [((chans, length), BF16, True)],
-                (in_vmem(cross), in_vmem(other), *home[2:]),
-                vmem_specs(2) + hbm_specs(len(home) - 2),
+                (in_vmem(cross), in_vmem(other)),
+                vmem_specs(2),
                 moved=6 * chans * length,
             )
-    grad_values, grad_gates = call(
-        functools.partial(unpack_kernel, pairs),
-        "unpack",
-        [(*token, False), (*token, False)],
-        tuple(in_vmem(x) for x in home + [grad_near]),
-        vmem_specs(pairs + 2),
-        scratch=[token, token, turned],
-        sems=2,
-        moved=10 * pos * width,
-    )
-    (grad_filters,) = call(
-        functools.partial(total_kernel, (seqs * length) ** (-0.5)),
-        "total",
-        [((chans, length), F32, False)],
-        (in_vmem(cross), in_vmem(other)),
-        vmem_specs(2),
-        scratch=[((chans, length), F32)],
-        sems=2,
-        moved=12 * chans * length,
+    grad_values, grad_gates, grad_filters = call(
+        functools.partial(finish_kernel, (seqs * length) ** (-0.5)),
+        "finish",
+        [(*token, False), (*token, False), ((chans, length), F32, False)],
+        tuple(in_vmem(x) for x in (cross, other, home, grad_near)),
+        vmem_specs(4),
+        scratch=[token, token, ((chans, length), F32)],
+        sems=3,
+        moved=10 * pos * width + 8 * chans * length,
     )
     return (grad_values, grad_gates, grad_filters)
 

time: 30 us -> 28.1 us (0.937)
  waiting for transfers between devices: 10.4 us -> 8.9 us
  starting transfers between devices: 12.2 us -> 11.8 us
    ppermute x8 -> x5, waiting for transfers between devices: 9.43 us -> 3.08 us  [the longest x3 1.82 us: exchange(): lax.ppermute(sent[d - 1], 'ctx', [(j, j ^ 2 * d) for j in range(2 * pairs)])]
    all_to_all x0 -> x1, waiting for transfers between devices: none -> 4.83 us  [per_device_short(): home = lax.all_to_all(back, 'ctx', split_axis=0, concat_axis=0, tiled=True)]
    ppermute x8 -> x5, starting transfers between devices: 11.6 us -> 7.89 us  [the longest x3 4.51 us: exchange(): lax.ppermute(sent[d - 1], 'ctx', [(j, j ^ 2 * d) for j in range(2 * pairs)])]
    all_to_all x0 -> x1, starting transfers between devices: none -> 3.41 us  [per_device_short(): home = lax.all_to_all(back, 'ctx', split_axis=0, concat_axis=0, tiled=True)]
    pallas_call x8 -> x6, Pallas kernels: 5.92 us -> 5.85 us  [call(): pl.pallas_call(kernel, out_shape=tuple((pltpu.VMEM(shape, dtype) if near...]
    ppermute x2 -> x1, waiting for transfers between devices: 0.99 us -> 0.99 us  [exchange(): got = lax.ppermute(sib, 'ctx', [(j, j ^ 1) for j in range(2 * pairs)])]
  transfers between devices with their start and end apart: 10 -> 7, of which waited for: 5 -> 5; matrix products, arithmetic and copies ran while one was open for 0% -> 0% of each run, Pallas kernels for 9% -> 7%
where the time goes in v3:
time: 28.1 us; the launch traced here: 27.8 us
  starting transfers between devices  11.8 us (42%)
  waiting for transfers between devices  8.9 us (32%)
  Pallas kernels  5.85 us (21%)
  between operations  0.68 us (2%)
  local copies, waits for them, and re-layouts  0.52 us (2%)
    pallas_call x6, Pallas kernels, call(): pl.pallas_call(kernel, out_shape=tuple((pltpu.VMEM(shape, dtype) if near...  5.85 us
    all_to_all x1, waiting for transfers between devices, per_device_short(): home = lax.all_to_all(back, 'ctx', split_axis=0, concat_axis=0, tiled=True)  4.83 us
    ppermute x3, starting transfers between devices, exchange(): lax.ppermute(sent[d - 1], 'ctx', [(j, j ^ 2 * d) for j in range(2 * pairs)])  4.51 us
    all_to_all x1, starting transfers between devices, per_device_short(): home = lax.all_to_all(back, 'ctx', split_axis=0, concat_axis=0, tiled=True)  3.41 us
    ppermute x2, starting transfers between devices, per_device_short(): other = lax.ppermute(cross, ('dp', 'ctx'), dp_pairs(seqs, parts, step))  3.39 us
    ppermute x3, waiting for transfers between devices, exchange(): lax.ppermute(sent[d - 1], 'ctx', [(j, j ^ 2 * d) for j in range(2 * pairs)])  1.82 us
    ppermute x2, waiting for transfers between devices, per_device_short(): other = lax.ppermute(cross, ('dp', 'ctx'), dp_pairs(seqs, parts, step))  1.27 us
    ppermute x1, waiting for transfers between devices, exchange(): got = lax.ppermute(sib, 'ctx', [(j, j ^ 1) for j in range(2 * pairs)])  0.99 us
  transfers between devices with their start and end apart: 7, of which 5 were waited for; matrix products, arithmetic and copies ran while one was open for 0% of the time, Pallas kernels for 7%

profile of v3, /device:TPU:0, one launch (start us, length us, event | category | flops | bytes accessed | tf_op | source)
XLA Modules:
  0.0 27.8 jit_solution(6206979381789268939)
XLA Ops:
  0.6 1.2 %pack.1 = (bf16[4,128,128]{2,1,0:T(8,128)(2,1)S(1)}, bf16[4,128,128]{2,1,0:T(8,128)(2,1)S(1)}, bf16[1,128,512]{2,1,0:T(8,128)(2,1)S(1)}) custom-call(bf16[1,128,512]{2,1,0:T(8,128)(2,1)} %vals_hbm.1, bf16[1,128,512]{2,1,0:T(8,128)(2,1)} %gate_hbm.1, bf16[1,128,512]{2,1,0:T(8,128)(2,1)} %grad_hbm.1), custom_call_target="tpu_custom_call" | custom-call | bytes 524288 | tf_op jit(solution)/shard_map/pack/pallas_call | solution.py:317
  1.8 0.5 %collective-permute-start = (bf16[4,128,128]{2,1,0:T(8,128)(2,1)S(1)}, bf16[4,128,128]{2,1,0:T(8,128)(2,1)S(1)}, u32[]{:S(2)}, u32[]{:S(2)}) collective-permute-start(bf16[4,128,128]{2,1,0:T(8,128)(2,1)S(1)} %get-tuple-element.16), channel_id=1, source_target_pairs={{0,1},{1,0},{2,3},{3,2},{4,5},{5,4},{6,7},{7,6},{8,9},{9,8},{10,11... | collective-permute-start | bytes 393224 | tf_op jit(solution)/shard_map/ppermute | solution.py:335
  2.3 1.0 %collective-permute-done.got_ref.refs_1_ = bf16[4,128,128]{2,1,0:T(8,128)(2,1)S(1)} collective-permute-done((bf16[4,128,128]{2,1,0:T(8,128)(2,1)S(1)}, bf16[4,128,128]{2,1,0:T(8,128)(2,1)S(1)}, u32[]{:S(2)}, u32[]{:S(2)}) %collective-permute-start) | collective-permute-done | bytes 131104 | tf_op jit(solution)/shard_map/ppermute | solution.py:335
  3.3 3.9 %collective-permute-start.1 = (bf16[2,128,128]{2,1,0:T(8,128)(2,1)S(1)}, bf16[2,128,128]{2,1,0:T(8,128)(2,1)S(1)}, u32[]{:S(2)}, u32[]{:S(2)}) collective-permute-start(bf16[2,128,128]{2,1,0:T(8,128)(2,1)S(1)} %get-tuple-element.17), channel_id=1, source_target_pairs={{0,6},{1,7},{2,4},{3,5},{4,2},{5,3},{6,0},{7,1},{8,14},{9,15},{10,... | collective-permute-start | bytes 196616 | tf_op jit(solution)/shard_map/ppermute | solution.py:345
  7.2 0.5 %collective-permute-start.2 = (bf16[2,128,128]{2,1,0:T(8,128)(2,1)S(1)}, bf16[2,128,128]{2,1,0:T(8,128)(2,1)S(1)}, u32[]{:S(2)}, u32[]{:S(2)}) collective-permute-start(bf16[2,128,128]{2,1,0:T(8,128)(2,1)S(1)} %get-tuple-element.18), channel_id=1, source_target_pairs={{0,4},{1,5},{2,6},{3,7},{4,0},{5,1},{6,2},{7,3},{8,12},{9,13},{10,... | collective-permute-start | bytes 196616 | tf_op jit(solution)/shard_map/ppermute | solution.py:345
  7.7 0.0 copy-start
  7.7 0.1 collective-permute-start.3
  7.9 0.5 %copy-done = f32[64]{0:T(128)S(1)} copy-done((f32[64]{0:T(128)S(1)}, f32[64]{0:T(128)}, u32[]{:S(2)}) %copy-start) | copy-done | bytes 280
  8.4 1.8 %filter_spectrum.1 = (f32[128,1024]{1,0:T(8,128)S(1)}, bf16[512,1024]{1,0:T(8,128)(2,1)S(1)}, bf16[1024,512]{1,0:T(8,128)(2,1)S(1)}, f32[128,128]{1,0:T(8,128)S(1)}) custom-call(f32[64,1024]{1,0:T(8,128)} %filt_hbm.1, bf16[512,1024]{1,0:T(8,128)(2,1)} %constant.4.clone.fwd_hbm, bf16[1024,512]{1,0:T(8,128)(2,1)} %constant.5.clone.inv_hbm, f32[1,64]{1,0:T(1,128)S(1)} %bitcast.1), custom_call_target="tpu_custom_call" | custom-call | flops 268435456 | bytes 8388608 | tf_op jit(solution)/shard_map/filter_spectrum/pallas_call | solution.py:317
  10.2 0.0 collective-permute-done.1.refs_2_
  10.2 1.3 %collective-permute-done.2.refs_3_ = bf16[2,128,128]{2,1,0:T(8,128)(2,1)S(1)} collective-permute-done((bf16[2,128,128]{2,1,0:T(8,128)(2,1)S(1)}, bf16[2,128,128]{2,1,0:T(8,128)(2,1)S(1)}, u32[]{:S(2)}, u32[]{:S(2)}) %collective-permute-start.2) | collective-permute-done | bytes 65568 | tf_op jit(solution)/shard_map/ppermute | solution.py:345
  11.5 0.5 %collective-permute-done.3.refs_4_ = bf16[2,128,128]{2,1,0:T(8,128)(2,1)S(1)} collective-permute-done((bf16[2,128,128]{2,1,0:T(8,128)(2,1)S(1)}, bf16[2,128,128]{2,1,0:T(8,128)(2,1)S(1)}, u32[]{:S(2)}, u32[]{:S(2)}) %collective-permute-start.3) | collective-permute-done | bytes 65568 | tf_op jit(solution)/shard_map/ppermute | solution.py:345
  12.0 1.9 %products.1 = (bf16[8,128,128]{2,1,0:T(8,128)(2,1)}, bf16[64,1024]{1,0:T(8,128)(2,1)S(1)}) custom-call(bf16[4,128,128]{2,1,0:T(8,128)(2,1)S(1)} %get-tuple-element.15.own_ref.refs_0_, bf16[4,128,128]{2,1,0:T(8,128)(2,1)S(1)} %collective-permute-done.got_ref.refs_1_, bf16[2,128,128]{2,1,0:T(8,128)(2,1)S(1)} %collective-permute-done.1.refs_2_, ...), custom_call_target="tpu_custom_call" | custom-call | flops 671088640 | bytes 8388608 | tf_op jit(solution)/shard_map/products/pallas_call | solution.py:317
  13.8 2.7 %collective-permute-start.4 = (bf16[64,1024]{1,0:T(8,128)(2,1)S(1)}, bf16[64,1024]{1,0:T(8,128)(2,1)S(1)}, u32[]{:S(2)}, u32[]{:S(2)}) collective-permute-start(bf16[64,1024]{1,0:T(8,128)(2,1)S(1)} %get-tuple-element.24.left_ref), channel_id=1, source_target_pairs={{0,16},{1,9},{2,18},{3,11},{4,20},{5,13},{6,22},{7,15},{8,24},{9,1... | collective-permute-start | bytes 393224 | tf_op jit(solution)/shard_map/ppermute | solution.py:417
  16.5 3.4 %all-to-all-start = ((bf16[8,128,128]{2,1,0:T(8,128)(2,1)}), bf16[8,128,128]{2,1,0:T(8,128)(2,1)S(1)}, u32[]{:S(2)}, u32[]{:S(2)}) async-start(bf16[8,128,128]{2,1,0:T(8,128)(2,1)} %get-tuple-element.25), calls=%async_computation | async-start | bytes 524288 | tf_op jit(solution)/shard_map/all_to_all | solution.py:414
  19.9 1.3 %collective-permute-done.4.right_ref = bf16[64,1024]{1,0:T(8,128)(2,1)S(1)} collective-permute-done((bf16[64,1024]{1,0:T(8,128)(2,1)S(1)}, bf16[64,1024]{1,0:T(8,128)(2,1)S(1)}, u32[]{:S(2)}, u32[]{:S(2)}) %collective-permute-start.4) | collective-permute-done | bytes 131104 | tf_op jit(solution)/shard_map/ppermute | solution.py:417
  21.2 0.7 %collective-permute-start.5 = (bf16[64,1024]{1,0:T(8,128)(2,1)S(1)}, bf16[64,1024]{1,0:T(8,128)(2,1)S(1)}, u32[]{:S(2)}, u32[]{:S(2)}) collective-permute-start(bf16[64,1024]{1,0:T(8,128)(2,1)S(1)} %pair_sum.1.left_ref), channel_id=1, source_target_pairs={{0,8},{1,17},{2,10},{3,19},{4,12},{5,21},{6,14},{7,23},{8,0},{9,25... | collective-permute-start | bytes 393224 | tf_op jit(solution)/shard_map/ppermute | solution.py:417
  22.0 4.8 %all-to-all-done.back_ref = bf16[8,128,128]{2,1,0:T(8,128)(2,1)S(1)} async-done(((bf16[8,128,128]{2,1,0:T(8,128)(2,1)}), bf16[8,128,128]{2,1,0:T(8,128)(2,1)S(1)}, u32[]{:S(2)}, u32[]{:S(2)}) %all-to-all-start) | async-done | bytes 262176 | tf_op jit(solution)/shard_map/all_to_all | solution.py:414
  26.8 0.0 collective-permute-done.5.right_ref
  26.8 1.0 %finish.1 = (bf16[1,128,512]{2,1,0:T(8,128)(2,1)}, bf16[1,128,512]{2,1,0:T(8,128)(2,1)}, f32[64,1024]{1,0:T(8,128)}) custom-call(bf16[64,1024]{1,0:T(8,128)(2,1)S(1)} %pair_sum.1.left_ref, bf16[64,1024]{1,0:T(8,128)(2,1)S(1)} %collective-permute-done.5.right_ref, bf16[8,128,128]{2,1,0:T(8,128)(2,1)S(1)} %all-to-all-done.back_ref, ...), custom_call_target="tpu_custom_call" | custom-call | bytes 1179648 | tf_op jit(solution)/shard_map/finish/pallas_call | solution.py:317
  (2 shorter events, 0.0 us)
Async XLA Ops:
  1.8 1.5 %collective-permute-start = (bf16[4,128,128]{2,1,0:T(8,128)(2,1)S(1)}, bf16[4,128,128]{2,1,0:T(8,128)(2,1)S(1)}, u32[]{:S(2)}, u32[]{:S(2)}) collective-permute-start(bf16[4,128,128]{2,1,0:T(8,128)(2,1)S(1)} %get-tuple-element.16), channel_id=1, source_target_pairs={{0,1},{1,0},{2,3},{3,2},{4,5},{5,4},{6,7},{7,6},{8,9},{9,8},{10,11... | collective-permute-start | bytes 393224 | tf_op jit(solution)/shard_map/ppermute | solution.py:335
  3.3 6.8 %collective-permute-start.1 = (bf16[2,128,128]{2,1,0:T(8,128)(2,1)S(1)}, bf16[2,128,128]{2,1,0:T(8,128)(2,1)S(1)}, u32[]{:S(2)}, u32[]{:S(2)}) collective-permute-start(bf16[2,128,128]{2,1,0:T(8,128)(2,1)S(1)} %get-tuple-element.17), channel_id=1, source_target_pairs={{0,6},{1,7},{2,4},{3,5},{4,2},{5,3},{6,0},{7,1},{8,14},{9,15},{10,... | collective-permute-start | bytes 196616 | tf_op jit(solution)/shard_map/ppermute | solution.py:345
  7.2 4.3 %collective-permute-start.2 = (bf16[2,128,128]{2,1,0:T(8,128)(2,1)S(1)}, bf16[2,128,128]{2,1,0:T(8,128)(2,1)S(1)}, u32[]{:S(2)}, u32[]{:S(2)}) collective-permute-start(bf16[2,128,128]{2,1,0:T(8,128)(2,1)S(1)} %get-tuple-element.18), channel_id=1, source_target_pairs={{0,4},{1,5},{2,6},{3,7},{4,0},{5,1},{6,2},{7,3},{8,12},{9,13},{10,... | collective-permute-start | bytes 196616 | tf_op jit(solution)/shard_map/ppermute | solution.py:345
  7.7 0.7 %copy-start = (f32[64]{0:T(128)S(1)}, f32[64]{0:T(128)}, u32[]{:S(2)}) copy-start(f32[64]{0:T(128)} %param.11) | copy-start | bytes 772
  7.7 4.3 %collective-permute-start.3 = (bf16[2,128,128]{2,1,0:T(8,128)(2,1)S(1)}, bf16[2,128,128]{2,1,0:T(8,128)(2,1)S(1)}, u32[]{:S(2)}, u32[]{:S(2)}) collective-permute-start(bf16[2,128,128]{2,1,0:T(8,128)(2,1)S(1)} %get-tuple-element.19), channel_id=1, source_target_pairs={{0,2},{1,3},{2,0},{3,1},{4,6},{5,7},{6,4},{7,5},{8,10},{9,11},{10,... | collective-permute-start | bytes 196616 | tf_op jit(solution)/shard_map/ppermute | solution.py:345
  13.8 7.3 %collective-permute-start.4 = (bf16[64,1024]{1,0:T(8,128)(2,1)S(1)}, bf16[64,1024]{1,0:T(8,128)(2,1)S(1)}, u32[]{:S(2)}, u32[]{:S(2)}) collective-permute-start(bf16[64,1024]{1,0:T(8,128)(2,1)S(1)} %get-tuple-element.24.left_ref), channel_id=1, source_target_pairs={{0,16},{1,9},{2,18},{3,11},{4,20},{5,13},{6,22},{7,15},{8,24},{9,1... | collective-permute-start | bytes 393224 | tf_op jit(solution)/shard_map/ppermute | solution.py:417
  16.5 10.3 %all-to-all-start = ((bf16[8,128,128]{2,1,0:T(8,128)(2,1)}), bf16[8,128,128]{2,1,0:T(8,128)(2,1)S(1)}, u32[]{:S(2)}, u32[]{:S(2)}) async-start(bf16[8,128,128]{2,1,0:T(8,128)(2,1)} %get-tuple-element.25), calls=%async_computation | async-start | bytes 524288 | tf_op jit(solution)/shard_map/all_to_all | solution.py:414
  21.2 5.6 %collective-permute-start.5 = (bf16[64,1024]{1,0:T(8,128)(2,1)S(1)}, bf16[64,1024]{1,0:T(8,128)(2,1)S(1)}, u32[]{:S(2)}, u32[]{:S(2)}) collective-permute-start(bf16[64,1024]{1,0:T(8,128)(2,1)S(1)} %pair_sum.1.left_ref), channel_id=1, source_target_pairs={{0,8},{1,17},{2,10},{3,19},{4,12},{5,21},{6,14},{7,23},{8,0},{9,25... | collective-permute-start | bytes 393224 | tf_op jit(solution)/shard_map/ppermute | solution.py:417

commit v4 on v3

--- a/solution.py
+++ b/solution.py
@@ -184,6 +184,11 @@
         out_ref[1] = got_ref[d]
 
 
+def join_kernel(own_ref, got_ref, out_ref):
+    out_ref[:, 0] = own_ref[...]
+    out_ref[:, 1] = got_ref[...]
+
+
 def arrived(own_ref, got_ref, *pair_refs):
     return lambda f, d: pair_refs[-d][f] if d else (got_ref if f else own_ref)[0]
 
@@ -228,7 +233,7 @@
 
 def main_kernel(pairs, *refs):
     fwd_ref, inv_ref, filt_ref, gain_ref = refs[pairs + 1 : pairs + 5]
-    back_hbm, cross_ref, spec_ref, prod_ref, block_ref, back_ref, sems = refs[pairs + 5 :]
+    own_ref, sib_ref, cross_ref, spec_ref, prod_ref, block_ref = refs[pairs + 5 :]
     parts, rows, pos = block_ref.shape
     chans = rows // 2
     half = parts // 2 * pos
@@ -242,43 +247,51 @@
     spec_ref[...] = jnp.dot(
         jnp.concatenate(x, axis=0), fwd_ref[...], preferred_element_type=F32
     )
-    for r in range(0, chans, 16):
-        for c in range(0, half, 128):
-            odd = c >= half // 2
-
-            def load(ref, row):
-                at = slice(row + r, row + r + 16)
-                return (ref[at, c : c + 128], ref[at, half + c : half + c + 128])
-
-            v0, g0, v1, g1 = [load(spec_ref, i * chans) for i in range(4)]
-            h0, h1 = [load(filt_ref, i * chans) for i in range(2)]
-            conv0 = mul(h0, v0)
-            conv1 = add(add(mul(h0, v1), mul(h1, v0)), later(conv0, odd))
-            corr1 = conj_mul(h0, g1)
-            corr0 = add(add(conj_mul(h0, g0), conj_mul(h1, g1)), later(corr1, not odd))
-            cross1 = conj_mul(v0, g1)
-            cross0 = add(add(conj_mul(v0, g0), conj_mul(v1, g1)), later(cross1, not odd))
-            for i, (re, im) in enumerate((conv0, corr0, conv1, corr1, cross0, cross1)):
-                at = slice(i * chans + r, i * chans + r + 16)
-                prod_ref[at, c : c + 128] = re.astype(BF16)
-                prod_ref[at, half + c : half + c + 128] = im.astype(BF16)
     inv = inv_ref[...]
     gains = jnp.concatenate([gain_ref[...]] * (half // 128), axis=1)
     scale = (2 * half) ** -0.5 / half
-    copies = []
-    res = jnp.dot(prod_ref[: 2 * rows], inv, preferred_element_type=F32) * scale
+
+    def products(count, terms):
+        for r in range(0, chans, 16):
+            for c in range(0, half, 128):
+
+                def load(ref, row):
+                    at = slice(row * chans + r, row * chans + r + 16)
+                    return (ref[at, c : c + 128], ref[at, half + c : half + c + 128])
+
+                for i, (re, im) in enumerate(terms(load, c >= half // 2)):
+                    at = slice(i * chans + r, i * chans + r + 16)
+                    prod_ref[at, c : c + 128] = re.astype(BF16)
+                    prod_ref[at, half + c : half + c + 128] = im.astype(BF16)
+        return jnp.dot(prod_ref[: count * chans], inv, preferred_element_type=F32)
+
+    def with_filter(load, odd):
+        v0, g0, v1, g1 = [load(spec_ref, i) for i in range(4)]
+        h0, h1 = [load(filt_ref, i) for i in range(2)]
+        conv0 = mul(h0, v0)
+        conv1 = add(add(mul(h0, v1), mul(h1, v0)), later(conv0, odd))
+        corr1 = conj_mul(h0, g1)
+        corr0 = add(add(conj_mul(h0, g0), conj_mul(h1, g1)), later(corr1, not odd))
+        return (conv0, corr0, conv1, corr1)
+
+    def with_values(load, odd):
+        v0, g0, v1, g1 = [load(spec_ref, i) for i in range(4)]
+        cross1 = conj_mul(v0, g1)
+        cross0 = add(add(conj_mul(v0, g0), conj_mul(v1, g1)), later(cross1, not odd))
+        return (cross0, cross1)
+
+    res = products(4, with_filter) * scale
     for i in range(2):
         both = (res[i * rows : (i + 1) * rows] + gains * x[i].astype(F32)).astype(BF16)
-        first = i * (parts // 2)
         for s in range(parts // 2):
-            back_ref[first + s] = both[:, s * pos : (s + 1) * pos]
-        at = pl.ds(first, parts // 2)
-        copies += start_copies([(back_ref.at[at], back_hbm.at[at])], sems.at[pl.ds(i, 1)])
-    res = jnp.dot(prod_ref[2 * rows :], inv, preferred_element_type=F32) * (1.0 / half)
+            block_ref[i * (parts // 2) + s] = both[:, s * pos : (s + 1) * pos]
+    core = lax.axis_index("ctx") % 2
+    for p in range(pairs):
+        own_ref[p] = block_ref[2 * p + core]
+        sib_ref[p] = block_ref[2 * p + 1 - core]
+    res = products(2, with_values) * (1.0 / half)
     for i in range(2):
         cross_ref[:, i * half : (i + 1) * half] = res[i * chans : (i + 1) * chans].astype(BF16)
-    for copy in copies:
-        copy.wait()
 
 
 def pair_kernel(left_ref, right_ref, out_ref):
@@ -299,14 +312,16 @@
     filt_ref,
     sems,
 ):
-    parts, rows, _ = back_ref.shape
+    pairs, _, rows, _ = back_ref.shape
     chans = rows // 2
     filt_ref[...] = (left_ref[...].astype(F32) + right_ref[...].astype(F32)) * scale
     copies = start_copies([(filt_ref, filt_hbm)], sems)
-    vals = jnp.concatenate([back_ref[s, chans:, :] for s in range(parts)], axis=0)
+    core = lax.axis_index("ctx") % 2
+    both = [back_ref[p, (core + f) % 2] for p in range(pairs) for f in range(2)]
+    vals = jnp.concatenate([block[chans:] for block in both], axis=0)
     val_ref[0] = vals.astype(F32).T.astype(BF16)
     copies += start_copies([(val_ref, val_hbm)], sems.at[pl.ds(1, 1)])
-    conv = jnp.concatenate([back_ref[s, :chans, :] for s in range(parts)], axis=0)
+    conv = jnp.concatenate([block[:chans] for block in both], axis=0)
     gate_ref[0] = (near_ref[0].astype(F32) * conv.astype(F32).T).astype(BF16)
     copies += start_copies([(gate_ref, gate_hbm)], sems.at[pl.ds(2, 1)])
     for copy in copies:
@@ -395,23 +410,33 @@
         flops=4 * chans * length * length,
         moved=8 * length * length,
     )
-    back, cross = call(
+    own, sib, cross = call(
         functools.partial(main_kernel, pairs),
         "products",
-        [((parts, rows, pos), BF16, False), ((chans, length), BF16, True)],
+        [(*pair_blocks, True), (*pair_blocks, True), ((chans, length), BF16, True)],
         tuple(in_vmem(x) for x in held + [fwd_near, inv_near, spec, gains]),
         vmem_specs(pairs + 5),
         scratch=[
             ((2 * rows, length), F32),
-            ((3 * rows, length), BF16),
-            ((parts, rows, pos), BF16),
+            ((2 * rows, length), BF16),
             ((parts, rows, pos), BF16),
         ],
-        sems=2,
         flops=10 * chans * length * length,
         moved=8 * length * length,
     )
-    home = lax.all_to_all(back, "ctx", split_axis=0, concat_axis=0, tiled=True)
+    got = lax.ppermute(sib, "ctx", [(j, j ^ 1) for j in range(parts)])
+    (sent,) = call(
+        join_kernel,
+        "join",
+        [((pairs, 2, rows, pos), BF16, True)],
+        (in_vmem(own), in_vmem(got)),
+        vmem_specs(2),
+        moved=8 * pairs * rows * pos,
+    )
+    cores = [list(range(f, parts, 2)) for f in range(2)]
+    home = lax.all_to_all(
+        sent, "ctx", split_axis=0, concat_axis=0, tiled=True, axis_index_groups=cores
+    )
     step = seqs // 2
     while step:
         other = lax.ppermute(cross, ("dp", "ctx"), dp_pairs(seqs, parts, step))

time: 28.1 us -> 27.2 us (0.968)
  waiting for transfers between devices: 8.9 us -> 6.7 us
  starting transfers between devices: 11.8 us -> 12.9 us
    all_to_all x1, waiting for transfers between devices: 4.83 us -> 0.01 us  [per_device_short(): lax.all_to_all(sent, 'ctx', split_axis=0, concat_axis=0, tiled=True, axis...]
    ppermute x2, waiting for transfers between devices: 1.27 us -> 3.89 us  [per_device_short(): other = lax.ppermute(cross, ('dp', 'ctx'), dp_pairs(seqs, parts, step))]
    ppermute x2, starting transfers between devices: 3.39 us -> 4.4 us  [per_device_short(): other = lax.ppermute(cross, ('dp', 'ctx'), dp_pairs(seqs, parts, step))]
    pallas_call x6 -> x7, Pallas kernels: 5.85 us -> 6.07 us  [call(): pl.pallas_call(kernel, out_shape=tuple((pltpu.VMEM(shape, dtype) if near...]
  transfers between devices with their start and end apart: 7 -> 8, of which waited for: 5 -> 4; matrix products, arithmetic and copies ran while one was open for 0% -> 0% of each run, Pallas kernels for 7% -> 9%
where the time goes in v4:
time: 27.2 us; the launch traced here: 26.9 us
  starting transfers between devices  12.9 us (47%)
  waiting for transfers between devices  6.7 us (25%)
  Pallas kernels  6.07 us (22%)
  between operations  0.7 us (3%)
  local copies, waits for them, and re-layouts  0.52 us (2%)
    pallas_call x7, Pallas kernels, call(): pl.pallas_call(kernel, out_shape=tuple((pltpu.VMEM(shape, dtype) if near...  6.07 us
    ppermute x3, starting transfers between devices, exchange(): lax.ppermute(sent[d - 1], 'ctx', [(j, j ^ 2 * d) for j in range(2 * pairs)])  4.51 us
    ppermute x2, starting transfers between devices, per_device_short(): other = lax.ppermute(cross, ('dp', 'ctx'), dp_pairs(seqs, parts, step))  4.4 us
    ppermute x2, waiting for transfers between devices, per_device_short(): other = lax.ppermute(cross, ('dp', 'ctx'), dp_pairs(seqs, parts, step))  3.89 us
    all_to_all x1, starting transfers between devices, per_device_short(): lax.all_to_all(sent, 'ctx', split_axis=0, concat_axis=0, tiled=True, axis...  3.41 us
    ppermute x3, waiting for transfers between devices, exchange(): lax.ppermute(sent[d - 1], 'ctx', [(j, j ^ 2 * d) for j in range(2 * pairs)])  1.82 us
    ppermute x1, waiting for transfers between devices, exchange(): got = lax.ppermute(sib, 'ctx', [(j, j ^ 1) for j in range(2 * pairs)])  0.99 us
  transfers between devices with their start and end apart: 8, of which 4 were waited for; matrix products, arithmetic and copies ran while one was open for 0% of the time, Pallas kernels for 9%

profile of v4, /device:TPU:0, one launch (start us, length us, event | category | flops | bytes accessed | tf_op | source)
XLA Modules:
  0.0 26.9 jit_solution(14057240883393204662)
XLA Ops:
  0.6 1.2 %pack.1 = (bf16[4,128,128]{2,1,0:T(8,128)(2,1)S(1)}, bf16[4,128,128]{2,1,0:T(8,128)(2,1)S(1)}, bf16[1,128,512]{2,1,0:T(8,128)(2,1)S(1)}) custom-call(bf16[1,128,512]{2,1,0:T(8,128)(2,1)} %vals_hbm.1, bf16[1,128,512]{2,1,0:T(8,128)(2,1)} %gate_hbm.1, bf16[1,128,512]{2,1,0:T(8,128)(2,1)} %grad_hbm.1), custom_call_target="tpu_custom_call" | custom-call | bytes 524288 | tf_op jit(solution)/shard_map/pack/pallas_call | solution.py:332
  1.8 0.5 %collective-permute-start = (bf16[4,128,128]{2,1,0:T(8,128)(2,1)S(1)}, bf16[4,128,128]{2,1,0:T(8,128)(2,1)S(1)}, u32[]{:S(2)}, u32[]{:S(2)}) collective-permute-start(bf16[4,128,128]{2,1,0:T(8,128)(2,1)S(1)} %get-tuple-element.17), channel_id=1, source_target_pairs={{0,1},{1,0},{2,3},{3,2},{4,5},{5,4},{6,7},{7,6},{8,9},{9,8},{10,11... | collective-permute-start | bytes 393224 | tf_op jit(solution)/shard_map/ppermute | solution.py:350
  2.3 1.0 %collective-permute-done.got_ref.refs_1_ = bf16[4,128,128]{2,1,0:T(8,128)(2,1)S(1)} collective-permute-done((bf16[4,128,128]{2,1,0:T(8,128)(2,1)S(1)}, bf16[4,128,128]{2,1,0:T(8,128)(2,1)S(1)}, u32[]{:S(2)}, u32[]{:S(2)}) %collective-permute-start) | collective-permute-done | bytes 131104 | tf_op jit(solution)/shard_map/ppermute | solution.py:350
  3.3 3.9 %collective-permute-start.1 = (bf16[2,128,128]{2,1,0:T(8,128)(2,1)S(1)}, bf16[2,128,128]{2,1,0:T(8,128)(2,1)S(1)}, u32[]{:S(2)}, u32[]{:S(2)}) collective-permute-start(bf16[2,128,128]{2,1,0:T(8,128)(2,1)S(1)} %get-tuple-element.18), channel_id=1, source_target_pairs={{0,6},{1,7},{2,4},{3,5},{4,2},{5,3},{6,0},{7,1},{8,14},{9,15},{10,... | collective-permute-start | bytes 196616 | tf_op jit(solution)/shard_map/ppermute | solution.py:360
  7.2 0.5 %collective-permute-start.2 = (bf16[2,128,128]{2,1,0:T(8,128)(2,1)S(1)}, bf16[2,128,128]{2,1,0:T(8,128)(2,1)S(1)}, u32[]{:S(2)}, u32[]{:S(2)}) collective-permute-start(bf16[2,128,128]{2,1,0:T(8,128)(2,1)S(1)} %get-tuple-element.19), channel_id=1, source_target_pairs={{0,4},{1,5},{2,6},{3,7},{4,0},{5,1},{6,2},{7,3},{8,12},{9,13},{10,... | collective-permute-start | bytes 196616 | tf_op jit(solution)/shard_map/ppermute | solution.py:360
  7.7 0.0 copy-start
  7.7 0.1 collective-permute-start.3
  7.9 0.5 %copy-done = f32[64]{0:T(128)S(1)} copy-done((f32[64]{0:T(128)S(1)}, f32[64]{0:T(128)}, u32[]{:S(2)}) %copy-start) | copy-done | bytes 280
  8.4 1.8 %filter_spectrum.1 = (f32[128,1024]{1,0:T(8,128)S(1)}, bf16[512,1024]{1,0:T(8,128)(2,1)S(1)}, bf16[1024,512]{1,0:T(8,128)(2,1)S(1)}, f32[128,128]{1,0:T(8,128)S(1)}) custom-call(f32[64,1024]{1,0:T(8,128)} %filt_hbm.1, bf16[512,1024]{1,0:T(8,128)(2,1)} %constant.4.clone.fwd_hbm, bf16[1024,512]{1,0:T(8,128)(2,1)} %constant.5.clone.inv_hbm, f32[1,64]{1,0:T(1,128)S(1)} %bitcast.1), custom_call_target="tpu_custom_call" | custom-call | flops 268435456 | bytes 8388608 | tf_op jit(solution)/shard_map/filter_spectrum/pallas_call | solution.py:332
  10.2 0.0 collective-permute-done.1.refs_2_
  10.2 1.3 %collective-permute-done.2.refs_3_ = bf16[2,128,128]{2,1,0:T(8,128)(2,1)S(1)} collective-permute-done((bf16[2,128,128]{2,1,0:T(8,128)(2,1)S(1)}, bf16[2,128,128]{2,1,0:T(8,128)(2,1)S(1)}, u32[]{:S(2)}, u32[]{:S(2)}) %collective-permute-start.2) | collective-permute-done | bytes 65568 | tf_op jit(solution)/shard_map/ppermute | solution.py:360
  11.5 0.5 %collective-permute-done.3.refs_4_ = bf16[2,128,128]{2,1,0:T(8,128)(2,1)S(1)} collective-permute-done((bf16[2,128,128]{2,1,0:T(8,128)(2,1)S(1)}, bf16[2,128,128]{2,1,0:T(8,128)(2,1)S(1)}, u32[]{:S(2)}, u32[]{:S(2)}) %collective-permute-start.3) | collective-permute-done | bytes 65568 | tf_op jit(solution)/shard_map/ppermute | solution.py:360
  12.0 1.3 %products.1 = (bf16[4,128,128]{2,1,0:T(8,128)(2,1)S(1)}, bf16[4,128,128]{2,1,0:T(8,128)(2,1)S(1)}, bf16[64,1024]{1,0:T(8,128)(2,1)S(1)}) custom-call(bf16[4,128,128]{2,1,0:T(8,128)(2,1)S(1)} %get-tuple-element.16.own_ref.refs_0_, bf16[4,128,128]{2,1,0:T(8,128)(2,1)S(1)} %collective-permute-done.got_ref.refs_1_, ...), custom_call_target="tpu_custom_call" | custom-call | flops 671088640 | bytes 8388608 | tf_op jit(solution)/shard_map/products/pallas_call | solution.py:332
  13.3 0.1 collective-permute-start.6
  13.4 2.7 %collective-permute-start.4 = (bf16[64,1024]{1,0:T(8,128)(2,1)S(1)}, bf16[64,1024]{1,0:T(8,128)(2,1)S(1)}, u32[]{:S(2)}, u32[]{:S(2)}) collective-permute-start(bf16[64,1024]{1,0:T(8,128)(2,1)S(1)} %get-tuple-element.25.left_ref), channel_id=1, source_target_pairs={{0,16},{1,9},{2,18},{3,11},{4,20},{5,13},{6,22},{7,15},{8,24},{9,1... | collective-permute-start | bytes 393224 | tf_op jit(solution)/shard_map/ppermute | solution.py:442
  16.1 0.0 collective-permute-done.6.got_ref
  16.1 0.7 %join.1 = bf16[4,2,128,128]{3,2,1,0:T(8,128)(2,1)} custom-call(bf16[4,128,128]{2,1,0:T(8,128)(2,1)S(1)} %get-tuple-element.26.own_ref, bf16[4,128,128]{2,1,0:T(8,128)(2,1)S(1)} %collective-permute-done.6.got_ref), custom_call_target="tpu_custom_call" | custom-call | bytes 524288 | tf_op jit(solution)/shard_map/join/pallas_call | solution.py:332
  16.8 3.4 %all-to-all-start = ((bf16[4,2,128,128]{3,2,1,0:T(8,128)(2,1)}), bf16[4,2,128,128]{3,2,1,0:T(8,128)(2,1)S(1)}, u32[]{:S(2)}, u32[]{:S(2)}) async-start(bf16[4,2,128,128]{3,2,1,0:T(8,128)(2,1)} %join.1), calls=%async_computation | async-start | bytes 524288 | tf_op jit(solution)/shard_map/all_to_all | solution.py:437
  20.2 0.0 collective-permute-done.4.right_ref
  20.3 1.7 %collective-permute-start.5 = (bf16[64,1024]{1,0:T(8,128)(2,1)S(1)}, bf16[64,1024]{1,0:T(8,128)(2,1)S(1)}, u32[]{:S(2)}, u32[]{:S(2)}) collective-permute-start(bf16[64,1024]{1,0:T(8,128)(2,1)S(1)} %pair_sum.1.left_ref), channel_id=1, source_target_pairs={{0,8},{1,17},{2,10},{3,19},{4,12},{5,21},{6,14},{7,23},{8,0},{9,25... | collective-permute-start | bytes 393224 | tf_op jit(solution)/shard_map/ppermute | solution.py:442
  22.0 3.9 %collective-permute-done.5.right_ref = bf16[64,1024]{1,0:T(8,128)(2,1)S(1)} collective-permute-done((bf16[64,1024]{1,0:T(8,128)(2,1)S(1)}, bf16[64,1024]{1,0:T(8,128)(2,1)S(1)}, u32[]{:S(2)}, u32[]{:S(2)}) %collective-permute-start.5) | collective-permute-done | bytes 131104 | tf_op jit(solution)/shard_map/ppermute | solution.py:442
  25.9 0.0 all-to-all-done.back_ref
  25.9 1.0 %finish.1 = (bf16[1,128,512]{2,1,0:T(8,128)(2,1)}, bf16[1,128,512]{2,1,0:T(8,128)(2,1)}, f32[64,1024]{1,0:T(8,128)}) custom-call(bf16[64,1024]{1,0:T(8,128)(2,1)S(1)} %pair_sum.1.left_ref, bf16[64,1024]{1,0:T(8,128)(2,1)S(1)} %collective-permute-done.5.right_ref, bf16[4,2,128,128]{3,2,1,0:T(8,128)(2,1)S(1)} %all-to-all-done.back_ref, ...), custom_call_target="tpu_custom_call" | custom-call | bytes 1179648 | tf_op jit(solution)/shard_map/finish/pallas_call | solution.py:332
  (2 shorter events, 0.1 us)
Async XLA Ops:
  1.8 1.5 %collective-permute-start = (bf16[4,128,128]{2,1,0:T(8,128)(2,1)S(1)}, bf16[4,128,128]{2,1,0:T(8,128)(2,1)S(1)}, u32[]{:S(2)}, u32[]{:S(2)}) collective-permute-start(bf16[4,128,128]{2,1,0:T(8,128)(2,1)S(1)} %get-tuple-element.17), channel_id=1, source_target_pairs={{0,1},{1,0},{2,3},{3,2},{4,5},{5,4},{6,7},{7,6},{8,9},{9,8},{10,11... | collective-permute-start | bytes 393224 | tf_op jit(solution)/shard_map/ppermute | solution.py:350
  3.3 6.8 %collective-permute-start.1 = (bf16[2,128,128]{2,1,0:T(8,128)(2,1)S(1)}, bf16[2,128,128]{2,1,0:T(8,128)(2,1)S(1)}, u32[]{:S(2)}, u32[]{:S(2)}) collective-permute-start(bf16[2,128,128]{2,1,0:T(8,128)(2,1)S(1)} %get-tuple-element.18), channel_id=1, source_target_pairs={{0,6},{1,7},{2,4},{3,5},{4,2},{5,3},{6,0},{7,1},{8,14},{9,15},{10,... | collective-permute-start | bytes 196616 | tf_op jit(solution)/shard_map/ppermute | solution.py:360
  7.2 4.3 %collective-permute-start.2 = (bf16[2,128,128]{2,1,0:T(8,128)(2,1)S(1)}, bf16[2,128,128]{2,1,0:T(8,128)(2,1)S(1)}, u32[]{:S(2)}, u32[]{:S(2)}) collective-permute-start(bf16[2,128,128]{2,1,0:T(8,128)(2,1)S(1)} %get-tuple-element.19), channel_id=1, source_target_pairs={{0,4},{1,5},{2,6},{3,7},{4,0},{5,1},{6,2},{7,3},{8,12},{9,13},{10,... | collective-permute-start | bytes 196616 | tf_op jit(solution)/shard_map/ppermute | solution.py:360
  7.7 0.7 %copy-start = (f32[64]{0:T(128)S(1)}, f32[64]{0:T(128)}, u32[]{:S(2)}) copy-start(f32[64]{0:T(128)} %param.11) | copy-start | bytes 772
  7.7 4.3 %collective-permute-start.3 = (bf16[2,128,128]{2,1,0:T(8,128)(2,1)S(1)}, bf16[2,128,128]{2,1,0:T(8,128)(2,1)S(1)}, u32[]{:S(2)}, u32[]{:S(2)}) collective-permute-start(bf16[2,128,128]{2,1,0:T(8,128)(2,1)S(1)} %get-tuple-element.20), channel_id=1, source_target_pairs={{0,2},{1,3},{2,0},{3,1},{4,6},{5,7},{6,4},{7,5},{8,10},{9,11},{10,... | collective-permute-start | bytes 196616 | tf_op jit(solution)/shard_map/ppermute | solution.py:360
  13.3 2.7 %collective-permute-start.6 = (bf16[4,128,128]{2,1,0:T(8,128)(2,1)S(1)}, bf16[4,128,128]{2,1,0:T(8,128)(2,1)S(1)}, u32[]{:S(2)}, u32[]{:S(2)}) collective-permute-start(bf16[4,128,128]{2,1,0:T(8,128)(2,1)S(1)} %get-tuple-element.27), channel_id=1, source_target_pairs={{0,1},{1,0},{2,3},{3,2},{4,5},{5,4},{6,7},{7,6},{8,9},{9,8},{10,11... | collective-permute-start | bytes 393224 | tf_op jit(solution)/shard_map/ppermute | solution.py:427
  13.4 6.8 %collective-permute-start.4 = (bf16[64,1024]{1,0:T(8,128)(2,1)S(1)}, bf16[64,1024]{1,0:T(8,128)(2,1)S(1)}, u32[]{:S(2)}, u32[]{:S(2)}) collective-permute-start(bf16[64,1024]{1,0:T(8,128)(2,1)S(1)} %get-tuple-element.25.left_ref), channel_id=1, source_target_pairs={{0,16},{1,9},{2,18},{3,11},{4,20},{5,13},{6,22},{7,15},{8,24},{9,1... | collective-permute-start | bytes 393224 | tf_op jit(solution)/shard_map/ppermute | solution.py:442
  16.8 9.1 %all-to-all-start = ((bf16[4,2,128,128]{3,2,1,0:T(8,128)(2,1)}), bf16[4,2,128,128]{3,2,1,0:T(8,128)(2,1)S(1)}, u32[]{:S(2)}, u32[]{:S(2)}) async-start(bf16[4,2,128,128]{3,2,1,0:T(8,128)(2,1)} %join.1), calls=%async_computation | async-start | bytes 524288 | tf_op jit(solution)/shard_map/all_to_all | solution.py:437
  20.3 5.6 %collective-permute-start.5 = (bf16[64,1024]{1,0:T(8,128)(2,1)S(1)}, bf16[64,1024]{1,0:T(8,128)(2,1)S(1)}, u32[]{:S(2)}, u32[]{:S(2)}) collective-permute-start(bf16[64,1024]{1,0:T(8,128)(2,1)S(1)} %pair_sum.1.left_ref), channel_id=1, source_target_pairs={{0,8},{1,17},{2,10},{3,19},{4,12},{5,21},{6,14},{7,23},{8,0},{9,25... | collective-permute-start | bytes 393224 | tf_op jit(solution)/shard_map/ppermute | solution.py:442

commit v5 on v4

--- a/solution.py
+++ b/solution.py
@@ -122,9 +122,12 @@
 
 def dense_tables(half):
     n = np.arange(half, dtype=np.int64)[:, None]
-    k = np.concatenate([np.arange(0, half, 2), np.arange(1, half, 2)])[None, :]
-    angle = ((2 * k + 1) * n % (4 * half)).astype(np.float64) * (math.pi / (2 * half))
-    full = np.concatenate([np.cos(angle), -np.sin(angle)], axis=1).astype(BF16)
+    columns = []
+    for first in range(2):
+        k = np.arange(first, half, 2)[None, :]
+        angle = ((2 * k + 1) * n % (4 * half)).astype(np.float64) * (math.pi / (2 * half))
+        columns += [np.cos(angle), -np.sin(angle)]
+    full = np.concatenate(columns, axis=1).astype(BF16)
     return full, np.ascontiguousarray(full.T)
 
 
@@ -187,10 +190,6 @@
 def join_kernel(own_ref, got_ref, out_ref):
     out_ref[:, 0] = own_ref[...]
     out_ref[:, 1] = got_ref[...]
-
-
-def arrived(own_ref, got_ref, *pair_refs):
-    return lambda f, d: pair_refs[-d][f] if d else (got_ref if f else own_ref)[0]
 
 
 def filter_kernel(
@@ -237,61 +236,50 @@
     parts, rows, pos = block_ref.shape
     chans = rows // 2
     half = parts // 2 * pos
-    block = arrived(*refs[: pairs + 1])
     for f, d, at in places(parts):
-        block_ref[at] = block(f, d)
+        block_ref[at] = refs[pairs + 1 - d][f] if d else refs[f][0]
     x = [
-        jnp.concatenate([block_ref[s] for s in range(parts // 2)], axis=1),
-        jnp.concatenate([block_ref[s] for s in range(parts // 2, parts)], axis=1),
+        jnp.concatenate([block_ref[s] for s in range(i, i + parts // 2)], axis=1)
+        for i in (0, parts // 2)
     ]
-    spec_ref[...] = jnp.dot(
-        jnp.concatenate(x, axis=0), fwd_ref[...], preferred_element_type=F32
-    )
-    inv = inv_ref[...]
+    signals = jnp.concatenate(x, axis=0)
+    res = 0.0
+    for odd in range(2):
+        bins = slice(odd * half, (odd + 1) * half)
+        spec_ref[odd] = jnp.dot(signals, fwd_ref[:, bins], preferred_element_type=F32)
+        for r in range(0, chans, 16):
+            for c in range(0, half // 2, 128):
+
+                def load(ref, row, col):
+                    at = slice(row * chans + r, row * chans + r + 16)
+                    return [ref[at, i + c : i + c + 128] for i in (col, col + half // 2)]
+
+                v0, g0, v1, g1 = [load(spec_ref.at[odd], i, 0) for i in range(4)]
+                h0, h1 = [load(filt_ref, i, odd * half) for i in range(2)]
+                conv0 = mul(h0, v0)
+                conv1 = add(add(mul(h0, v1), mul(h1, v0)), later(conv0, odd))
+                corr1 = conj_mul(h0, g1)
+                corr0 = add(add(conj_mul(h0, g0), conj_mul(h1, g1)), later(corr1, not odd))
+                cross1 = conj_mul(v0, g1)
+                cross0 = add(add(conj_mul(v0, g0), conj_mul(v1, g1)), later(cross1, not odd))
+                for i, parts_of in enumerate((conv0, corr0, cross0, conv1, corr1, cross1)):
+                    at = slice(i * chans + r, i * chans + r + 16)
+                    for col, part in zip((c, c + half // 2), parts_of):
+                        prod_ref[odd, at, col : col + 128] = part.astype(BF16)
+        res = res + jnp.dot(prod_ref[odd], inv_ref[bins, :], preferred_element_type=F32)
     gains = jnp.concatenate([gain_ref[...]] * (half // 128), axis=1)
     scale = (2 * half) ** -0.5 / half
-
-    def products(count, terms):
-        for r in range(0, chans, 16):
-            for c in range(0, half, 128):
-
-                def load(ref, row):
-                    at = slice(row * chans + r, row * chans + r + 16)
-                    return (ref[at, c : c + 128], ref[at, half + c : half + c + 128])
-
-                for i, (re, im) in enumerate(terms(load, c >= half // 2)):
-                    at = slice(i * chans + r, i * chans + r + 16)
-                    prod_ref[at, c : c + 128] = re.astype(BF16)
-                    prod_ref[at, half + c : half + c + 128] = im.astype(BF16)
-        return jnp.dot(prod_ref[: count * chans], inv, preferred_element_type=F32)
-
-    def with_filter(load, odd):
-        v0, g0, v1, g1 = [load(spec_ref, i) for i in range(4)]
-        h0, h1 = [load(filt_ref, i) for i in range(2)]
-        conv0 = mul(h0, v0)
-        conv1 = add(add(mul(h0, v1), mul(h1, v0)), later(conv0, odd))
-        corr1 = conj_mul(h0, g1)
-        corr0 = add(add(conj_mul(h0, g0), conj_mul(h1, g1)), later(corr1, not odd))
-        return (conv0, corr0, conv1, corr1)
-
-    def with_values(load, odd):
-        v0, g0, v1, g1 = [load(spec_ref, i) for i in range(4)]
-        cross1 = conj_mul(v0, g1)
-        cross0 = add(add(conj_mul(v0, g0), conj_mul(v1, g1)), later(cross1, not odd))
-        return (cross0, cross1)
-
-    res = products(4, with_filter) * scale
     for i in range(2):
-        both = (res[i * rows : (i + 1) * rows] + gains * x[i].astype(F32)).astype(BF16)
+        top = i * 3 * chans
+        both = (res[top : top + rows] * scale + gains * x[i].astype(F32)).astype(BF16)
         for s in range(parts // 2):
             block_ref[i * (parts // 2) + s] = both[:, s * pos : (s + 1) * pos]
+        cross = res[top + rows : top + rows + chans] * (1.0 / half)
+        cross_ref[:, i * half : (i + 1) * half] = cross.astype(BF16)
     core = lax.axis_index("ctx") % 2
     for p in range(pairs):
         own_ref[p] = block_ref[2 * p + core]
         sib_ref[p] = block_ref[2 * p + 1 - core]
-    res = products(2, with_values) * (1.0 / half)
-    for i in range(2):
-        cross_ref[:, i * half : (i + 1) * half] = res[i * chans : (i + 1) * chans].astype(BF16)
 
 
 def pair_kernel(left_ref, right_ref, out_ref):
@@ -417,8 +405,8 @@
         tuple(in_vmem(x) for x in held + [fwd_near, inv_near, spec, gains]),
         vmem_specs(pairs + 5),
         scratch=[
-            ((2 * rows, length), F32),
-            ((2 * rows, length), BF16),
+            ((2, 2 * rows, length // 2), F32),
+            ((2, 3 * rows, length // 2), BF16),
             ((parts, rows, pos), BF16),
         ],
         flops=10 * chans * length * length,

time: 27.2 us -> 27 us (level)
  no operation moved by 1% of the time
where the time goes in v5:
time: 27 us; the launch traced here: 26.8 us
  starting transfers between devices  12.9 us (48%)
  waiting for transfers between devices  6.7 us (25%)
  Pallas kernels  5.93 us (22%)
  between operations  0.7 us (3%)
  local copies, waits for them, and re-layouts  0.52 us (2%)
    pallas_call x7, Pallas kernels, call(): pl.pallas_call(kernel, out_shape=tuple((pltpu.VMEM(shape, dtype) if near...  5.93 us
    ppermute x3, starting transfers between devices, exchange(): lax.ppermute(sent[d - 1], 'ctx', [(j, j ^ 2 * d) for j in range(2 * pairs)])  4.51 us
    ppermute x2, starting transfers between devices, per_device_short(): other = lax.ppermute(cross, ('dp', 'ctx'), dp_pairs(seqs, parts, step))  4.4 us
    ppermute x2, waiting for transfers between devices, per_device_short(): other = lax.ppermute(cross, ('dp', 'ctx'), dp_pairs(seqs, parts, step))  3.89 us
    all_to_all x1, starting transfers between devices, per_device_short(): lax.all_to_all(sent, 'ctx', split_axis=0, concat_axis=0, tiled=True, axis...  3.41 us
    ppermute x3, waiting for transfers between devices, exchange(): lax.ppermute(sent[d - 1], 'ctx', [(j, j ^ 2 * d) for j in range(2 * pairs)])  1.82 us
    ppermute x1, waiting for transfers between devices, exchange(): got = lax.ppermute(sib, 'ctx', [(j, j ^ 1) for j in range(2 * pairs)])  0.99 us
  transfers between devices with their start and end apart: 8, of which 4 were waited for; matrix products, arithmetic and copies ran while one was open for 0% of the time, Pallas kernels for 9%

profile of v5, /device:TPU:0, one launch (start us, length us, event | category | flops | bytes accessed | tf_op | source)
XLA Modules:
  0.0 26.8 jit_solution(13372363310333213315)
XLA Ops:
  0.6 1.2 %pack.1 = (bf16[4,128,128]{2,1,0:T(8,128)(2,1)S(1)}, bf16[4,128,128]{2,1,0:T(8,128)(2,1)S(1)}, bf16[1,128,512]{2,1,0:T(8,128)(2,1)S(1)}) custom-call(bf16[1,128,512]{2,1,0:T(8,128)(2,1)} %vals_hbm.1, bf16[1,128,512]{2,1,0:T(8,128)(2,1)} %gate_hbm.1, bf16[1,128,512]{2,1,0:T(8,128)(2,1)} %grad_hbm.1), custom_call_target="tpu_custom_call" | custom-call | bytes 524288 | tf_op jit(solution)/shard_map/pack/pallas_call | solution.py:320
  1.8 0.5 %collective-permute-start = (bf16[4,128,128]{2,1,0:T(8,128)(2,1)S(1)}, bf16[4,128,128]{2,1,0:T(8,128)(2,1)S(1)}, u32[]{:S(2)}, u32[]{:S(2)}) collective-permute-start(bf16[4,128,128]{2,1,0:T(8,128)(2,1)S(1)} %get-tuple-element.17), channel_id=1, source_target_pairs={{0,1},{1,0},{2,3},{3,2},{4,5},{5,4},{6,7},{7,6},{8,9},{9,8},{10,11... | collective-permute-start | bytes 393224 | tf_op jit(solution)/shard_map/ppermute | solution.py:338
  2.3 1.0 %collective-permute-done.got_ref.refs_1_ = bf16[4,128,128]{2,1,0:T(8,128)(2,1)S(1)} collective-permute-done((bf16[4,128,128]{2,1,0:T(8,128)(2,1)S(1)}, bf16[4,128,128]{2,1,0:T(8,128)(2,1)S(1)}, u32[]{:S(2)}, u32[]{:S(2)}) %collective-permute-start) | collective-permute-done | bytes 131104 | tf_op jit(solution)/shard_map/ppermute | solution.py:338
  3.3 3.9 %collective-permute-start.1 = (bf16[2,128,128]{2,1,0:T(8,128)(2,1)S(1)}, bf16[2,128,128]{2,1,0:T(8,128)(2,1)S(1)}, u32[]{:S(2)}, u32[]{:S(2)}) collective-permute-start(bf16[2,128,128]{2,1,0:T(8,128)(2,1)S(1)} %get-tuple-element.18), channel_id=1, source_target_pairs={{0,6},{1,7},{2,4},{3,5},{4,2},{5,3},{6,0},{7,1},{8,14},{9,15},{10,... | collective-permute-start | bytes 196616 | tf_op jit(solution)/shard_map/ppermute | solution.py:348
  7.2 0.5 %collective-permute-start.2 = (bf16[2,128,128]{2,1,0:T(8,128)(2,1)S(1)}, bf16[2,128,128]{2,1,0:T(8,128)(2,1)S(1)}, u32[]{:S(2)}, u32[]{:S(2)}) collective-permute-start(bf16[2,128,128]{2,1,0:T(8,128)(2,1)S(1)} %get-tuple-element.19), channel_id=1, source_target_pairs={{0,4},{1,5},{2,6},{3,7},{4,0},{5,1},{6,2},{7,3},{8,12},{9,13},{10,... | collective-permute-start | bytes 196616 | tf_op jit(solution)/shard_map/ppermute | solution.py:348
  7.7 0.0 copy-start
  7.7 0.1 collective-permute-start.3
  7.9 0.5 %copy-done = f32[64]{0:T(128)S(1)} copy-done((f32[64]{0:T(128)S(1)}, f32[64]{0:T(128)}, u32[]{:S(2)}) %copy-start) | copy-done | bytes 280
  8.4 1.8 %filter_spectrum.1 = (f32[128,1024]{1,0:T(8,128)S(1)}, bf16[512,1024]{1,0:T(8,128)(2,1)S(1)}, bf16[1024,512]{1,0:T(8,128)(2,1)S(1)}, f32[128,128]{1,0:T(8,128)S(1)}) custom-call(f32[64,1024]{1,0:T(8,128)} %filt_hbm.1, bf16[512,1024]{1,0:T(8,128)(2,1)} %constant.4.clone.fwd_hbm, bf16[1024,512]{1,0:T(8,128)(2,1)} %constant.5.clone.inv_hbm, f32[1,64]{1,0:T(1,128)S(1)} %bitcast.1), custom_call_target="tpu_custom_call" | custom-call | flops 268435456 | bytes 8388608 | tf_op jit(solution)/shard_map/filter_spectrum/pallas_call | solution.py:320
  10.2 0.0 collective-permute-done.1.refs_2_
  10.2 1.3 %collective-permute-done.2.refs_3_ = bf16[2,128,128]{2,1,0:T(8,128)(2,1)S(1)} collective-permute-done((bf16[2,128,128]{2,1,0:T(8,128)(2,1)S(1)}, bf16[2,128,128]{2,1,0:T(8,128)(2,1)S(1)}, u32[]{:S(2)}, u32[]{:S(2)}) %collective-permute-start.2) | collective-permute-done | bytes 65568 | tf_op jit(solution)/shard_map/ppermute | solution.py:348
  11.5 0.5 %collective-permute-done.3.refs_4_ = bf16[2,128,128]{2,1,0:T(8,128)(2,1)S(1)} collective-permute-done((bf16[2,128,128]{2,1,0:T(8,128)(2,1)S(1)}, bf16[2,128,128]{2,1,0:T(8,128)(2,1)S(1)}, u32[]{:S(2)}, u32[]{:S(2)}) %collective-permute-start.3) | collective-permute-done | bytes 65568 | tf_op jit(solution)/shard_map/ppermute | solution.py:348
  12.0 1.2 %products.1 = (bf16[4,128,128]{2,1,0:T(8,128)(2,1)S(1)}, bf16[4,128,128]{2,1,0:T(8,128)(2,1)S(1)}, bf16[64,1024]{1,0:T(8,128)(2,1)S(1)}) custom-call(bf16[4,128,128]{2,1,0:T(8,128)(2,1)S(1)} %get-tuple-element.16.own_ref.refs_0_, bf16[4,128,128]{2,1,0:T(8,128)(2,1)S(1)} %collective-permute-done.got_ref.refs_1_, ...), custom_call_target="tpu_custom_call" | custom-call | flops 671088640 | bytes 8388608 | tf_op jit(solution)/shard_map/products/pallas_call | solution.py:320
  13.2 0.1 collective-permute-start.6
  13.3 2.7 %collective-permute-start.4 = (bf16[64,1024]{1,0:T(8,128)(2,1)S(1)}, bf16[64,1024]{1,0:T(8,128)(2,1)S(1)}, u32[]{:S(2)}, u32[]{:S(2)}) collective-permute-start(bf16[64,1024]{1,0:T(8,128)(2,1)S(1)} %get-tuple-element.25.left_ref), channel_id=1, source_target_pairs={{0,16},{1,9},{2,18},{3,11},{4,20},{5,13},{6,22},{7,15},{8,24},{9,1... | collective-permute-start | bytes 393224 | tf_op jit(solution)/shard_map/ppermute | solution.py:430
  15.9 0.0 collective-permute-done.6.got_ref
  15.9 0.7 %join.1 = bf16[4,2,128,128]{3,2,1,0:T(8,128)(2,1)} custom-call(bf16[4,128,128]{2,1,0:T(8,128)(2,1)S(1)} %get-tuple-element.26.own_ref, bf16[4,128,128]{2,1,0:T(8,128)(2,1)S(1)} %collective-permute-done.6.got_ref), custom_call_target="tpu_custom_call" | custom-call | bytes 524288 | tf_op jit(solution)/shard_map/join/pallas_call | solution.py:320
  16.7 3.4 %all-to-all-start = ((bf16[4,2,128,128]{3,2,1,0:T(8,128)(2,1)}), bf16[4,2,128,128]{3,2,1,0:T(8,128)(2,1)S(1)}, u32[]{:S(2)}, u32[]{:S(2)}) async-start(bf16[4,2,128,128]{3,2,1,0:T(8,128)(2,1)} %join.1), calls=%async_computation | async-start | bytes 524288 | tf_op jit(solution)/shard_map/all_to_all | solution.py:425
  20.1 0.0 collective-permute-done.4.right_ref
  20.1 1.7 %collective-permute-start.5 = (bf16[64,1024]{1,0:T(8,128)(2,1)S(1)}, bf16[64,1024]{1,0:T(8,128)(2,1)S(1)}, u32[]{:S(2)}, u32[]{:S(2)}) collective-permute-start(bf16[64,1024]{1,0:T(8,128)(2,1)S(1)} %pair_sum.1.left_ref), channel_id=1, source_target_pairs={{0,8},{1,17},{2,10},{3,19},{4,12},{5,21},{6,14},{7,23},{8,0},{9,25... | collective-permute-start | bytes 393224 | tf_op jit(solution)/shard_map/ppermute | solution.py:430
  21.9 3.9 %collective-permute-done.5.right_ref = bf16[64,1024]{1,0:T(8,128)(2,1)S(1)} collective-permute-done((bf16[64,1024]{1,0:T(8,128)(2,1)S(1)}, bf16[64,1024]{1,0:T(8,128)(2,1)S(1)}, u32[]{:S(2)}, u32[]{:S(2)}) %collective-permute-start.5) | collective-permute-done | bytes 131104 | tf_op jit(solution)/shard_map/ppermute | solution.py:430
  25.8 0.0 all-to-all-done.back_ref
  25.8 1.0 %finish.1 = (bf16[1,128,512]{2,1,0:T(8,128)(2,1)}, bf16[1,128,512]{2,1,0:T(8,128)(2,1)}, f32[64,1024]{1,0:T(8,128)}) custom-call(bf16[64,1024]{1,0:T(8,128)(2,1)S(1)} %pair_sum.1.left_ref, bf16[64,1024]{1,0:T(8,128)(2,1)S(1)} %collective-permute-done.5.right_ref, bf16[4,2,128,128]{3,2,1,0:T(8,128)(2,1)S(1)} %all-to-all-done.back_ref, ...), custom_call_target="tpu_custom_call" | custom-call | bytes 1179648 | tf_op jit(solution)/shard_map/finish/pallas_call | solution.py:320
  (2 shorter events, 0.0 us)
Async XLA Ops:
  1.8 1.5 %collective-permute-start = (bf16[4,128,128]{2,1,0:T(8,128)(2,1)S(1)}, bf16[4,128,128]{2,1,0:T(8,128)(2,1)S(1)}, u32[]{:S(2)}, u32[]{:S(2)}) collective-permute-start(bf16[4,128,128]{2,1,0:T(8,128)(2,1)S(1)} %get-tuple-element.17), channel_id=1, source_target_pairs={{0,1},{1,0},{2,3},{3,2},{4,5},{5,4},{6,7},{7,6},{8,9},{9,8},{10,11... | collective-permute-start | bytes 393224 | tf_op jit(solution)/shard_map/ppermute | solution.py:338
  3.3 6.8 %collective-permute-start.1 = (bf16[2,128,128]{2,1,0:T(8,128)(2,1)S(1)}, bf16[2,128,128]{2,1,0:T(8,128)(2,1)S(1)}, u32[]{:S(2)}, u32[]{:S(2)}) collective-permute-start(bf16[2,128,128]{2,1,0:T(8,128)(2,1)S(1)} %get-tuple-element.18), channel_id=1, source_target_pairs={{0,6},{1,7},{2,4},{3,5},{4,2},{5,3},{6,0},{7,1},{8,14},{9,15},{10,... | collective-permute-start | bytes 196616 | tf_op jit(solution)/shard_map/ppermute | solution.py:348
  7.2 4.3 %collective-permute-start.2 = (bf16[2,128,128]{2,1,0:T(8,128)(2,1)S(1)}, bf16[2,128,128]{2,1,0:T(8,128)(2,1)S(1)}, u32[]{:S(2)}, u32[]{:S(2)}) collective-permute-start(bf16[2,128,128]{2,1,0:T(8,128)(2,1)S(1)} %get-tuple-element.19), channel_id=1, source_target_pairs={{0,4},{1,5},{2,6},{3,7},{4,0},{5,1},{6,2},{7,3},{8,12},{9,13},{10,... | collective-permute-start | bytes 196616 | tf_op jit(solution)/shard_map/ppermute | solution.py:348
  7.7 0.7 %copy-start = (f32[64]{0:T(128)S(1)}, f32[64]{0:T(128)}, u32[]{:S(2)}) copy-start(f32[64]{0:T(128)} %param.11) | copy-start | bytes 772
  7.7 4.3 %collective-permute-start.3 = (bf16[2,128,128]{2,1,0:T(8,128)(2,1)S(1)}, bf16[2,128,128]{2,1,0:T(8,128)(2,1)S(1)}, u32[]{:S(2)}, u32[]{:S(2)}) collective-permute-start(bf16[2,128,128]{2,1,0:T(8,128)(2,1)S(1)} %get-tuple-element.20), channel_id=1, source_target_pairs={{0,2},{1,3},{2,0},{3,1},{4,6},{5,7},{6,4},{7,5},{8,10},{9,11},{10,... | collective-permute-start | bytes 196616 | tf_op jit(solution)/shard_map/ppermute | solution.py:348
  13.2 2.7 %collective-permute-start.6 = (bf16[4,128,128]{2,1,0:T(8,128)(2,1)S(1)}, bf16[4,128,128]{2,1,0:T(8,128)(2,1)S(1)}, u32[]{:S(2)}, u32[]{:S(2)}) collective-permute-start(bf16[4,128,128]{2,1,0:T(8,128)(2,1)S(1)} %get-tuple-element.27), channel_id=1, source_target_pairs={{0,1},{1,0},{2,3},{3,2},{4,5},{5,4},{6,7},{7,6},{8,9},{9,8},{10,11... | collective-permute-start | bytes 393224 | tf_op jit(solution)/shard_map/ppermute | solution.py:415
  13.3 6.8 %collective-permute-start.4 = (bf16[64,1024]{1,0:T(8,128)(2,1)S(1)}, bf16[64,1024]{1,0:T(8,128)(2,1)S(1)}, u32[]{:S(2)}, u32[]{:S(2)}) collective-permute-start(bf16[64,1024]{1,0:T(8,128)(2,1)S(1)} %get-tuple-element.25.left_ref), channel_id=1, source_target_pairs={{0,16},{1,9},{2,18},{3,11},{4,20},{5,13},{6,22},{7,15},{8,24},{9,1... | collective-permute-start | bytes 393224 | tf_op jit(solution)/shard_map/ppermute | solution.py:430
  16.7 9.1 %all-to-all-start = ((bf16[4,2,128,128]{3,2,1,0:T(8,128)(2,1)}), bf16[4,2,128,128]{3,2,1,0:T(8,128)(2,1)S(1)}, u32[]{:S(2)}, u32[]{:S(2)}) async-start(bf16[4,2,128,128]{3,2,1,0:T(8,128)(2,1)} %join.1), calls=%async_computation | async-start | bytes 524288 | tf_op jit(solution)/shard_map/all_to_all | solution.py:425
  20.1 5.6 %collective-permute-start.5 = (bf16[64,1024]{1,0:T(8,128)(2,1)S(1)}, bf16[64,1024]{1,0:T(8,128)(2,1)S(1)}, u32[]{:S(2)}, u32[]{:S(2)}) collective-permute-start(bf16[64,1024]{1,0:T(8,128)(2,1)S(1)} %pair_sum.1.left_ref), channel_id=1, source_target_pairs={{0,8},{1,17},{2,10},{3,19},{4,12},{5,21},{6,14},{7,23},{8,0},{9,25... | collective-permute-start | bytes 393224 | tf_op jit(solution)/shard_map/ppermute | solution.py:430

commit v6 on v5

--- a/solution.py
+++ b/solution.py
@@ -14,6 +14,7 @@
 F32 = jnp.float32
 DENSE_LIMIT = 1024
 VMEM_BYTES = 16 * 2**20
+UNPACK_COST = 5 * 10**9
 
 
 def twiddle(rows, cols, period):
@@ -185,11 +186,6 @@
     for d, out_ref in enumerate(out_refs, 1):
         out_ref[0] = own_ref[d]
         out_ref[1] = got_ref[d]
-
-
-def join_kernel(own_ref, got_ref, out_ref):
-    out_ref[:, 0] = own_ref[...]
-    out_ref[:, 1] = got_ref[...]
 
 
 def filter_kernel(
@@ -276,42 +272,38 @@
             block_ref[i * (parts // 2) + s] = both[:, s * pos : (s + 1) * pos]
         cross = res[top + rows : top + rows + chans] * (1.0 / half)
         cross_ref[:, i * half : (i + 1) * half] = cross.astype(BF16)
-    core = lax.axis_index("ctx") % 2
-    for p in range(pairs):
-        own_ref[p] = block_ref[2 * p + core]
-        sib_ref[p] = block_ref[2 * p + 1 - core]
+    for f, d, at in places(parts):
+        (sib_ref if f else own_ref)[d] = block_ref[at]
 
 
 def pair_kernel(left_ref, right_ref, out_ref):
     out_ref[...] = (left_ref[...].astype(F32) + right_ref[...].astype(F32)).astype(BF16)
 
 
-def finish_kernel(
-    scale,
-    left_ref,
-    right_ref,
-    back_ref,
-    near_ref,
-    val_hbm,
-    gate_hbm,
-    filt_hbm,
-    val_ref,
-    gate_ref,
-    filt_ref,
-    sems,
-):
-    pairs, _, rows, _ = back_ref.shape
-    chans = rows // 2
-    filt_ref[...] = (left_ref[...].astype(F32) + right_ref[...].astype(F32)) * scale
-    copies = start_copies([(filt_ref, filt_hbm)], sems)
-    core = lax.axis_index("ctx") % 2
-    both = [back_ref[p, (core + f) % 2] for p in range(pairs) for f in range(2)]
-    vals = jnp.concatenate([block[chans:] for block in both], axis=0)
-    val_ref[0] = vals.astype(F32).T.astype(BF16)
-    copies += start_copies([(val_ref, val_hbm)], sems.at[pl.ds(1, 1)])
-    conv = jnp.concatenate([block[:chans] for block in both], axis=0)
-    gate_ref[0] = (near_ref[0].astype(F32) * conv.astype(F32).T).astype(BF16)
-    copies += start_copies([(gate_ref, gate_hbm)], sems.at[pl.ds(2, 1)])
+def unpack_kernel(pairs, *refs):
+    near_ref, val_hbm, gate_hbm, val_ref, gate_ref, turn_ref, sems = refs[pairs + 1 :]
+    chans = turn_ref.shape[1] // (2 * pairs)
+    for f, d, at in places(2 * pairs):
+        at = pl.multiple_of(at * chans, chans)
+        both = refs[pairs + 1 - d][f] if d else refs[f][0]
+        turn_ref[0, pl.ds(at, chans), :] = both[:chans]
+        turn_ref[1, pl.ds(at, chans), :] = both[chans:]
+    val_ref[0] = turn_ref[1].astype(F32).T.astype(BF16)
+    copies = start_copies([(val_ref, val_hbm)], sems)
+    gate_ref[0] = (near_ref[0].astype(F32) * turn_ref[0].astype(F32).T).astype(BF16)
+    copies += start_copies([(gate_ref, gate_hbm)], sems.at[pl.ds(1, 1)])
+    for copy in copies:
+        copy.wait()
+
+
+def total_kernel(scale, left_ref, right_ref, _, out_hbm, out_ref, sems):
+    cuts = sems.shape[0]
+    each = out_ref.shape[0] // cuts
+    copies = []
+    for i in range(cuts):
+        at = pl.ds(i * each, each)
+        out_ref[at, :] = (left_ref[at, :].astype(F32) + right_ref[at, :].astype(F32)) * scale
+        copies += start_copies([(out_ref.at[at, :], out_hbm.at[at, :])], sems.at[pl.ds(i, 1)])
     for copy in copies:
         copy.wait()
 
@@ -352,12 +344,10 @@
 
 
 def dp_pairs(seqs, parts, step):
-    pairs = []
-    for s in range(seqs):
-        for c in range(parts):
-            other = s ^ (seqs // 2 // step if c % 2 else step)
-            pairs.append((s * parts + c, other * parts + c))
-    return pairs
+    masks = (step, 2 * (seqs // 2 // step) - 1)
+    return [
+        (s * parts + c, (s ^ masks[c % 2]) * parts + c) for s in range(seqs) for c in range(parts)
+    ]
 
 
 def per_device_short(values, gates, grad_out, filters, skip):
@@ -412,19 +402,7 @@
         flops=10 * chans * length * length,
         moved=8 * length * length,
     )
-    got = lax.ppermute(sib, "ctx", [(j, j ^ 1) for j in range(parts)])
-    (sent,) = call(
-        join_kernel,
-        "join",
-        [((pairs, 2, rows, pos), BF16, True)],
-        (in_vmem(own), in_vmem(got)),
-        vmem_specs(2),
-        moved=8 * pairs * rows * pos,
-    )
-    cores = [list(range(f, parts, 2)) for f in range(2)]
-    home = lax.all_to_all(
-        sent, "ctx", split_axis=0, concat_axis=0, tiled=True, axis_index_groups=cores
-    )
+    home = exchange(own, sib, "home")
     step = seqs // 2
     while step:
         other = lax.ppermute(cross, ("dp", "ctx"), dp_pairs(seqs, parts, step))
@@ -438,15 +416,26 @@
                 vmem_specs(2),
                 moved=6 * chans * length,
             )
-    grad_values, grad_gates, grad_filters = call(
-        functools.partial(finish_kernel, (seqs * length) ** (-0.5)),
-        "finish",
-        [(*token, False), (*token, False), ((chans, length), F32, False)],
-        tuple(in_vmem(x) for x in (cross, other, home, grad_near)),
-        vmem_specs(4),
-        scratch=[token, token, ((chans, length), F32)],
-        sems=3,
-        moved=10 * pos * width + 8 * chans * length,
+    grad_values, grad_gates = call(
+        functools.partial(unpack_kernel, pairs),
+        "unpack",
+        [(*token, False), (*token, False)],
+        tuple(in_vmem(x) for x in home + [grad_near]),
+        vmem_specs(pairs + 2),
+        scratch=[token, token, turned],
+        sems=2,
+        flops=UNPACK_COST,
+        moved=10 * pos * width,
+    )
+    (grad_filters,) = call(
+        functools.partial(total_kernel, (seqs * length) ** (-0.5)),
+        "total",
+        [((chans, length), F32, False)],
+        (in_vmem(cross), in_vmem(other), in_hbm(grad_gates)),
+        vmem_specs(2) + hbm_specs(1),
+        scratch=[((chans, length), F32)],
+        sems=4,
+        moved=8 * chans * length,
     )
     return (grad_values, grad_gates, grad_filters)
 

time: 27 us -> 26.1 us (0.967)
  waiting for transfers between devices: 6.7 us -> 5.45 us
  starting transfers between devices: 12.9 us -> 13.5 us
    ppermute x3 -> x6, starting transfers between devices: 4.51 us -> 8.06 us  [exchange(): lax.ppermute(sent[d - 1], 'ctx', [(j, j ^ 2 * d) for j in range(2 * pairs)])]
    all_to_all x1 -> x0, starting transfers between devices: 3.41 us -> none  [per_device_short(): lax.all_to_all(sent, 'ctx', split_axis=0, concat_axis=0, tiled=True, axis...]
    ppermute x2, waiting for transfers between devices: 3.89 us -> 1.99 us  [per_device_short(): other = lax.ppermute(cross, ('dp', 'ctx'), dp_pairs(seqs, parts, step))]
    ppermute x3 -> x6, waiting for transfers between devices: 1.82 us -> 2.47 us  [exchange(): lax.ppermute(sent[d - 1], 'ctx', [(j, j ^ 2 * d) for j in range(2 * pairs)])]
    ppermute x2, starting transfers between devices: 4.4 us -> 4.8 us  [per_device_short(): other = lax.ppermute(cross, ('dp', 'ctx'), dp_pairs(seqs, parts, step))]
    pallas_call x7 -> x8, Pallas kernels: 5.93 us -> 5.78 us  [call(): pl.pallas_call(kernel, out_shape=tuple((pltpu.VMEM(shape, dtype) if near...]
    ppermute x1 -> x2, starting transfers between devices: 0.52 us -> 0.59 us  [exchange(): got = lax.ppermute(sib, 'ctx', [(j, j ^ 1) for j in range(2 * pairs)])]
    ppermute x1 -> x2, waiting for transfers between devices: 0.99 us -> 0.99 us  [exchange(): got = lax.ppermute(sib, 'ctx', [(j, j ^ 1) for j in range(2 * pairs)])]
  transfers between devices with their start and end apart: 8 -> 10, of which waited for: 4 -> 7; matrix products, arithmetic and copies ran while one was open for 0% -> 0% of each run, Pallas kernels for 9% -> 10%
where the time goes in v6:
time: 26.1 us; the launch traced here: 25.9 us
  starting transfers between devices  13.5 us (52%)
  Pallas kernels  5.78 us (22%)
  waiting for transfers between devices  5.45 us (21%)
  between operations  0.7 us (3%)
  local copies, waits for them, and re-layouts  0.52 us (2%)
    ppermute x6, starting transfers between devices, exchange(): lax.ppermute(sent[d - 1], 'ctx', [(j, j ^ 2 * d) for j in range(2 * pairs)])  8.06 us
    pallas_call x8, Pallas kernels, call(): pl.pallas_call(kernel, out_shape=tuple((pltpu.VMEM(shape, dtype) if near...  5.78 us
    ppermute x2, starting transfers between devices, per_device_short(): other = lax.ppermute(cross, ('dp', 'ctx'), dp_pairs(seqs, parts, step))  4.8 us
    ppermute x6, waiting for transfers between devices, exchange(): lax.ppermute(sent[d - 1], 'ctx', [(j, j ^ 2 * d) for j in range(2 * pairs)])  2.47 us
    ppermute x2, waiting for transfers between devices, per_device_short(): other = lax.ppermute(cross, ('dp', 'ctx'), dp_pairs(seqs, parts, step))  1.99 us
    ppermute x2, waiting for transfers between devices, exchange(): got = lax.ppermute(sib, 'ctx', [(j, j ^ 1) for j in range(2 * pairs)])  0.99 us
    ppermute x2, starting transfers between devices, exchange(): got = lax.ppermute(sib, 'ctx', [(j, j ^ 1) for j in range(2 * pairs)])  0.59 us
  transfers between devices with their start and end apart: 10, of which 7 were waited for; matrix products, arithmetic and copies ran while one was open for 0% of the time, Pallas kernels for 10%

profile of v6, /device:TPU:0, one launch (start us, length us, event | category | flops | bytes accessed | tf_op | source)
XLA Modules:
  0.0 25.9 jit_solution(925155090402405926)
XLA Ops:
  0.6 1.2 %pack.1 = (bf16[4,128,128]{2,1,0:T(8,128)(2,1)S(1)}, bf16[4,128,128]{2,1,0:T(8,128)(2,1)S(1)}, bf16[1,128,512]{2,1,0:T(8,128)(2,1)S(1)}) custom-call(bf16[1,128,512]{2,1,0:T(8,128)(2,1)} %vals_hbm.1, bf16[1,128,512]{2,1,0:T(8,128)(2,1)} %gate_hbm.1, bf16[1,128,512]{2,1,0:T(8,128)(2,1)} %grad_hbm.1), custom_call_target="tpu_custom_call" | custom-call | bytes 524288 | tf_op jit(solution)/shard_map/pack/pallas_call | solution.py:312
  1.8 0.5 %collective-permute-start = (bf16[4,128,128]{2,1,0:T(8,128)(2,1)S(1)}, bf16[4,128,128]{2,1,0:T(8,128)(2,1)S(1)}, u32[]{:S(2)}, u32[]{:S(2)}) collective-permute-start(bf16[4,128,128]{2,1,0:T(8,128)(2,1)S(1)} %get-tuple-element.22), channel_id=1, source_target_pairs={{0,1},{1,0},{2,3},{3,2},{4,5},{5,4},{6,7},{7,6},{8,9},{9,8},{10,11... | collective-permute-start | bytes 393224 | tf_op jit(solution)/shard_map/ppermute | solution.py:330
  2.3 1.0 %collective-permute-done.got_ref.refs_1_ = bf16[4,128,128]{2,1,0:T(8,128)(2,1)S(1)} collective-permute-done((bf16[4,128,128]{2,1,0:T(8,128)(2,1)S(1)}, bf16[4,128,128]{2,1,0:T(8,128)(2,1)S(1)}, u32[]{:S(2)}, u32[]{:S(2)}) %collective-permute-start) | collective-permute-done | bytes 131104 | tf_op jit(solution)/shard_map/ppermute | solution.py:330
  3.3 3.9 %collective-permute-start.1 = (bf16[2,128,128]{2,1,0:T(8,128)(2,1)S(1)}, bf16[2,128,128]{2,1,0:T(8,128)(2,1)S(1)}, u32[]{:S(2)}, u32[]{:S(2)}) collective-permute-start(bf16[2,128,128]{2,1,0:T(8,128)(2,1)S(1)} %get-tuple-element.23), channel_id=1, source_target_pairs={{0,6},{1,7},{2,4},{3,5},{4,2},{5,3},{6,0},{7,1},{8,14},{9,15},{10,... | collective-permute-start | bytes 196616 | tf_op jit(solution)/shard_map/ppermute | solution.py:340
  7.2 0.5 %collective-permute-start.2 = (bf16[2,128,128]{2,1,0:T(8,128)(2,1)S(1)}, bf16[2,128,128]{2,1,0:T(8,128)(2,1)S(1)}, u32[]{:S(2)}, u32[]{:S(2)}) collective-permute-start(bf16[2,128,128]{2,1,0:T(8,128)(2,1)S(1)} %get-tuple-element.24), channel_id=1, source_target_pairs={{0,4},{1,5},{2,6},{3,7},{4,0},{5,1},{6,2},{7,3},{8,12},{9,13},{10,... | collective-permute-start | bytes 196616 | tf_op jit(solution)/shard_map/ppermute | solution.py:340
  7.7 0.1 collective-permute-start.3
  7.9 0.5 %copy-done = f32[64]{0:T(128)S(1)} copy-done((f32[64]{0:T(128)S(1)}, f32[64]{0:T(128)}, u32[]{:S(2)}) %copy-start) | copy-done | bytes 280
  8.4 1.8 %filter_spectrum.1 = (f32[128,1024]{1,0:T(8,128)S(1)}, bf16[512,1024]{1,0:T(8,128)(2,1)S(1)}, bf16[1024,512]{1,0:T(8,128)(2,1)S(1)}, f32[128,128]{1,0:T(8,128)S(1)}) custom-call(f32[64,1024]{1,0:T(8,128)} %filt_hbm.1, bf16[512,1024]{1,0:T(8,128)(2,1)} %constant.4.clone.fwd_hbm, bf16[1024,512]{1,0:T(8,128)(2,1)} %constant.5.clone.inv_hbm, f32[1,64]{1,0:T(1,128)S(1)} %bitcast.1), custom_call_target="tpu_custom_call" | custom-call | flops 268435456 | bytes 8388608 | tf_op jit(solution)/shard_map/filter_spectrum/pallas_call | solution.py:312
  10.2 1.3 %collective-permute-done.2.refs_3_ = bf16[2,128,128]{2,1,0:T(8,128)(2,1)S(1)} collective-permute-done((bf16[2,128,128]{2,1,0:T(8,128)(2,1)S(1)}, bf16[2,128,128]{2,1,0:T(8,128)(2,1)S(1)}, u32[]{:S(2)}, u32[]{:S(2)}) %collective-permute-start.2) | collective-permute-done | bytes 65568 | tf_op jit(solution)/shard_map/ppermute | solution.py:340
  11.5 0.5 %collective-permute-done.3.refs_4_ = bf16[2,128,128]{2,1,0:T(8,128)(2,1)S(1)} collective-permute-done((bf16[2,128,128]{2,1,0:T(8,128)(2,1)S(1)}, bf16[2,128,128]{2,1,0:T(8,128)(2,1)S(1)}, u32[]{:S(2)}, u32[]{:S(2)}) %collective-permute-start.3) | collective-permute-done | bytes 65568 | tf_op jit(solution)/shard_map/ppermute | solution.py:340
  12.0 1.2 %products.1 = (bf16[4,128,128]{2,1,0:T(8,128)(2,1)S(1)}, bf16[4,128,128]{2,1,0:T(8,128)(2,1)S(1)}, bf16[64,1024]{1,0:T(8,128)(2,1)S(1)}) custom-call(bf16[4,128,128]{2,1,0:T(8,128)(2,1)S(1)} %get-tuple-element.21.own_ref.refs_0_, bf16[4,128,128]{2,1,0:T(8,128)(2,1)S(1)} %collective-permute-done.got_ref.refs_1_, ...), custom_call_target="tpu_custom_call" | custom-call | flops 671088640 | bytes 8388608 | tf_op jit(solution)/shard_map/products/pallas_call | solution.py:312
  13.2 0.1 collective-permute-start.4
  13.2 2.7 %collective-permute-start.8 = (bf16[64,1024]{1,0:T(8,128)(2,1)S(1)}, bf16[64,1024]{1,0:T(8,128)(2,1)S(1)}, u32[]{:S(2)}, u32[]{:S(2)}) collective-permute-start(bf16[64,1024]{1,0:T(8,128)(2,1)S(1)} %get-tuple-element.38.left_ref), channel_id=1, source_target_pairs={{0,16},{1,9},{2,18},{3,11},{4,20},{5,13},{6,22},{7,15},{8,24},{9,1... | collective-permute-start | bytes 393224 | tf_op jit(solution)/shard_map/ppermute | solution.py:408
  15.9 0.0 collective-permute-done.4.got_ref.refs_1_
  15.9 1.6 %collective-permute-start.5 = (bf16[2,128,128]{2,1,0:T(8,128)(2,1)S(1)}, bf16[2,128,128]{2,1,0:T(8,128)(2,1)S(1)}, u32[]{:S(2)}, u32[]{:S(2)}) collective-permute-start(bf16[2,128,128]{2,1,0:T(8,128)(2,1)S(1)} %get-tuple-element.32), channel_id=1, source_target_pairs={{0,6},{1,7},{2,4},{3,5},{4,2},{5,3},{6,0},{7,1},{8,14},{9,15},{10,... | collective-permute-start | bytes 196616 | tf_op jit(solution)/shard_map/ppermute | solution.py:340
  17.5 0.7 %collective-permute-start.6 = (bf16[2,128,128]{2,1,0:T(8,128)(2,1)S(1)}, bf16[2,128,128]{2,1,0:T(8,128)(2,1)S(1)}, u32[]{:S(2)}, u32[]{:S(2)}) collective-permute-start(bf16[2,128,128]{2,1,0:T(8,128)(2,1)S(1)} %get-tuple-element.33), channel_id=1, source_target_pairs={{0,4},{1,5},{2,6},{3,7},{4,0},{5,1},{6,2},{7,3},{8,12},{9,13},{10,... | collective-permute-start | bytes 196616 | tf_op jit(solution)/shard_map/ppermute | solution.py:340
  18.2 1.3 %collective-permute-start.7 = (bf16[2,128,128]{2,1,0:T(8,128)(2,1)S(1)}, bf16[2,128,128]{2,1,0:T(8,128)(2,1)S(1)}, u32[]{:S(2)}, u32[]{:S(2)}) collective-permute-start(bf16[2,128,128]{2,1,0:T(8,128)(2,1)S(1)} %get-tuple-element.34), channel_id=1, source_target_pairs={{0,2},{1,3},{2,0},{3,1},{4,6},{5,7},{6,4},{7,5},{8,10},{9,11},{10,... | collective-permute-start | bytes 196616 | tf_op jit(solution)/shard_map/ppermute | solution.py:340
  19.5 0.2 collective-permute-done.8.right_ref
  19.7 2.1 %collective-permute-start.9 = (bf16[64,1024]{1,0:T(8,128)(2,1)S(1)}, bf16[64,1024]{1,0:T(8,128)(2,1)S(1)}, u32[]{:S(2)}, u32[]{:S(2)}) collective-permute-start(bf16[64,1024]{1,0:T(8,128)(2,1)S(1)} %pair_sum.1.left_ref), channel_id=1, source_target_pairs={{0,8},{1,25},{2,10},{3,27},{4,12},{5,29},{6,14},{7,31},{8,0},{9,17... | collective-permute-start | bytes 393224 | tf_op jit(solution)/shard_map/ppermute | solution.py:408
  21.8 0.3 %collective-permute-done.6.refs_3_ = bf16[2,128,128]{2,1,0:T(8,128)(2,1)S(1)} collective-permute-done((bf16[2,128,128]{2,1,0:T(8,128)(2,1)S(1)}, bf16[2,128,128]{2,1,0:T(8,128)(2,1)S(1)}, u32[]{:S(2)}, u32[]{:S(2)}) %collective-permute-start.6) | collective-permute-done | bytes 65568 | tf_op jit(solution)/shard_map/ppermute | solution.py:340
  22.1 0.3 %collective-permute-done.7.refs_4_ = bf16[2,128,128]{2,1,0:T(8,128)(2,1)S(1)} collective-permute-done((bf16[2,128,128]{2,1,0:T(8,128)(2,1)S(1)}, bf16[2,128,128]{2,1,0:T(8,128)(2,1)S(1)}, u32[]{:S(2)}, u32[]{:S(2)}) %collective-permute-start.7) | collective-permute-done | bytes 65568 | tf_op jit(solution)/shard_map/ppermute | solution.py:340
  22.5 0.9 %unpack.1 = (bf16[1,128,512]{2,1,0:T(8,128)(2,1)}, bf16[1,128,512]{2,1,0:T(8,128)(2,1)}) custom-call(bf16[4,128,128]{2,1,0:T(8,128)(2,1)S(1)} %get-tuple-element.30.own_ref.refs_0_, bf16[4,128,128]{2,1,0:T(8,128)(2,1)S(1)} %collective-permute-done.4.got_ref.refs_1_, bf16[2,128,128]{2,1,0:T(8,128)(2,1)S(1)} %collective-permute-done.5.refs_2_, ...), custom_call_target="tpu_custom_call" | custom-call | flops 5000000000 | bytes 655360 | tf_op jit(solution)/shard_map/unpack/pallas_call | solution.py:312
  23.3 1.8 %collective-permute-done.9.right_ref = bf16[64,1024]{1,0:T(8,128)(2,1)S(1)} collective-permute-done((bf16[64,1024]{1,0:T(8,128)(2,1)S(1)}, bf16[64,1024]{1,0:T(8,128)(2,1)S(1)}, u32[]{:S(2)}, u32[]{:S(2)}) %collective-permute-start.9) | collective-permute-done | bytes 131104 | tf_op jit(solution)/shard_map/ppermute | solution.py:408
  25.2 0.7 %total.1 = f32[64,1024]{1,0:T(8,128)} custom-call(bf16[64,1024]{1,0:T(8,128)(2,1)S(1)} %pair_sum.1.left_ref, bf16[64,1024]{1,0:T(8,128)(2,1)S(1)} %collective-permute-done.9.right_ref, bf16[1,128,512]{2,1,0:T(8,128)(2,1)} %get-tuple-element.19._), custom_call_target="tpu_custom_call" | custom-call | bytes 524288 | tf_op jit(solution)/shard_map/total/pallas_call | solution.py:312
  (6 shorter events, 0.1 us)
Async XLA Ops:
  1.8 1.5 %collective-permute-start = (bf16[4,128,128]{2,1,0:T(8,128)(2,1)S(1)}, bf16[4,128,128]{2,1,0:T(8,128)(2,1)S(1)}, u32[]{:S(2)}, u32[]{:S(2)}) collective-permute-start(bf16[4,128,128]{2,1,0:T(8,128)(2,1)S(1)} %get-tuple-element.22), channel_id=1, source_target_pairs={{0,1},{1,0},{2,3},{3,2},{4,5},{5,4},{6,7},{7,6},{8,9},{9,8},{10,11... | collective-permute-start | bytes 393224 | tf_op jit(solution)/shard_map/ppermute | solution.py:330
  3.3 6.8 %collective-permute-start.1 = (bf16[2,128,128]{2,1,0:T(8,128)(2,1)S(1)}, bf16[2,128,128]{2,1,0:T(8,128)(2,1)S(1)}, u32[]{:S(2)}, u32[]{:S(2)}) collective-permute-start(bf16[2,128,128]{2,1,0:T(8,128)(2,1)S(1)} %get-tuple-element.23), channel_id=1, source_target_pairs={{0,6},{1,7},{2,4},{3,5},{4,2},{5,3},{6,0},{7,1},{8,14},{9,15},{10,... | collective-permute-start | bytes 196616 | tf_op jit(solution)/shard_map/ppermute | solution.py:340
  7.2 4.3 %collective-permute-start.2 = (bf16[2,128,128]{2,1,0:T(8,128)(2,1)S(1)}, bf16[2,128,128]{2,1,0:T(8,128)(2,1)S(1)}, u32[]{:S(2)}, u32[]{:S(2)}) collective-permute-start(bf16[2,128,128]{2,1,0:T(8,128)(2,1)S(1)} %get-tuple-element.24), channel_id=1, source_target_pairs={{0,4},{1,5},{2,6},{3,7},{4,0},{5,1},{6,2},{7,3},{8,12},{9,13},{10,... | collective-permute-start | bytes 196616 | tf_op jit(solution)/shard_map/ppermute | solution.py:340
  7.7 0.7 %copy-start = (f32[64]{0:T(128)S(1)}, f32[64]{0:T(128)}, u32[]{:S(2)}) copy-start(f32[64]{0:T(128)} %param.11) | copy-start | bytes 772
  7.7 4.3 %collective-permute-start.3 = (bf16[2,128,128]{2,1,0:T(8,128)(2,1)S(1)}, bf16[2,128,128]{2,1,0:T(8,128)(2,1)S(1)}, u32[]{:S(2)}, u32[]{:S(2)}) collective-permute-start(bf16[2,128,128]{2,1,0:T(8,128)(2,1)S(1)} %get-tuple-element.25), channel_id=1, source_target_pairs={{0,2},{1,3},{2,0},{3,1},{4,6},{5,7},{6,4},{7,5},{8,10},{9,11},{10,... | collective-permute-start | bytes 196616 | tf_op jit(solution)/shard_map/ppermute | solution.py:340
  13.2 2.7 %collective-permute-start.4 = (bf16[4,128,128]{2,1,0:T(8,128)(2,1)S(1)}, bf16[4,128,128]{2,1,0:T(8,128)(2,1)S(1)}, u32[]{:S(2)}, u32[]{:S(2)}) collective-permute-start(bf16[4,128,128]{2,1,0:T(8,128)(2,1)S(1)} %get-tuple-element.31), channel_id=1, source_target_pairs={{0,1},{1,0},{2,3},{3,2},{4,5},{5,4},{6,7},{7,6},{8,9},{9,8},{10,11... | collective-permute-start | bytes 393224 | tf_op jit(solution)/shard_map/ppermute | solution.py:330
  13.2 6.4 %collective-permute-start.8 = (bf16[64,1024]{1,0:T(8,128)(2,1)S(1)}, bf16[64,1024]{1,0:T(8,128)(2,1)S(1)}, u32[]{:S(2)}, u32[]{:S(2)}) collective-permute-start(bf16[64,1024]{1,0:T(8,128)(2,1)S(1)} %get-tuple-element.38.left_ref), channel_id=1, source_target_pairs={{0,16},{1,9},{2,18},{3,11},{4,20},{5,13},{6,22},{7,15},{8,24},{9,1... | collective-permute-start | bytes 393224 | tf_op jit(solution)/shard_map/ppermute | solution.py:408
  15.9 5.9 %collective-permute-start.5 = (bf16[2,128,128]{2,1,0:T(8,128)(2,1)S(1)}, bf16[2,128,128]{2,1,0:T(8,128)(2,1)S(1)}, u32[]{:S(2)}, u32[]{:S(2)}) collective-permute-start(bf16[2,128,128]{2,1,0:T(8,128)(2,1)S(1)} %get-tuple-element.32), channel_id=1, source_target_pairs={{0,6},{1,7},{2,4},{3,5},{4,2},{5,3},{6,0},{7,1},{8,14},{9,15},{10,... | collective-permute-start | bytes 196616 | tf_op jit(solution)/shard_map/ppermute | solution.py:340
  17.5 4.7 %collective-permute-start.6 = (bf16[2,128,128]{2,1,0:T(8,128)(2,1)S(1)}, bf16[2,128,128]{2,1,0:T(8,128)(2,1)S(1)}, u32[]{:S(2)}, u32[]{:S(2)}) collective-permute-start(bf16[2,128,128]{2,1,0:T(8,128)(2,1)S(1)} %get-tuple-element.33), channel_id=1, source_target_pairs={{0,4},{1,5},{2,6},{3,7},{4,0},{5,1},{6,2},{7,3},{8,12},{9,13},{10,... | collective-permute-start | bytes 196616 | tf_op jit(solution)/shard_map/ppermute | solution.py:340
  18.2 4.3 %collective-permute-start.7 = (bf16[2,128,128]{2,1,0:T(8,128)(2,1)S(1)}, bf16[2,128,128]{2,1,0:T(8,128)(2,1)S(1)}, u32[]{:S(2)}, u32[]{:S(2)}) collective-permute-start(bf16[2,128,128]{2,1,0:T(8,128)(2,1)S(1)} %get-tuple-element.34), channel_id=1, source_target_pairs={{0,2},{1,3},{2,0},{3,1},{4,6},{5,7},{6,4},{7,5},{8,10},{9,11},{10,... | collective-permute-start | bytes 196616 | tf_op jit(solution)/shard_map/ppermute | solution.py:340
  19.7 5.5 %collective-permute-start.9 = (bf16[64,1024]{1,0:T(8,128)(2,1)S(1)}, bf16[64,1024]{1,0:T(8,128)(2,1)S(1)}, u32[]{:S(2)}, u32[]{:S(2)}) collective-permute-start(bf16[64,1024]{1,0:T(8,128)(2,1)S(1)} %pair_sum.1.left_ref), channel_id=1, source_target_pairs={{0,8},{1,25},{2,10},{3,27},{4,12},{5,29},{6,14},{7,31},{8,0},{9,17... | collective-permute-start | bytes 393224 | tf_op jit(solution)/shard_map/ppermute | solution.py:408

commit v7 on v6

--- a/solution.py
+++ b/solution.py
@@ -226,9 +226,13 @@
     return (a[1], -a[0]) if odd else (-a[1], a[0])
 
 
-def main_kernel(pairs, *refs):
-    fwd_ref, inv_ref, filt_ref, gain_ref = refs[pairs + 1 : pairs + 5]
-    own_ref, sib_ref, cross_ref, spec_ref, prod_ref, block_ref = refs[pairs + 5 :]
+def main_kernel(pairs, home, *refs):
+    fwd_ref, inv_ref = refs[pairs + 1 : pairs + 3]
+    if home:
+        filt_ref, gain_ref, _, own_ref, sib_ref, *sent_refs = refs[pairs + 3 : -3]
+    else:
+        (cross_ref,) = refs[pairs + 3 : -3]
+    spec_ref, prod_ref, block_ref = refs[-3:]
     parts, rows, pos = block_ref.shape
     chans = rows // 2
     half = parts // 2 * pos
@@ -251,29 +255,44 @@
                     return [ref[at, i + c : i + c + 128] for i in (col, col + half // 2)]
 
                 v0, g0, v1, g1 = [load(spec_ref.at[odd], i, 0) for i in range(4)]
-                h0, h1 = [load(filt_ref, i, odd * half) for i in range(2)]
-                conv0 = mul(h0, v0)
-                conv1 = add(add(mul(h0, v1), mul(h1, v0)), later(conv0, odd))
-                corr1 = conj_mul(h0, g1)
-                corr0 = add(add(conj_mul(h0, g0), conj_mul(h1, g1)), later(corr1, not odd))
-                cross1 = conj_mul(v0, g1)
-                cross0 = add(add(conj_mul(v0, g0), conj_mul(v1, g1)), later(cross1, not odd))
-                for i, parts_of in enumerate((conv0, corr0, cross0, conv1, corr1, cross1)):
+                if home:
+                    h0, h1 = [load(filt_ref, i, odd * half) for i in range(2)]
+                    conv0 = mul(h0, v0)
+                    conv1 = add(add(mul(h0, v1), mul(h1, v0)), later(conv0, odd))
+                    corr1 = conj_mul(h0, g1)
+                    corr0 = add(add(conj_mul(h0, g0), conj_mul(h1, g1)), later(corr1, not odd))
+                    spectra = (conv0, corr0, conv1, corr1)
+                else:
+                    cross1 = conj_mul(v0, g1)
+                    cross0 = add(add(conj_mul(v0, g0), conj_mul(v1, g1)), later(cross1, not odd))
+                    spectra = (cross0, cross1)
+                for i, parts_of in enumerate(spectra):
                     at = slice(i * chans + r, i * chans + r + 16)
                     for col, part in zip((c, c + half // 2), parts_of):
                         prod_ref[odd, at, col : col + 128] = part.astype(BF16)
         res = res + jnp.dot(prod_ref[odd], inv_ref[bins, :], preferred_element_type=F32)
+    if not home:
+        for i in range(2):
+            cross = res[i * chans : (i + 1) * chans] * (1.0 / half)
+            cross_ref[:, i * half : (i + 1) * half] = cross.astype(BF16)
+        return
     gains = jnp.concatenate([gain_ref[...]] * (half // 128), axis=1)
     scale = (2 * half) ** -0.5 / half
     for i in range(2):
-        top = i * 3 * chans
-        both = (res[top : top + rows] * scale + gains * x[i].astype(F32)).astype(BF16)
+        both = (res[i * rows : (i + 1) * rows] * scale + gains * x[i].astype(F32)).astype(BF16)
         for s in range(parts // 2):
             block_ref[i * (parts // 2) + s] = both[:, s * pos : (s + 1) * pos]
-        cross = res[top + rows : top + rows + chans] * (1.0 / half)
-        cross_ref[:, i * half : (i + 1) * half] = cross.astype(BF16)
     for f, d, at in places(parts):
-        (sib_ref if f else own_ref)[d] = block_ref[at]
+        if d:
+            sent_refs[d - 1][f] = block_ref[at]
+        else:
+            (sib_ref if f else own_ref)[...] = block_ref[at]
+
+
+def gather_kernel(*refs):
+    *pair_refs, _, out_ref = refs
+    for d in range(1, out_ref.shape[0] + 1):
+        out_ref[d - 1] = pair_refs[-d][1]
 
 
 def pair_kernel(left_ref, right_ref, out_ref):
@@ -281,11 +300,14 @@
 
 
 def unpack_kernel(pairs, *refs):
-    near_ref, val_hbm, gate_hbm, val_ref, gate_ref, turn_ref, sems = refs[pairs + 1 :]
+    near_ref, val_hbm, gate_hbm, val_ref, gate_ref, turn_ref, sems = refs[pairs + 2 :]
     chans = turn_ref.shape[1] // (2 * pairs)
     for f, d, at in places(2 * pairs):
         at = pl.multiple_of(at * chans, chans)
-        both = refs[pairs + 1 - d][f] if d else refs[f][0]
+        if f:
+            both = refs[1][d - 1] if d else refs[pairs + 1][...]
+        else:
+            both = refs[pairs + 1 - d][0] if d else refs[0][...]
         turn_ref[0, pl.ds(at, chans), :] = both[:chans]
         turn_ref[1, pl.ds(at, chans), :] = both[chans:]
     val_ref[0] = turn_ref[1].astype(F32).T.astype(BF16)
@@ -388,21 +410,38 @@
         flops=4 * chans * length * length,
         moved=8 * length * length,
     )
-    own, sib, cross = call(
-        functools.partial(main_kernel, pairs),
-        "products",
-        [(*pair_blocks, True), (*pair_blocks, True), ((chans, length), BF16, True)],
-        tuple(in_vmem(x) for x in held + [fwd_near, inv_near, spec, gains]),
-        vmem_specs(pairs + 5),
-        scratch=[
+    def scratch(count):
+        return [
             ((2, 2 * rows, length // 2), F32),
-            ((2, 3 * rows, length // 2), BF16),
+            ((2, count * chans, length // 2), BF16),
             ((parts, rows, pos), BF16),
-        ],
-        flops=10 * chans * length * length,
+        ]
+
+    (cross,) = call(
+        functools.partial(main_kernel, pairs, False),
+        "filter_products",
+        [((chans, length), BF16, True)],
+        tuple(in_vmem(x) for x in held + [fwd_near, inv_near]),
+        vmem_specs(pairs + 3),
+        scratch=scratch(2),
+        flops=6 * chans * length * length,
         moved=8 * length * length,
     )
-    home = exchange(own, sib, "home")
+    block = ((rows, pos), BF16, True)
+    own, sib, *sent = call(
+        functools.partial(main_kernel, pairs, True),
+        "home_products",
+        [block, block] + [((2, rows, pos), BF16, True)] * (pairs - 1),
+        tuple(in_vmem(x) for x in held + [fwd_near, inv_near, spec, gains, cross]),
+        vmem_specs(pairs + 6),
+        scratch=scratch(4),
+        flops=8 * chans * length * length,
+        moved=8 * length * length,
+    )
+    came = [
+        lax.ppermute(sent[d - 1], "ctx", [(j, j ^ (2 * d)) for j in range(parts)])
+        for d in reversed(range(1, pairs))
+    ]
     step = seqs // 2
     while step:
         other = lax.ppermute(cross, ("dp", "ctx"), dp_pairs(seqs, parts, step))
@@ -416,15 +455,24 @@
                 vmem_specs(2),
                 moved=6 * chans * length,
             )
+    (theirs,) = call(
+        gather_kernel,
+        "gather",
+        [((pairs - 1, rows, pos), BF16, True)],
+        tuple(in_vmem(x) for x in came + [cross]),
+        vmem_specs(pairs),
+        moved=4 * pairs * rows * pos,
+    )
+    swap = [(j, j ^ 1) for j in range(parts)]
+    home = [own, lax.ppermute(theirs, "ctx", swap)] + came + [lax.ppermute(sib, "ctx", swap)]
     grad_values, grad_gates = call(
         functools.partial(unpack_kernel, pairs),
         "unpack",
         [(*token, False), (*token, False)],
         tuple(in_vmem(x) for x in home + [grad_near]),
-        vmem_specs(pairs + 2),
+        vmem_specs(pairs + 3),
         scratch=[token, token, turned],
         sems=2,
-        flops=UNPACK_COST,
         moved=10 * pos * width,
     )
     (grad_filters,) = call(

time: 26.1 us -> 26.6 us (1.019)
  waiting for transfers between devices: 5.45 us -> 4.5 us
  starting transfers between devices: 13.5 us -> 14.4 us
  Pallas kernels: 5.78 us -> 6.26 us
    ppermute x0 -> x5, starting transfers between devices: none -> 4.12 us  [the longest x3 3.55 us: per_device_short(): lax.ppermute(sent[d - 1], 'ctx', [(j, j ^ 2 * d) for j in range(parts)])]
    ppermute x6 -> x3, starting transfers between devices: 8.06 us -> 4.51 us  [exchange(): lax.ppermute(sent[d - 1], 'ctx', [(j, j ^ 2 * d) for j in range(2 * pairs)])]
    ppermute x2, waiting for transfers between devices: 1.99 us -> 0.66 us  [per_device_short(): other = lax.ppermute(cross, ('dp', 'ctx'), dp_pairs(seqs, parts, step))]
    ppermute x0 -> x5, waiting for transfers between devices: none -> 1.04 us  [the longest x1 0.86 us: per_device_short(): lax.ppermute(sib, 'ctx', swap)]
    ppermute x6 -> x3, waiting for transfers between devices: 2.47 us -> 1.82 us  [exchange(): lax.ppermute(sent[d - 1], 'ctx', [(j, j ^ 2 * d) for j in range(2 * pairs)])]
    pallas_call x8 -> x9, Pallas kernels: 5.78 us -> 6.26 us  [call(): pl.pallas_call(kernel, out_shape=tuple((pltpu.VMEM(shape, dtype) if near...]
    ppermute x2, starting transfers between devices: 4.8 us -> 5.25 us  [per_device_short(): other = lax.ppermute(cross, ('dp', 'ctx'), dp_pairs(seqs, parts, step))]
    ppermute x2 -> x1, starting transfers between devices: 0.59 us -> 0.52 us  [exchange(): got = lax.ppermute(sib, 'ctx', [(j, j ^ 1) for j in range(2 * pairs)])]
  transfers between devices with their start and end apart: 10 -> 11, of which waited for: 7 -> 7; matrix products, arithmetic and copies ran while one was open for 0% -> 0% of each run, Pallas kernels for 10% -> 14%
where the time goes in v7:
time: 26.6 us; the launch traced here: 26.4 us
  starting transfers between devices  14.4 us (54%)
  Pallas kernels  6.26 us (24%)
  waiting for transfers between devices  4.5 us (17%)
  between operations  0.71 us (3%)
  local copies, waits for them, and re-layouts  0.52 us (2%)
    pallas_call x9, Pallas kernels, call(): pl.pallas_call(kernel, out_shape=tuple((pltpu.VMEM(shape, dtype) if near...  6.26 us
    ppermute x2, starting transfers between devices, per_device_short(): other = lax.ppermute(cross, ('dp', 'ctx'), dp_pairs(seqs, parts, step))  5.25 us
    ppermute x3, starting transfers between devices, exchange(): lax.ppermute(sent[d - 1], 'ctx', [(j, j ^ 2 * d) for j in range(2 * pairs)])  4.51 us
    ppermute x3, starting transfers between devices, per_device_short(): lax.ppermute(sent[d - 1], 'ctx', [(j, j ^ 2 * d) for j in range(parts)])  3.55 us
    ppermute x3, waiting for transfers between devices, exchange(): lax.ppermute(sent[d - 1], 'ctx', [(j, j ^ 2 * d) for j in range(2 * pairs)])  1.82 us
    ppermute x1, waiting for transfers between devices, exchange(): got = lax.ppermute(sib, 'ctx', [(j, j ^ 1) for j in range(2 * pairs)])  0.99 us
    ppermute x1, waiting for transfers between devices, per_device_short(): lax.ppermute(sib, 'ctx', swap)  0.86 us
    ppermute x2, waiting for transfers between devices, per_device_short(): other = lax.ppermute(cross, ('dp', 'ctx'), dp_pairs(seqs, parts, step))  0.66 us
  transfers between devices with their start and end apart: 11, of which 7 were waited for; matrix products, arithmetic and copies ran while one was open for 0% of the time, Pallas kernels for 14%

profile of v7, /device:TPU:0, one launch (start us, length us, event | category | flops | bytes accessed | tf_op | source)
XLA Modules:
  0.0 26.4 jit_solution(9690622820278135651)
XLA Ops:
  0.6 1.2 %pack.1 = (bf16[4,128,128]{2,1,0:T(8,128)(2,1)S(1)}, bf16[4,128,128]{2,1,0:T(8,128)(2,1)S(1)}, bf16[1,128,512]{2,1,0:T(8,128)(2,1)S(1)}) custom-call(bf16[1,128,512]{2,1,0:T(8,128)(2,1)} %vals_hbm.1, bf16[1,128,512]{2,1,0:T(8,128)(2,1)} %gate_hbm.1, bf16[1,128,512]{2,1,0:T(8,128)(2,1)} %grad_hbm.1), custom_call_target="tpu_custom_call" | custom-call | bytes 524288 | tf_op jit(solution)/shard_map/pack/pallas_call | solution.py:334
  1.8 0.5 %collective-permute-start = (bf16[4,128,128]{2,1,0:T(8,128)(2,1)S(1)}, bf16[4,128,128]{2,1,0:T(8,128)(2,1)S(1)}, u32[]{:S(2)}, u32[]{:S(2)}) collective-permute-start(bf16[4,128,128]{2,1,0:T(8,128)(2,1)S(1)} %get-tuple-element.21), channel_id=1, source_target_pairs={{0,1},{1,0},{2,3},{3,2},{4,5},{5,4},{6,7},{7,6},{8,9},{9,8},{10,11... | collective-permute-start | bytes 393224 | tf_op jit(solution)/shard_map/ppermute | solution.py:352
  2.3 1.0 %collective-permute-done.got_ref.refs_1_ = bf16[4,128,128]{2,1,0:T(8,128)(2,1)S(1)} collective-permute-done((bf16[4,128,128]{2,1,0:T(8,128)(2,1)S(1)}, bf16[4,128,128]{2,1,0:T(8,128)(2,1)S(1)}, u32[]{:S(2)}, u32[]{:S(2)}) %collective-permute-start) | collective-permute-done | bytes 131104 | tf_op jit(solution)/shard_map/ppermute | solution.py:352
  3.3 3.9 %collective-permute-start.1 = (bf16[2,128,128]{2,1,0:T(8,128)(2,1)S(1)}, bf16[2,128,128]{2,1,0:T(8,128)(2,1)S(1)}, u32[]{:S(2)}, u32[]{:S(2)}) collective-permute-start(bf16[2,128,128]{2,1,0:T(8,128)(2,1)S(1)} %get-tuple-element.22), channel_id=1, source_target_pairs={{0,6},{1,7},{2,4},{3,5},{4,2},{5,3},{6,0},{7,1},{8,14},{9,15},{10,... | collective-permute-start | bytes 196616 | tf_op jit(solution)/shard_map/ppermute | solution.py:362
  7.2 0.5 %collective-permute-start.2 = (bf16[2,128,128]{2,1,0:T(8,128)(2,1)S(1)}, bf16[2,128,128]{2,1,0:T(8,128)(2,1)S(1)}, u32[]{:S(2)}, u32[]{:S(2)}) collective-permute-start(bf16[2,128,128]{2,1,0:T(8,128)(2,1)S(1)} %get-tuple-element.23), channel_id=1, source_target_pairs={{0,4},{1,5},{2,6},{3,7},{4,0},{5,1},{6,2},{7,3},{8,12},{9,13},{10,... | collective-permute-start | bytes 196616 | tf_op jit(solution)/shard_map/ppermute | solution.py:362
  7.7 0.1 collective-permute-start.3
  7.9 0.5 %copy-done = f32[64]{0:T(128)S(1)} copy-done((f32[64]{0:T(128)S(1)}, f32[64]{0:T(128)}, u32[]{:S(2)}) %copy-start) | copy-done | bytes 280
  8.4 1.8 %filter_spectrum.1 = (f32[128,1024]{1,0:T(8,128)S(1)}, bf16[512,1024]{1,0:T(8,128)(2,1)S(1)}, bf16[1024,512]{1,0:T(8,128)(2,1)S(1)}, f32[128,128]{1,0:T(8,128)S(1)}) custom-call(f32[64,1024]{1,0:T(8,128)} %filt_hbm.1, bf16[512,1024]{1,0:T(8,128)(2,1)} %constant.4.clone.fwd_hbm, bf16[1024,512]{1,0:T(8,128)(2,1)} %constant.5.clone.inv_hbm, f32[1,64]{1,0:T(1,128)S(1)} %bitcast.1), custom_call_target="tpu_custom_call" | custom-call | flops 268435456 | bytes 8388608 | tf_op jit(solution)/shard_map/filter_spectrum/pallas_call | solution.py:334
  10.2 1.3 %collective-permute-done.2.refs_3_ = bf16[2,128,128]{2,1,0:T(8,128)(2,1)S(1)} collective-permute-done((bf16[2,128,128]{2,1,0:T(8,128)(2,1)S(1)}, bf16[2,128,128]{2,1,0:T(8,128)(2,1)S(1)}, u32[]{:S(2)}, u32[]{:S(2)}) %collective-permute-start.2) | collective-permute-done | bytes 65568 | tf_op jit(solution)/shard_map/ppermute | solution.py:362
  11.5 0.5 %collective-permute-done.3.refs_4_ = bf16[2,128,128]{2,1,0:T(8,128)(2,1)S(1)} collective-permute-done((bf16[2,128,128]{2,1,0:T(8,128)(2,1)S(1)}, bf16[2,128,128]{2,1,0:T(8,128)(2,1)S(1)}, u32[]{:S(2)}, u32[]{:S(2)}) %collective-permute-start.3) | collective-permute-done | bytes 65568 | tf_op jit(solution)/shard_map/ppermute | solution.py:362
  12.0 0.7 %filter_products.1.refs_9_.left_ref = bf16[64,1024]{1,0:T(8,128)(2,1)S(1)} custom-call(bf16[4,128,128]{2,1,0:T(8,128)(2,1)S(1)} %get-tuple-element.20.own_ref.refs_0_, bf16[4,128,128]{2,1,0:T(8,128)(2,1)S(1)} %collective-permute-done.got_ref.refs_1_, bf16[2,128,128]{2,1,0:T(8,128)(2,1)S(1)} %collective-permute-done.1.refs_2_, ...), custom_call_target="tpu_custom_call" | custom-call | flops 402653184 | bytes 8388608 | tf_op jit(solution)/shard_map/filter_products/pallas_call | solution.py:334
  12.7 2.7 %collective-permute-start.7 = (bf16[64,1024]{1,0:T(8,128)(2,1)S(1)}, bf16[64,1024]{1,0:T(8,128)(2,1)S(1)}, u32[]{:S(2)}, u32[]{:S(2)}) collective-permute-start(bf16[64,1024]{1,0:T(8,128)(2,1)S(1)} %filter_products.1.refs_9_.left_ref), channel_id=1, source_target_pairs={{0,16},{1,9},{2,18},{3,11},{4,20},{5,13},{6,22},{7,15},{8,24},{9,1... | collective-permute-start | bytes 393224 | tf_op jit(solution)/shard_map/ppermute | solution.py:447
  15.4 0.9 %home_products.1 = (bf16[128,128]{1,0:T(8,128)(2,1)S(1)}, bf16[128,128]{1,0:T(8,128)(2,1)S(1)}, bf16[2,128,128]{2,1,0:T(8,128)(2,1)S(1)}, bf16[2,128,128]{2,1,0:T(8,128)(2,1)S(1)}, bf16[2,128,128]{2,1,0:T(8,128)(2,1)S(1)}) custom-call(bf16[4,128,128]{2,1,0:T(8,128)(2,1)S(1)} %get-tuple-element.20.own_ref.refs_0_, ...), custom_call_target="tpu_custom_call" | custom-call | flops 536870912 | bytes 8388608 | tf_op jit(solution)/shard_map/home_products/pallas_call | solution.py:334
  16.3 1.6 %collective-permute-start.4 = (bf16[2,128,128]{2,1,0:T(8,128)(2,1)S(1)}, bf16[2,128,128]{2,1,0:T(8,128)(2,1)S(1)}, u32[]{:S(2)}, u32[]{:S(2)}) collective-permute-start(bf16[2,128,128]{2,1,0:T(8,128)(2,1)S(1)} %get-tuple-element.30), channel_id=1, source_target_pairs={{0,6},{1,7},{2,4},{3,5},{4,2},{5,3},{6,0},{7,1},{8,14},{9,15},{10,... | collective-permute-start | bytes 196616 | tf_op jit(solution)/shard_map/ppermute | solution.py:442
  17.9 0.7 %collective-permute-start.5 = (bf16[2,128,128]{2,1,0:T(8,128)(2,1)S(1)}, bf16[2,128,128]{2,1,0:T(8,128)(2,1)S(1)}, u32[]{:S(2)}, u32[]{:S(2)}) collective-permute-start(bf16[2,128,128]{2,1,0:T(8,128)(2,1)S(1)} %get-tuple-element.31), channel_id=1, source_target_pairs={{0,4},{1,5},{2,6},{3,7},{4,0},{5,1},{6,2},{7,3},{8,12},{9,13},{10,... | collective-permute-start | bytes 196616 | tf_op jit(solution)/shard_map/ppermute | solution.py:442
  18.6 1.3 %collective-permute-start.6 = (bf16[2,128,128]{2,1,0:T(8,128)(2,1)S(1)}, bf16[2,128,128]{2,1,0:T(8,128)(2,1)S(1)}, u32[]{:S(2)}, u32[]{:S(2)}) collective-permute-start(bf16[2,128,128]{2,1,0:T(8,128)(2,1)S(1)} %get-tuple-element.32), channel_id=1, source_target_pairs={{0,2},{1,3},{2,0},{3,1},{4,6},{5,7},{6,4},{7,5},{8,10},{9,11},{10,... | collective-permute-start | bytes 196616 | tf_op jit(solution)/shard_map/ppermute | solution.py:442
  19.9 0.2 collective-permute-done.7.right_ref
  20.1 2.6 %collective-permute-start.10 = (bf16[64,1024]{1,0:T(8,128)(2,1)S(1)}, bf16[64,1024]{1,0:T(8,128)(2,1)S(1)}, u32[]{:S(2)}, u32[]{:S(2)}) collective-permute-start(bf16[64,1024]{1,0:T(8,128)(2,1)S(1)} %pair_sum.1.refs_3_.left_ref), channel_id=1, source_target_pairs={{0,8},{1,25},{2,10},{3,27},{4,12},{5,29},{6,14},{7,31},{8,0},{9,17... | collective-permute-start | bytes 393224 | tf_op jit(solution)/shard_map/ppermute | solution.py:447
  22.7 0.2 collective-permute-done.6.refs_2_.refs_4_
  23.0 0.5 %collective-permute-start.9 = (bf16[128,128]{1,0:T(8,128)(2,1)S(1)}, bf16[128,128]{1,0:T(8,128)(2,1)S(1)}, u32[]{:S(2)}, u32[]{:S(2)}) collective-permute-start(bf16[128,128]{1,0:T(8,128)(2,1)S(1)} %get-tuple-element.33), channel_id=1, source_target_pairs={{0,1},{1,0},{2,3},{3,2},{4,5},{5,4},{6,7},{7,6},{8,9},{9,8},{10,11... | collective-permute-start | bytes 98312 | tf_op jit(solution)/shard_map/ppermute | solution.py:467
  23.5 0.9 %collective-permute-done.9.refs_5_ = bf16[128,128]{1,0:T(8,128)(2,1)S(1)} collective-permute-done((bf16[128,128]{1,0:T(8,128)(2,1)S(1)}, bf16[128,128]{1,0:T(8,128)(2,1)S(1)}, u32[]{:S(2)}, u32[]{:S(2)}) %collective-permute-start.9) | collective-permute-done | bytes 32800 | tf_op jit(solution)/shard_map/ppermute | solution.py:467
  24.3 0.9 %unpack.1 = (bf16[1,128,512]{2,1,0:T(8,128)(2,1)}, bf16[1,128,512]{2,1,0:T(8,128)(2,1)}) custom-call(bf16[128,128]{1,0:T(8,128)(2,1)S(1)} %get-tuple-element.29.refs_0_, bf16[3,128,128]{2,1,0:T(8,128)(2,1)S(1)} %collective-permute-done.8.refs_1_, bf16[2,128,128]{2,1,0:T(8,128)(2,1)S(1)} %collective-permute-done.4.refs_0_.refs_2_, ...), custom_call_target="tpu_custom_call" | custom-call | bytes 655360 | tf_op jit(solution)/shard_map/unpack/pallas_call | solution.py:334
  25.2 0.5 %collective-permute-done.10.right_ref = bf16[64,1024]{1,0:T(8,128)(2,1)S(1)} collective-permute-done((bf16[64,1024]{1,0:T(8,128)(2,1)S(1)}, bf16[64,1024]{1,0:T(8,128)(2,1)S(1)}, u32[]{:S(2)}, u32[]{:S(2)}) %collective-permute-start.10) | collective-permute-done | bytes 131104 | tf_op jit(solution)/shard_map/ppermute | solution.py:447
  25.6 0.7 %total.1 = f32[64,1024]{1,0:T(8,128)} custom-call(bf16[64,1024]{1,0:T(8,128)(2,1)S(1)} %pair_sum.1.refs_3_.left_ref, bf16[64,1024]{1,0:T(8,128)(2,1)S(1)} %collective-permute-done.10.right_ref, bf16[1,128,512]{2,1,0:T(8,128)(2,1)} %get-tuple-element.18._), custom_call_target="tpu_custom_call" | custom-call | bytes 524288 | tf_op jit(solution)/shard_map/total/pallas_call | solution.py:334
  (9 shorter events, 0.1 us)
Async XLA Ops:
  1.8 1.5 %collective-permute-start = (bf16[4,128,128]{2,1,0:T(8,128)(2,1)S(1)}, bf16[4,128,128]{2,1,0:T(8,128)(2,1)S(1)}, u32[]{:S(2)}, u32[]{:S(2)}) collective-permute-start(bf16[4,128,128]{2,1,0:T(8,128)(2,1)S(1)} %get-tuple-element.21), channel_id=1, source_target_pairs={{0,1},{1,0},{2,3},{3,2},{4,5},{5,4},{6,7},{7,6},{8,9},{9,8},{10,11... | collective-permute-start | bytes 393224 | tf_op jit(solution)/shard_map/ppermute | solution.py:352
  3.3 6.8 %collective-permute-start.1 = (bf16[2,128,128]{2,1,0:T(8,128)(2,1)S(1)}, bf16[2,128,128]{2,1,0:T(8,128)(2,1)S(1)}, u32[]{:S(2)}, u32[]{:S(2)}) collective-permute-start(bf16[2,128,128]{2,1,0:T(8,128)(2,1)S(1)} %get-tuple-element.22), channel_id=1, source_target_pairs={{0,6},{1,7},{2,4},{3,5},{4,2},{5,3},{6,0},{7,1},{8,14},{9,15},{10,... | collective-permute-start | bytes 196616 | tf_op jit(solution)/shard_map/ppermute | solution.py:362
  7.2 4.3 %collective-permute-start.2 = (bf16[2,128,128]{2,1,0:T(8,128)(2,1)S(1)}, bf16[2,128,128]{2,1,0:T(8,128)(2,1)S(1)}, u32[]{:S(2)}, u32[]{:S(2)}) collective-permute-start(bf16[2,128,128]{2,1,0:T(8,128)(2,1)S(1)} %get-tuple-element.23), channel_id=1, source_target_pairs={{0,4},{1,5},{2,6},{3,7},{4,0},{5,1},{6,2},{7,3},{8,12},{9,13},{10,... | collective-permute-start | bytes 196616 | tf_op jit(solution)/shard_map/ppermute | solution.py:362
  7.7 0.7 %copy-start = (f32[64]{0:T(128)S(1)}, f32[64]{0:T(128)}, u32[]{:S(2)}) copy-start(f32[64]{0:T(128)} %param.11) | copy-start | bytes 772
  7.7 4.3 %collective-permute-start.3 = (bf16[2,128,128]{2,1,0:T(8,128)(2,1)S(1)}, bf16[2,128,128]{2,1,0:T(8,128)(2,1)S(1)}, u32[]{:S(2)}, u32[]{:S(2)}) collective-permute-start(bf16[2,128,128]{2,1,0:T(8,128)(2,1)S(1)} %get-tuple-element.24), channel_id=1, source_target_pairs={{0,2},{1,3},{2,0},{3,1},{4,6},{5,7},{6,4},{7,5},{8,10},{9,11},{10,... | collective-permute-start | bytes 196616 | tf_op jit(solution)/shard_map/ppermute | solution.py:362
  12.7 7.3 %collective-permute-start.7 = (bf16[64,1024]{1,0:T(8,128)(2,1)S(1)}, bf16[64,1024]{1,0:T(8,128)(2,1)S(1)}, u32[]{:S(2)}, u32[]{:S(2)}) collective-permute-start(bf16[64,1024]{1,0:T(8,128)(2,1)S(1)} %filter_products.1.refs_9_.left_ref), channel_id=1, source_target_pairs={{0,16},{1,9},{2,18},{3,11},{4,20},{5,13},{6,22},{7,15},{8,24},{9,1... | collective-permute-start | bytes 393224 | tf_op jit(solution)/shard_map/ppermute | solution.py:447
  16.3 6.4 %collective-permute-start.4 = (bf16[2,128,128]{2,1,0:T(8,128)(2,1)S(1)}, bf16[2,128,128]{2,1,0:T(8,128)(2,1)S(1)}, u32[]{:S(2)}, u32[]{:S(2)}) collective-permute-start(bf16[2,128,128]{2,1,0:T(8,128)(2,1)S(1)} %get-tuple-element.30), channel_id=1, source_target_pairs={{0,6},{1,7},{2,4},{3,5},{4,2},{5,3},{6,0},{7,1},{8,14},{9,15},{10,... | collective-permute-start | bytes 196616 | tf_op jit(solution)/shard_map/ppermute | solution.py:442
  17.9 4.8 %collective-permute-start.5 = (bf16[2,128,128]{2,1,0:T(8,128)(2,1)S(1)}, bf16[2,128,128]{2,1,0:T(8,128)(2,1)S(1)}, u32[]{:S(2)}, u32[]{:S(2)}) collective-permute-start(bf16[2,128,128]{2,1,0:T(8,128)(2,1)S(1)} %get-tuple-element.31), channel_id=1, source_target_pairs={{0,4},{1,5},{2,6},{3,7},{4,0},{5,1},{6,2},{7,3},{8,12},{9,13},{10,... | collective-permute-start | bytes 196616 | tf_op jit(solution)/shard_map/ppermute | solution.py:442
  18.6 4.3 %collective-permute-start.6 = (bf16[2,128,128]{2,1,0:T(8,128)(2,1)S(1)}, bf16[2,128,128]{2,1,0:T(8,128)(2,1)S(1)}, u32[]{:S(2)}, u32[]{:S(2)}) collective-permute-start(bf16[2,128,128]{2,1,0:T(8,128)(2,1)S(1)} %get-tuple-element.32), channel_id=1, source_target_pairs={{0,2},{1,3},{2,0},{3,1},{4,6},{5,7},{6,4},{7,5},{8,10},{9,11},{10,... | collective-permute-start | bytes 196616 | tf_op jit(solution)/shard_map/ppermute | solution.py:442
  20.1 5.5 %collective-permute-start.10 = (bf16[64,1024]{1,0:T(8,128)(2,1)S(1)}, bf16[64,1024]{1,0:T(8,128)(2,1)S(1)}, u32[]{:S(2)}, u32[]{:S(2)}) collective-permute-start(bf16[64,1024]{1,0:T(8,128)(2,1)S(1)} %pair_sum.1.refs_3_.left_ref), channel_id=1, source_target_pairs={{0,8},{1,25},{2,10},{3,27},{4,12},{5,29},{6,14},{7,31},{8,0},{9,17... | collective-permute-start | bytes 393224 | tf_op jit(solution)/shard_map/ppermute | solution.py:447
  22.9 1.4 %collective-permute-start.8 = (bf16[3,128,128]{2,1,0:T(8,128)(2,1)S(1)}, bf16[3,128,128]{2,1,0:T(8,128)(2,1)S(1)}, u32[]{:S(2)}, u32[]{:S(2)}) collective-permute-start(bf16[3,128,128]{2,1,0:T(8,128)(2,1)S(1)} %gather.1), channel_id=1, source_target_pairs={{0,1},{1,0},{2,3},{3,2},{4,5},{5,4},{6,7},{7,6},{8,9},{9,8},{10,11... | collective-permute-start | bytes 294920 | tf_op jit(solution)/shard_map/ppermute | solution.py:467
  23.0 1.4 %collective-permute-start.9 = (bf16[128,128]{1,0:T(8,128)(2,1)S(1)}, bf16[128,128]{1,0:T(8,128)(2,1)S(1)}, u32[]{:S(2)}, u32[]{:S(2)}) collective-permute-start(bf16[128,128]{1,0:T(8,128)(2,1)S(1)} %get-tuple-element.33), channel_id=1, source_target_pairs={{0,1},{1,0},{2,3},{3,2},{4,5},{5,4},{6,7},{7,6},{8,9},{9,8},{10,11... | collective-permute-start | bytes 98312 | tf_op jit(solution)/shard_map/ppermute | solution.py:467

commit v8 on v6

--- a/solution.py
+++ b/solution.py
@@ -167,14 +167,17 @@
 ):
     pairs, rows, _ = own_ref.shape
     chans = rows // 2
-    copies = start_copies(
-        [(vals_hbm, vals_ref), (gate_hbm, gate_ref), (grad_hbm, grad_ref)], sems
-    )
-    copies[0].wait()
-    turn_ref[0] = vals_ref[0].astype(F32).T.astype(BF16)
-    copies[1].wait()
-    copies[2].wait()
-    turn_ref[1] = (grad_ref[0].astype(F32) * gate_ref[0].astype(F32)).T.astype(BF16)
+    moves = [(vals_hbm, vals_ref), (gate_hbm, gate_ref), (grad_hbm, grad_ref)]
+    width = vals_ref.shape[2] // 2
+    halves = [pl.ds(i * width, width) for i in range(2)]
+    copies = start_copies([(a.at[:, :, h], b.at[:, :, h]) for h in halves for a, b in moves], sems)
+    for i, h in enumerate(halves):
+        copies[3 * i].wait()
+        turn_ref[0, h, :] = vals_ref[0, :, h].astype(F32).T.astype(BF16)
+        copies[3 * i + 1].wait()
+        copies[3 * i + 2].wait()
+        dz = grad_ref[0, :, h].astype(F32) * gate_ref[0, :, h].astype(F32)
+        turn_ref[1, h, :] = dz.T.astype(BF16)
     for f, d, at in places(2 * pairs):
         out_ref = sib_ref if f else own_ref
         at = pl.multiple_of(at * chans, chans)
@@ -368,7 +371,7 @@
         tuple(in_hbm(x) for x in (values, gates, grad_out)),
         hbm_specs(3),
         scratch=[token, token, turned],
-        sems=3,
+        sems=6,
         moved=8 * pos * width,
     )
     held = exchange(own, sib, "out")

time: 26.1 us -> 26.3 us (level)
  no operation moved by 1% of the time
where the time goes in v8:
time: 26.3 us; the launch traced here: 26.1 us
  starting transfers between devices  13.5 us (51%)
  Pallas kernels  5.93 us (23%)
  waiting for transfers between devices  5.44 us (21%)
  between operations  0.7 us (3%)
  local copies, waits for them, and re-layouts  0.52 us (2%)
    ppermute x6, starting transfers between devices, exchange(): lax.ppermute(sent[d - 1], 'ctx', [(j, j ^ 2 * d) for j in range(2 * pairs)])  8.06 us
    pallas_call x8, Pallas kernels, call(): pl.pallas_call(kernel, out_shape=tuple((pltpu.VMEM(shape, dtype) if near...  5.93 us
    ppermute x2, starting transfers between devices, per_device_short(): other = lax.ppermute(cross, ('dp', 'ctx'), dp_pairs(seqs, parts, step))  4.81 us
    ppermute x6, waiting for transfers between devices, exchange(): lax.ppermute(sent[d - 1], 'ctx', [(j, j ^ 2 * d) for j in range(2 * pairs)])  2.47 us
    ppermute x2, waiting for transfers between devices, per_device_short(): other = lax.ppermute(cross, ('dp', 'ctx'), dp_pairs(seqs, parts, step))  1.98 us
    ppermute x2, waiting for transfers between devices, exchange(): got = lax.ppermute(sib, 'ctx', [(j, j ^ 1) for j in range(2 * pairs)])  0.99 us
    ppermute x2, starting transfers between devices, exchange(): got = lax.ppermute(sib, 'ctx', [(j, j ^ 1) for j in range(2 * pairs)])  0.59 us
  transfers between devices with their start and end apart: 10, of which 7 were waited for; matrix products, arithmetic and copies ran while one was open for 0% of the time, Pallas kernels for 10%

profile of v8, /device:TPU:0, one launch (start us, length us, event | category | flops | bytes accessed | tf_op | source)
XLA Modules:
  0.0 26.1 jit_solution(16803533325827905732)
XLA Ops:
  0.6 1.3 %pack.1 = (bf16[4,128,128]{2,1,0:T(8,128)(2,1)S(1)}, bf16[4,128,128]{2,1,0:T(8,128)(2,1)S(1)}, bf16[1,128,512]{2,1,0:T(8,128)(2,1)S(1)}) custom-call(bf16[1,128,512]{2,1,0:T(8,128)(2,1)} %vals_hbm.1, bf16[1,128,512]{2,1,0:T(8,128)(2,1)} %gate_hbm.1, bf16[1,128,512]{2,1,0:T(8,128)(2,1)} %grad_hbm.1), custom_call_target="tpu_custom_call" | custom-call | bytes 524288 | tf_op jit(solution)/shard_map/pack/pallas_call | solution.py:315
  2.0 0.5 %collective-permute-start = (bf16[4,128,128]{2,1,0:T(8,128)(2,1)S(1)}, bf16[4,128,128]{2,1,0:T(8,128)(2,1)S(1)}, u32[]{:S(2)}, u32[]{:S(2)}) collective-permute-start(bf16[4,128,128]{2,1,0:T(8,128)(2,1)S(1)} %get-tuple-element.22), channel_id=1, source_target_pairs={{0,1},{1,0},{2,3},{3,2},{4,5},{5,4},{6,7},{7,6},{8,9},{9,8},{10,11... | collective-permute-start | bytes 393224 | tf_op jit(solution)/shard_map/ppermute | solution.py:333
  2.5 1.0 %collective-permute-done.got_ref.refs_1_ = bf16[4,128,128]{2,1,0:T(8,128)(2,1)S(1)} collective-permute-done((bf16[4,128,128]{2,1,0:T(8,128)(2,1)S(1)}, bf16[4,128,128]{2,1,0:T(8,128)(2,1)S(1)}, u32[]{:S(2)}, u32[]{:S(2)}) %collective-permute-start) | collective-permute-done | bytes 131104 | tf_op jit(solution)/shard_map/ppermute | solution.py:333
  3.5 3.9 %collective-permute-start.1 = (bf16[2,128,128]{2,1,0:T(8,128)(2,1)S(1)}, bf16[2,128,128]{2,1,0:T(8,128)(2,1)S(1)}, u32[]{:S(2)}, u32[]{:S(2)}) collective-permute-start(bf16[2,128,128]{2,1,0:T(8,128)(2,1)S(1)} %get-tuple-element.23), channel_id=1, source_target_pairs={{0,6},{1,7},{2,4},{3,5},{4,2},{5,3},{6,0},{7,1},{8,14},{9,15},{10,... | collective-permute-start | bytes 196616 | tf_op jit(solution)/shard_map/ppermute | solution.py:343
  7.4 0.5 %collective-permute-start.2 = (bf16[2,128,128]{2,1,0:T(8,128)(2,1)S(1)}, bf16[2,128,128]{2,1,0:T(8,128)(2,1)S(1)}, u32[]{:S(2)}, u32[]{:S(2)}) collective-permute-start(bf16[2,128,128]{2,1,0:T(8,128)(2,1)S(1)} %get-tuple-element.24), channel_id=1, source_target_pairs={{0,4},{1,5},{2,6},{3,7},{4,0},{5,1},{6,2},{7,3},{8,12},{9,13},{10,... | collective-permute-start | bytes 196616 | tf_op jit(solution)/shard_map/ppermute | solution.py:343
  7.9 0.1 collective-permute-start.3
  8.0 0.5 %copy-done = f32[64]{0:T(128)S(1)} copy-done((f32[64]{0:T(128)S(1)}, f32[64]{0:T(128)}, u32[]{:S(2)}) %copy-start) | copy-done | bytes 280
  8.5 1.8 %filter_spectrum.1 = (f32[128,1024]{1,0:T(8,128)S(1)}, bf16[512,1024]{1,0:T(8,128)(2,1)S(1)}, bf16[1024,512]{1,0:T(8,128)(2,1)S(1)}, f32[128,128]{1,0:T(8,128)S(1)}) custom-call(f32[64,1024]{1,0:T(8,128)} %filt_hbm.1, bf16[512,1024]{1,0:T(8,128)(2,1)} %constant.4.clone.fwd_hbm, bf16[1024,512]{1,0:T(8,128)(2,1)} %constant.5.clone.inv_hbm, f32[1,64]{1,0:T(1,128)S(1)} %bitcast.1), custom_call_target="tpu_custom_call" | custom-call | flops 268435456 | bytes 8388608 | tf_op jit(solution)/shard_map/filter_spectrum/pallas_call | solution.py:315
  10.3 1.3 %collective-permute-done.2.refs_3_ = bf16[2,128,128]{2,1,0:T(8,128)(2,1)S(1)} collective-permute-done((bf16[2,128,128]{2,1,0:T(8,128)(2,1)S(1)}, bf16[2,128,128]{2,1,0:T(8,128)(2,1)S(1)}, u32[]{:S(2)}, u32[]{:S(2)}) %collective-permute-start.2) | collective-permute-done | bytes 65568 | tf_op jit(solution)/shard_map/ppermute | solution.py:343
  11.6 0.5 %collective-permute-done.3.refs_4_ = bf16[2,128,128]{2,1,0:T(8,128)(2,1)S(1)} collective-permute-done((bf16[2,128,128]{2,1,0:T(8,128)(2,1)S(1)}, bf16[2,128,128]{2,1,0:T(8,128)(2,1)S(1)}, u32[]{:S(2)}, u32[]{:S(2)}) %collective-permute-start.3) | collective-permute-done | bytes 65568 | tf_op jit(solution)/shard_map/ppermute | solution.py:343
  12.1 1.2 %products.1 = (bf16[4,128,128]{2,1,0:T(8,128)(2,1)S(1)}, bf16[4,128,128]{2,1,0:T(8,128)(2,1)S(1)}, bf16[64,1024]{1,0:T(8,128)(2,1)S(1)}) custom-call(bf16[4,128,128]{2,1,0:T(8,128)(2,1)S(1)} %get-tuple-element.21.own_ref.refs_0_, bf16[4,128,128]{2,1,0:T(8,128)(2,1)S(1)} %collective-permute-done.got_ref.refs_1_, ...), custom_call_target="tpu_custom_call" | custom-call | flops 671088640 | bytes 8388608 | tf_op jit(solution)/shard_map/products/pallas_call | solution.py:315
  13.3 0.1 collective-permute-start.4
  13.4 2.7 %collective-permute-start.8 = (bf16[64,1024]{1,0:T(8,128)(2,1)S(1)}, bf16[64,1024]{1,0:T(8,128)(2,1)S(1)}, u32[]{:S(2)}, u32[]{:S(2)}) collective-permute-start(bf16[64,1024]{1,0:T(8,128)(2,1)S(1)} %get-tuple-element.38.left_ref), channel_id=1, source_target_pairs={{0,16},{1,9},{2,18},{3,11},{4,20},{5,13},{6,22},{7,15},{8,24},{9,1... | collective-permute-start | bytes 393224 | tf_op jit(solution)/shard_map/ppermute | solution.py:411
  16.0 0.0 collective-permute-done.4.got_ref.refs_1_
  16.1 1.6 %collective-permute-start.5 = (bf16[2,128,128]{2,1,0:T(8,128)(2,1)S(1)}, bf16[2,128,128]{2,1,0:T(8,128)(2,1)S(1)}, u32[]{:S(2)}, u32[]{:S(2)}) collective-permute-start(bf16[2,128,128]{2,1,0:T(8,128)(2,1)S(1)} %get-tuple-element.32), channel_id=1, source_target_pairs={{0,6},{1,7},{2,4},{3,5},{4,2},{5,3},{6,0},{7,1},{8,14},{9,15},{10,... | collective-permute-start | bytes 196616 | tf_op jit(solution)/shard_map/ppermute | solution.py:343
  17.6 0.7 %collective-permute-start.6 = (bf16[2,128,128]{2,1,0:T(8,128)(2,1)S(1)}, bf16[2,128,128]{2,1,0:T(8,128)(2,1)S(1)}, u32[]{:S(2)}, u32[]{:S(2)}) collective-permute-start(bf16[2,128,128]{2,1,0:T(8,128)(2,1)S(1)} %get-tuple-element.33), channel_id=1, source_target_pairs={{0,4},{1,5},{2,6},{3,7},{4,0},{5,1},{6,2},{7,3},{8,12},{9,13},{10,... | collective-permute-start | bytes 196616 | tf_op jit(solution)/shard_map/ppermute | solution.py:343
  18.4 1.3 %collective-permute-start.7 = (bf16[2,128,128]{2,1,0:T(8,128)(2,1)S(1)}, bf16[2,128,128]{2,1,0:T(8,128)(2,1)S(1)}, u32[]{:S(2)}, u32[]{:S(2)}) collective-permute-start(bf16[2,128,128]{2,1,0:T(8,128)(2,1)S(1)} %get-tuple-element.34), channel_id=1, source_target_pairs={{0,2},{1,3},{2,0},{3,1},{4,6},{5,7},{6,4},{7,5},{8,10},{9,11},{10,... | collective-permute-start | bytes 196616 | tf_op jit(solution)/shard_map/ppermute | solution.py:343
  19.6 0.2 collective-permute-done.8.right_ref
  19.8 2.2 %collective-permute-start.9 = (bf16[64,1024]{1,0:T(8,128)(2,1)S(1)}, bf16[64,1024]{1,0:T(8,128)(2,1)S(1)}, u32[]{:S(2)}, u32[]{:S(2)}) collective-permute-start(bf16[64,1024]{1,0:T(8,128)(2,1)S(1)} %pair_sum.1.left_ref), channel_id=1, source_target_pairs={{0,8},{1,25},{2,10},{3,27},{4,12},{5,29},{6,14},{7,31},{8,0},{9,17... | collective-permute-start | bytes 393224 | tf_op jit(solution)/shard_map/ppermute | solution.py:411
  22.0 0.3 %collective-permute-done.6.refs_3_ = bf16[2,128,128]{2,1,0:T(8,128)(2,1)S(1)} collective-permute-done((bf16[2,128,128]{2,1,0:T(8,128)(2,1)S(1)}, bf16[2,128,128]{2,1,0:T(8,128)(2,1)S(1)}, u32[]{:S(2)}, u32[]{:S(2)}) %collective-permute-start.6) | collective-permute-done | bytes 65568 | tf_op jit(solution)/shard_map/ppermute | solution.py:343
  22.3 0.3 %collective-permute-done.7.refs_4_ = bf16[2,128,128]{2,1,0:T(8,128)(2,1)S(1)} collective-permute-done((bf16[2,128,128]{2,1,0:T(8,128)(2,1)S(1)}, bf16[2,128,128]{2,1,0:T(8,128)(2,1)S(1)}, u32[]{:S(2)}, u32[]{:S(2)}) %collective-permute-start.7) | collective-permute-done | bytes 65568 | tf_op jit(solution)/shard_map/ppermute | solution.py:343
  22.6 0.9 %unpack.1 = (bf16[1,128,512]{2,1,0:T(8,128)(2,1)}, bf16[1,128,512]{2,1,0:T(8,128)(2,1)}) custom-call(bf16[4,128,128]{2,1,0:T(8,128)(2,1)S(1)} %get-tuple-element.30.own_ref.refs_0_, bf16[4,128,128]{2,1,0:T(8,128)(2,1)S(1)} %collective-permute-done.4.got_ref.refs_1_, bf16[2,128,128]{2,1,0:T(8,128)(2,1)S(1)} %collective-permute-done.5.refs_2_, ...), custom_call_target="tpu_custom_call" | custom-call | flops 5000000000 | bytes 655360 | tf_op jit(solution)/shard_map/unpack/pallas_call | solution.py:315
  23.5 1.8 %collective-permute-done.9.right_ref = bf16[64,1024]{1,0:T(8,128)(2,1)S(1)} collective-permute-done((bf16[64,1024]{1,0:T(8,128)(2,1)S(1)}, bf16[64,1024]{1,0:T(8,128)(2,1)S(1)}, u32[]{:S(2)}, u32[]{:S(2)}) %collective-permute-start.9) | collective-permute-done | bytes 131104 | tf_op jit(solution)/shard_map/ppermute | solution.py:411
  25.3 0.7 %total.1 = f32[64,1024]{1,0:T(8,128)} custom-call(bf16[64,1024]{1,0:T(8,128)(2,1)S(1)} %pair_sum.1.left_ref, bf16[64,1024]{1,0:T(8,128)(2,1)S(1)} %collective-permute-done.9.right_ref, bf16[1,128,512]{2,1,0:T(8,128)(2,1)} %get-tuple-element.19._), custom_call_target="tpu_custom_call" | custom-call | bytes 524288 | tf_op jit(solution)/shard_map/total/pallas_call | solution.py:315
  (6 shorter events, 0.1 us)
Async XLA Ops:
  2.0 1.5 %collective-permute-start = (bf16[4,128,128]{2,1,0:T(8,128)(2,1)S(1)}, bf16[4,128,128]{2,1,0:T(8,128)(2,1)S(1)}, u32[]{:S(2)}, u32[]{:S(2)}) collective-permute-start(bf16[4,128,128]{2,1,0:T(8,128)(2,1)S(1)} %get-tuple-element.22), channel_id=1, source_target_pairs={{0,1},{1,0},{2,3},{3,2},{4,5},{5,4},{6,7},{7,6},{8,9},{9,8},{10,11... | collective-permute-start | bytes 393224 | tf_op jit(solution)/shard_map/ppermute | solution.py:333
  3.5 6.8 %collective-permute-start.1 = (bf16[2,128,128]{2,1,0:T(8,128)(2,1)S(1)}, bf16[2,128,128]{2,1,0:T(8,128)(2,1)S(1)}, u32[]{:S(2)}, u32[]{:S(2)}) collective-permute-start(bf16[2,128,128]{2,1,0:T(8,128)(2,1)S(1)} %get-tuple-element.23), channel_id=1, source_target_pairs={{0,6},{1,7},{2,4},{3,5},{4,2},{5,3},{6,0},{7,1},{8,14},{9,15},{10,... | collective-permute-start | bytes 196616 | tf_op jit(solution)/shard_map/ppermute | solution.py:343
  7.4 4.3 %collective-permute-start.2 = (bf16[2,128,128]{2,1,0:T(8,128)(2,1)S(1)}, bf16[2,128,128]{2,1,0:T(8,128)(2,1)S(1)}, u32[]{:S(2)}, u32[]{:S(2)}) collective-permute-start(bf16[2,128,128]{2,1,0:T(8,128)(2,1)S(1)} %get-tuple-element.24), channel_id=1, source_target_pairs={{0,4},{1,5},{2,6},{3,7},{4,0},{5,1},{6,2},{7,3},{8,12},{9,13},{10,... | collective-permute-start | bytes 196616 | tf_op jit(solution)/shard_map/ppermute | solution.py:343
  7.9 0.7 %copy-start = (f32[64]{0:T(128)S(1)}, f32[64]{0:T(128)}, u32[]{:S(2)}) copy-start(f32[64]{0:T(128)} %param.11) | copy-start | bytes 772
  7.9 4.3 %collective-permute-start.3 = (bf16[2,128,128]{2,1,0:T(8,128)(2,1)S(1)}, bf16[2,128,128]{2,1,0:T(8,128)(2,1)S(1)}, u32[]{:S(2)}, u32[]{:S(2)}) collective-permute-start(bf16[2,128,128]{2,1,0:T(8,128)(2,1)S(1)} %get-tuple-element.25), channel_id=1, source_target_pairs={{0,2},{1,3},{2,0},{3,1},{4,6},{5,7},{6,4},{7,5},{8,10},{9,11},{10,... | collective-permute-start | bytes 196616 | tf_op jit(solution)/shard_map/ppermute | solution.py:343
  13.3 2.7 %collective-permute-start.4 = (bf16[4,128,128]{2,1,0:T(8,128)(2,1)S(1)}, bf16[4,128,128]{2,1,0:T(8,128)(2,1)S(1)}, u32[]{:S(2)}, u32[]{:S(2)}) collective-permute-start(bf16[4,128,128]{2,1,0:T(8,128)(2,1)S(1)} %get-tuple-element.31), channel_id=1, source_target_pairs={{0,1},{1,0},{2,3},{3,2},{4,5},{5,4},{6,7},{7,6},{8,9},{9,8},{10,11... | collective-permute-start | bytes 393224 | tf_op jit(solution)/shard_map/ppermute | solution.py:333
  13.4 6.4 %collective-permute-start.8 = (bf16[64,1024]{1,0:T(8,128)(2,1)S(1)}, bf16[64,1024]{1,0:T(8,128)(2,1)S(1)}, u32[]{:S(2)}, u32[]{:S(2)}) collective-permute-start(bf16[64,1024]{1,0:T(8,128)(2,1)S(1)} %get-tuple-element.38.left_ref), channel_id=1, source_target_pairs={{0,16},{1,9},{2,18},{3,11},{4,20},{5,13},{6,22},{7,15},{8,24},{9,1... | collective-permute-start | bytes 393224 | tf_op jit(solution)/shard_map/ppermute | solution.py:411
  16.1 5.9 %collective-permute-start.5 = (bf16[2,128,128]{2,1,0:T(8,128)(2,1)S(1)}, bf16[2,128,128]{2,1,0:T(8,128)(2,1)S(1)}, u32[]{:S(2)}, u32[]{:S(2)}) collective-permute-start(bf16[2,128,128]{2,1,0:T(8,128)(2,1)S(1)} %get-tuple-element.32), channel_id=1, source_target_pairs={{0,6},{1,7},{2,4},{3,5},{4,2},{5,3},{6,0},{7,1},{8,14},{9,15},{10,... | collective-permute-start | bytes 196616 | tf_op jit(solution)/shard_map/ppermute | solution.py:343
  17.6 4.7 %collective-permute-start.6 = (bf16[2,128,128]{2,1,0:T(8,128)(2,1)S(1)}, bf16[2,128,128]{2,1,0:T(8,128)(2,1)S(1)}, u32[]{:S(2)}, u32[]{:S(2)}) collective-permute-start(bf16[2,128,128]{2,1,0:T(8,128)(2,1)S(1)} %get-tuple-element.33), channel_id=1, source_target_pairs={{0,4},{1,5},{2,6},{3,7},{4,0},{5,1},{6,2},{7,3},{8,12},{9,13},{10,... | collective-permute-start | bytes 196616 | tf_op jit(solution)/shard_map/ppermute | solution.py:343
  18.4 4.3 %collective-permute-start.7 = (bf16[2,128,128]{2,1,0:T(8,128)(2,1)S(1)}, bf16[2,128,128]{2,1,0:T(8,128)(2,1)S(1)}, u32[]{:S(2)}, u32[]{:S(2)}) collective-permute-start(bf16[2,128,128]{2,1,0:T(8,128)(2,1)S(1)} %get-tuple-element.34), channel_id=1, source_target_pairs={{0,2},{1,3},{2,0},{3,1},{4,6},{5,7},{6,4},{7,5},{8,10},{9,11},{10,... | collective-permute-start | bytes 196616 | tf_op jit(solution)/shard_map/ppermute | solution.py:343
  19.8 5.5 %collective-permute-start.9 = (bf16[64,1024]{1,0:T(8,128)(2,1)S(1)}, bf16[64,1024]{1,0:T(8,128)(2,1)S(1)}, u32[]{:S(2)}, u32[]{:S(2)}) collective-permute-start(bf16[64,1024]{1,0:T(8,128)(2,1)S(1)} %pair_sum.1.left_ref), channel_id=1, source_target_pairs={{0,8},{1,25},{2,10},{3,27},{4,12},{5,29},{6,14},{7,31},{8,0},{9,17... | collective-permute-start | bytes 393224 | tf_op jit(solution)/shard_map/ppermute | solution.py:411
